TPU v7x, 32 devices: a whole 2x2x4 slice. The times are simulated.
32 devices in a mesh: groups: 2 (over y), shard: 4 (over z), qgrp: 2 (over x), dim: 2 (over core).
Axes of the slice: x: 2, y: 2, z: 4, core: 2. Of those that a mesh axis runs over, the one named last changes fastest.
Arguments:
- queries: bfloat16 [32, 32, 128], P(('groups', 'shard', 'qgrp')), parts along dimension 0, may hold values from -0.5 to 0.5
- doc_tokens: bfloat16 [512, 128, 128], P(('groups', 'shard', 'qgrp'), 'dim'), parts along dimension 0, may hold values from -0.5 to 0.5
- doc_lens: int32 [512], P(('groups', 'shard', 'qgrp')), parts along dimension 0, may hold values from 1 to 128
- candidates: int32 [32, 1000], P(('groups', 'shard', 'qgrp')), parts along dimension 0, may hold values from 0 to 255
Outputs:
- scores: float32 [32, 1000], P(('groups', 'shard', 'qgrp')), parts along dimension 0
There are 2 independent parts, one for each index of `groups`. A program takes and returns all parts, laid end to end along the dimension named above; each array names one. Nothing has to cross between parts.
All inputs are finite; a program needn't handle non-finite values.
Results may differ from a plain program's by a relative error of at most 0.0003.
Values may be sent and summed in bfloat16 or wider, within the bound.
No kernel may reach another device: no remote copies, remote signals or barrier semaphores. Data moves between devices by JAX's collectives and lax.ppermute only.
A program may use at most 64 MiB of HBM per device.

v0:
```python
import jax
import jax.numpy as jnp
from jax import lax
from jax.sharding import PartitionSpec as P


def make_scorer(docs, lens_float, offset, tok_take):
    count, half, width = docs.shape
    tiles = docs.reshape(count // 8, 8 * half, width)
    positions = (offset + jnp.arange(half, dtype=jnp.int32)).astype(jnp.float32)
    valid = (positions[None, :] < lens_float[:, None]).reshape(count // 8, 8 * half)

    def scorer(piece, start):
        rows = piece.shape[0]
        flat_queries = piece.reshape(rows * tok_take, width)

        def one_tile(pair):
            tile, mask = pair
            token_score = jnp.dot(flat_queries, tile.T, preferred_element_type=jnp.float32)
            token_score = jnp.where(mask[None, :], token_score, jnp.float32(-1e30))
            return jnp.max(token_score.reshape(flat_queries.shape[0], 8, half), axis=2)

        token_max = lax.map(one_tile, (tiles, valid))
        token_max = jnp.transpose(token_max, (1, 0, 2))
        return token_max.reshape(rows, tok_take, count)

    return scorer


def per_device(queries, doc_tokens, doc_lens, candidates):
    q_owned = candidates.shape[0]
    n_shard = lax.axis_size("shard")
    n_qgrp = lax.axis_size("qgrp")
    q_tokens = queries.shape[1]
    offset = lax.axis_index("dim") * doc_tokens.shape[1]
    scorer = make_scorer(doc_tokens, doc_lens.astype(jnp.float32), offset, q_tokens)
    maxima = scorer(lax.all_gather(queries, ("shard", "qgrp"), axis=0, tiled=True), jnp.int32(0))
    maxima = lax.pmax(maxima, "dim")
    block = jnp.sum(maxima, axis=1)
    local_pas = block.shape[1]
    moved = lax.all_to_all(
        block.reshape(n_shard * n_qgrp, q_owned, 1, local_pas),
        ("shard", "qgrp"),
        split_axis=0,
        concat_axis=2,
        tiled=True,
    )
    passage_score = moved.reshape(q_owned, -1)
    return jnp.take_along_axis(passage_score, candidates, axis=1)


def solution(mesh):
    in_specs = (
        P(("groups", "shard", "qgrp"), None, None),
        P(("groups", "shard", "qgrp"), "dim", None),
        P(("groups", "shard", "qgrp")),
        P(("groups", "shard", "qgrp"), None),
    )
    out_specs = P(("groups", "shard", "qgrp"), None)
    return jax.shard_map(
        per_device, mesh=mesh, in_specs=in_specs, out_specs=out_specs, check_vma=False
    )
```

profile of v0, /device:TPU:0, one launch (start us, length us, event | category | flops | bytes accessed | tf_op | source)
XLA Modules:
  0.0 112.3 jit_solution(12965334814740704118)
XLA Ops:
  6.5 0.0 all-reduce.2.cloned.1.call-start
  6.5 0.0 copy-start.1
  6.5 32.6 %all_gather.3 = bf16[16,32,128]{2,1,0:T(8,128)(2,1)S(1)} all-gather(bf16[2,32,128]{2,1,0:T(8,128)(2,1)} %param.6), channel_id=1, replica_groups=mesh['groups'=2,'shard'=4,'qgrp'=2,'dim'=2] {'shard','qgrp'}, dimensions={0}, use_global_device_ids=true | all-gather | bytes 147456 | tf_op jit(solution)/shard_map/all_gather | solution.py:37
  39.2 0.0 copy-done.1
  39.2 0.1 lt.38
  39.3 0.1 lt.39
  39.3 0.1 lt.40
  39.4 0.1 lt.36
  39.5 5.1 %while.10 = (s32[]{:T(128)}, f32[4,512,8]{1,2,0:T(8,128)S(1)}, pred[4,512]{1,0:T(4,128)(4,1)S(1)}, bf16[4,512,128]{2,1,0:T(8,128)(2,1)}, bf16[512,128]{1,0:T(8,128)(2,1)S(1)}, /*index=5*/s32[]{:T(128)}) while((s32[]{:T(128)}, f32[4,512,8]{1,2,0:T(8,128)S(1)}, pred[4,512]{1,0:T(4,128)(4,1)S(1)}, bf16[4,512,128]{2,1,0:T(8,128)(2,1)}, ...), condition=%wide.region_2.3_spmd, body=%wide.region_0.2_spmd.sunk | while | flops 67629056 | bytes 313421 | solution.py:23
  39.6 1.2 %bitcast_reduce_fusion.2 = f32[512,8]{0,1:T(8,128)S(1)} fusion(bf16[512,128]{1,0:T(8,128)(2,1)S(1)} %get-tuple-element.90, pred[512]{0:T(512)(128)(4,1)S(1)} %dynamic-slice_reduce_fusion.2, bf16[4,512,128]{2,1,0:T(8,128)(2,1)} %get-tuple-element.89, s32[]{:T(128)} %get-tuple-element.80), kind=kOutput, calls=%fused_computation.2.clone.1 | convolution fusion | flops 67629056 | bytes 279552 | tf_op jit(solution)/shard_map/while/body/eval_jaxpr/dot_general | solution.py:19
  40.8 1.2 %bitcast_reduce_fusion.2 = f32[512,8]{0,1:T(8,128)S(1)} fusion(bf16[512,128]{1,0:T(8,128)(2,1)S(1)} %get-tuple-element.90, pred[512]{0:T(512)(128)(4,1)S(1)} %dynamic-slice_reduce_fusion.2, bf16[4,512,128]{2,1,0:T(8,128)(2,1)} %get-tuple-element.89, s32[]{:T(128)} %get-tuple-element.80), kind=kOutput, calls=%fused_computation.2.clone.1 | convolution fusion | flops 67629056 | bytes 279552 | tf_op jit(solution)/shard_map/while/body/eval_jaxpr/dot_general | solution.py:19
  42.1 1.2 %bitcast_reduce_fusion.2 = f32[512,8]{0,1:T(8,128)S(1)} fusion(bf16[512,128]{1,0:T(8,128)(2,1)S(1)} %get-tuple-element.90, pred[512]{0:T(512)(128)(4,1)S(1)} %dynamic-slice_reduce_fusion.2, bf16[4,512,128]{2,1,0:T(8,128)(2,1)} %get-tuple-element.89, s32[]{:T(128)} %get-tuple-element.80), kind=kOutput, calls=%fused_computation.2.clone.1 | convolution fusion | flops 67629056 | bytes 279552 | tf_op jit(solution)/shard_map/while/body/eval_jaxpr/dot_general | solution.py:19
  43.4 1.2 %bitcast_reduce_fusion.2 = f32[512,8]{0,1:T(8,128)S(1)} fusion(bf16[512,128]{1,0:T(8,128)(2,1)S(1)} %get-tuple-element.90, pred[512]{0:T(512)(128)(4,1)S(1)} %dynamic-slice_reduce_fusion.2, bf16[4,512,128]{2,1,0:T(8,128)(2,1)} %get-tuple-element.89, s32[]{:T(128)} %get-tuple-element.80), kind=kOutput, calls=%fused_computation.2.clone.1 | convolution fusion | flops 67629056 | bytes 279552 | tf_op jit(solution)/shard_map/while/body/eval_jaxpr/dot_general | solution.py:19
  44.6 0.8 reshape.41
  45.5 0.0 all-reduce.2.cloned.1.call-update
  45.5 19.3 %all-reduce.2.cloned.1.call-done = f32[16,32,32]{1,0,2:T(8,128)} async-done(((f32[16,32,32]{1,0,2:T(8,128)}), f32[16,32,32]{1,0,2:T(8,128)}) %all-reduce.2.cloned.1.call-update) | async-done | bytes 65552 | tf_op jit(solution)/shard_map/pmax | solution.py:38
  64.8 1.1 reduce_sum.9
  65.9 0.7 copy.6
  66.6 0.0 copy-start
  66.6 5.9 %all-to-all-start = ((f32[8,2,1,32]{3,1,2,0:T(2,128)}), f32[8,2,1,32]{3,1,2,0:T(2,128)S(1)}, u32[]{:S(2)}, u32[]{:S(2)}) async-start(f32[8,2,1,32]{3,1,2,0:T(2,128)} %bitcast.8), calls=%async_computation | async-start | bytes 16384 | tf_op jit(solution)/shard_map/all_to_all | solution.py:41
  72.5 0.0 copy-done
  72.5 0.1 reshape.45
  72.6 6.4 %all-to-all-done = f32[8,2,1,32]{3,1,2,0:T(2,128)S(1)} async-done(((f32[8,2,1,32]{3,1,2,0:T(2,128)}), f32[8,2,1,32]{3,1,2,0:T(2,128)S(1)}, u32[]{:S(2)}, u32[]{:S(2)}) %all-to-all-start) | async-done | bytes 2080 | tf_op jit(solution)/shard_map/all_to_all | solution.py:41
  79.0 0.1 reshape.43
  79.1 25.6 %gather_fusion = f32[2000]{0:T(1024)S(1)} fusion(f32[2,256]{1,0:T(2,128)S(1)} %reshape.43, s32[2000]{0:T(1024)S(1)} %reshape.45), kind=kCustom, calls=%fused_computation | custom fusion | bytes 32000 | tf_op jit(solution)/shard_map/jit(take_along_axis)/gather | solution.py:49
  104.7 0.1 reshape.48
  104.8 0.6 and_select_fusion
  (15 shorter events, 0.2 us)
Async XLA Ops:
  6.5 58.3 %all-reduce.2.cloned.1.call-start = ((), (), s32[]{:S(2)}) async-start(), calls=%async_computation.1 | async-start | bytes 524288 | tf_op jit(solution)/shard_map/pmax | solution.py:38
  6.5 32.6 %copy-start.1 = (s32[32]{0:T(128)S(1)}, s32[32]{0:T(128)}, u32[]{:S(2)}) copy-start(s32[32]{0:T(128)} %param.8) | copy-start | bytes 388
  66.6 5.9 %copy-start = (s32[2,1000]{1,0:T(2,128)S(1)}, s32[2,1000]{1,0:T(2,128)}, u32[]{:S(2)}) copy-start(s32[2,1000]{1,0:T(2,128)} %param.9) | copy-start | bytes 24004
  66.6 12.4 %all-to-all-start = ((f32[8,2,1,32]{3,1,2,0:T(2,128)}), f32[8,2,1,32]{3,1,2,0:T(2,128)S(1)}, u32[]{:S(2)}, u32[]{:S(2)}) async-start(f32[8,2,1,32]{3,1,2,0:T(2,128)} %bitcast.8), calls=%async_computation | async-start | bytes 16384 | tf_op jit(solution)/shard_map/all_to_all | solution.py:41
Sparse Core Ops, SparseCore 0:
  45.6 19.1 all-reduce.1
where the time goes:
time: 113 us; the launch traced here: 112 us
  blocking collectives  32.6 us (29%)
  local copies, waits for them, and re-layouts  27.8 us (25%)
  waiting for transfers between devices  25.7 us (23%)
  between operations  13.4 us (12%)
  starting transfers between devices  5.9 us (5%)
  matrix products  4.87 us (4%)
  other arithmetic  1.73 us (2%)
    all_gather x1, blocking collectives, per_device(): lax.all_gather(queries, ('shard', 'qgrp'), axis=0, tiled=True)  32.6 us
    gather x3, local copies, waits for them, and re-layouts, per_device(): return jnp.take_along_axis(passage_score, candidates, axis=1)  25.8 us
    pmax x1, waiting for transfers between devices, per_device(): maxima = lax.pmax(maxima, 'dim')  19.3 us
    all_to_all x1, waiting for transfers between devices, per_device(): lax.all_to_all(block.reshape(n_shard * n_qgrp, q_owned, 1, local_pas), ('...  6.41 us
    all_to_all x1, starting transfers between devices, per_device(): lax.all_to_all(block.reshape(n_shard * n_qgrp, q_owned, 1, local_pas), ('...  5.9 us
    dot_general x4, matrix products, one_tile(): jnp.dot(flat_queries, tile.T, preferred_element_type=jnp.float32)  4.87 us
  transfers between devices with their start and end apart: 2, of which 2 were waited for; matrix products, arithmetic and copies ran while one was open for 0% of the time, Pallas kernels for 0%

commit v1 on v0

v1 whole, which is shorter than its diff:
```python
import functools

import jax
import jax.numpy as jnp
from jax import lax
from jax.experimental import pallas as pl
from jax.experimental.pallas import tpu as pltpu
from jax.sharding import PartitionSpec as P

INDEX_AXES = ("shard", "qgrp")
LOW = -1e30
STEP = 4
DIRECT = 16


def score_kernel(n_own, count, me_ref, lens_ref, *refs):
    piece_refs = refs[: n_own]
    own_ref, other_ref = refs[n_own: n_own + 2]
    out_refs = refs[n_own + 2: -2]
    flat_ref, max_ref = refs[-2:]
    core = me_ref[0]
    at = 0
    for piece_ref in piece_refs:
        rows, q_tokens, width = piece_ref.shape
        flat_ref[pl.ds(at, rows * q_tokens), :] = piece_ref[...].reshape(rows * q_tokens, width)
        at += rows * q_tokens
    half = own_ref.shape[1]
    q_tokens = piece_refs[0].shape[1]
    total = flat_ref.shape[0]
    rows = lax.broadcasted_iota(jnp.int32, (half, 1), 0)
    block = 512 if total % 512 == 0 else total

    def group(step, _):
        start = step * STEP
        for at in range(0, total, block):
            flat = flat_ref[pl.ds(at, block), :]
            for k in range(STEP):
                p = start + k
                length = lens_ref[p]
                best = None
                for ref, offset in ((own_ref, core * half), (other_ref, (1 - core) * half)):
                    score = lax.dot_general(
                        ref[p], flat, (((1,), (1,)), ((), ())), preferred_element_type=jnp.float32
                    )
                    score = jnp.where(rows + offset < length, score, LOW)
                    best = score if best is None else jnp.maximum(best, score)
                max_ref[pl.ds(p, 1), pl.ds(at, block)] = jnp.max(best, axis=0, keepdims=True)
        return 0

    lax.fori_loop(0, count // STEP, group, 0)
    queries = total // q_tokens
    summed = jnp.sum(max_ref[...].T.reshape(queries, q_tokens, count), axis=1)
    q_each = out_refs[0].shape[0]
    if len(out_refs) == 1:
        out_refs[0][...] = summed
    else:
        for r, out_ref in enumerate(out_refs):
            out_ref[...] = summed[r * q_each: (r + 1) * q_each]


def pick_kernel(n_own, base_ref, cand_ref, *refs):
    piece_refs, out_ref = refs[:n_own], refs[n_own]
    parts = [ref[...] for ref in piece_refs]
    table = jnp.concatenate(parts, axis=1) if len(parts) > 1 else parts[0]
    size = table.shape[1]
    spot = cand_ref[...] - base_ref[0]
    spot = jnp.where(spot < 0, spot + size, spot)
    rows, width = spot.shape
    lane_count = 128
    for at in range(0, width, lane_count):
        index = spot[:, at: at + lane_count]
        low = jnp.bitwise_and(index, lane_count - 1)
        high = lax.shift_right_logical(index, 7)
        value = jnp.zeros((rows, lane_count), jnp.float32)
        for t in range(0, size, lane_count):
            found = jnp.take_along_axis(table[:, t: t + lane_count], low, axis=1, mode="promise_in_bounds")
            value = jnp.where(high == t // lane_count, found, value)
        out_ref[:, pl.ds(at, lane_count)] = value


def per_device(queries, doc_tokens, doc_lens, candidates):
    q_owned, cand = candidates.shape
    n = lax.axis_size("shard") * lax.axis_size("qgrp")
    cores = lax.axis_size("dim")
    _, q_tokens, width = queries.shape
    count = doc_tokens.shape[0]
    me = lax.axis_index(INDEX_AXES)
    core = lax.axis_index("dim")
    direct = n <= DIRECT

    def turn(x, r):
        return lax.ppermute(x, INDEX_AXES, [(s, (s + r) % n) for s in range(n)])

    if direct:
        pieces = [queries] + [turn(queries, n - r) for r in range(1, n)]
    else:
        pieces = [lax.all_gather(queries, INDEX_AXES, axis=0, tiled=True)]
    other = lax.ppermute(doc_tokens, "dim", [(s, cores - 1 - s) for s in range(cores)])

    smem = pl.BlockSpec(memory_space=pltpu.SMEM)
    vmem = pl.BlockSpec(memory_space=pltpu.VMEM)
    outs = n if direct else 1
    blocks = pl.pallas_call(
        functools.partial(score_kernel, len(pieces), count),
        out_shape=[jax.ShapeDtypeStruct((n * q_owned // outs, count), jnp.float32)] * outs,
        in_specs=[smem, smem] + [vmem] * (len(pieces) + 2),
        out_specs=[vmem] * outs,
        scratch_shapes=[
            pltpu.VMEM((n * q_owned * q_tokens, width), jnp.bfloat16),
            pltpu.VMEM((count, n * q_owned * q_tokens), jnp.float32),
        ],
        compiler_params=pltpu.CompilerParams(vmem_limit_bytes=48 * 1024 * 1024),
        name="score",
    )(core.reshape(1), doc_lens, *pieces, doc_tokens, other)

    if direct:
        moved = [blocks[0]] + [turn(blocks[r], r) for r in range(1, n)]
        moved = [moved[0]] + [moved[n - r] for r in range(1, n)]
        base = me * count
    else:
        moved = [
            lax.all_to_all(
                blocks[0].reshape(n, q_owned, count), INDEX_AXES, split_axis=0, concat_axis=0, tiled=True
            ).transpose(1, 0, 2).reshape(q_owned, n * count)
        ]
        base = jnp.zeros((), jnp.int32)
    padded = -(-cand // 128) * 128
    return pl.pallas_call(
        functools.partial(pick_kernel, len(moved)),
        grid=(1,),
        out_shape=jax.ShapeDtypeStruct((q_owned, cand), jnp.float32),
        in_specs=[smem, pl.BlockSpec((q_owned, padded), lambda i: (0, 0))]
        + [pl.BlockSpec(m.shape, lambda i: (0, 0)) for m in moved],
        out_specs=pl.BlockSpec((q_owned, padded), lambda i: (0, 0)),
        name="pick",
    )(base.reshape(1), candidates, *moved)


def solution(mesh):
    in_specs = (
        P(("groups",) + INDEX_AXES, None, None),
        P(("groups",) + INDEX_AXES, "dim", None),
        P(("groups",) + INDEX_AXES),
        P(("groups",) + INDEX_AXES, None),
    )
    out_specs = P(("groups",) + INDEX_AXES, None)
    return jax.shard_map(
        per_device, mesh=mesh, in_specs=in_specs, out_specs=out_specs, check_vma=False
    )
```

time: 113 us -> 39.8 us (0.35)
  blocking collectives: 32.6 us -> 0 us
  local copies, waits for them, and re-layouts: 27.8 us -> 2.13 us
  waiting for transfers between devices: 25.7 us -> 10.8 us
  starting transfers between devices: 5.9 us -> 20.3 us
  between operations: 13.4 us -> 0.08 us
  Pallas kernels: 0 us -> 6.18 us
  matrix products: 4.87 us -> 0 us
  other arithmetic: 1.73 us -> 0 us
    all_gather x1 -> x0, blocking collectives: 32.6 us -> none  [per_device(): lax.all_gather(queries, ('shard', 'qgrp'), axis=0, tiled=True)]
    gather x3 -> x0, local copies, waits for them, and re-layouts: 25.8 us -> none  [per_device(): return jnp.take_along_axis(passage_score, candidates, axis=1)]
    ppermute x0 -> x15, starting transfers between devices: none -> 20.3 us  [the longest x14 19.9 us: turn(): return lax.ppermute(x, INDEX_AXES, [(s, (s + r) % n) for s in range(n)])]
    pmax x1 -> x0, waiting for transfers between devices: 19.3 us -> none  [per_device(): maxima = lax.pmax(maxima, 'dim')]
    ppermute x0 -> x15, waiting for transfers between devices: none -> 10.8 us  [the longest x14 10.8 us: turn(): return lax.ppermute(x, INDEX_AXES, [(s, (s + r) % n) for s in range(n)])]
    all_to_all x1 -> x0, waiting for transfers between devices: 6.41 us -> none  [per_device(): lax.all_to_all(block.reshape(n_shard * n_qgrp, q_owned, 1, local_pas), ('...]
    pallas_call x0 -> x2, Pallas kernels: none -> 6.18 us  [the longest x1 4.67 us: per_device(): pl.pallas_call(functools.partial(score_kernel, len(pieces), count), out_s...]
    all_to_all x1 -> x0, starting transfers between devices: 5.9 us -> none  [per_device(): lax.all_to_all(block.reshape(n_shard * n_qgrp, q_owned, 1, local_pas), ('...]
  transfers between devices with their start and end apart: 2 -> 15, of which waited for: 2 -> 6; matrix products, arithmetic and copies ran while one was open for 0% -> 0% of each run, Pallas kernels for 0% -> 0%
where the time goes in v1:
time: 39.8 us; the launch traced here: 39.6 us
  starting transfers between devices  20.3 us (51%)
  waiting for transfers between devices  10.8 us (27%)
  Pallas kernels  6.18 us (16%)
  local copies, waits for them, and re-layouts  2.13 us (5%)
    ppermute x14, starting transfers between devices, turn(): return lax.ppermute(x, INDEX_AXES, [(s, (s + r) % n) for s in range(n)])  19.9 us
    ppermute x14, waiting for transfers between devices, turn(): return lax.ppermute(x, INDEX_AXES, [(s, (s + r) % n) for s in range(n)])  10.8 us
    pallas_call x1, Pallas kernels, per_device(): pl.pallas_call(functools.partial(score_kernel, len(pieces), count), out_s...  4.67 us
    unnamed x22, local copies, waits for them, and re-layouts  2.13 us
    pallas_call x1, Pallas kernels, per_device(): pl.pallas_call(functools.partial(pick_kernel, len(moved)), grid=(1,), out...  1.5 us
  transfers between devices with their start and end apart: 15, of which 6 were waited for; matrix products, arithmetic and copies ran while one was open for 0% of the time, Pallas kernels for 0%

profile of v1, /device:TPU:0, one launch (start us, length us, event | category | flops | bytes accessed | tf_op | source)
XLA Modules:
  0.0 39.6 jit_solution(14200842340008111831)
XLA Ops:
  0.0 0.5 %collective-permute-start.7 = (bf16[32,64,128]{2,1,0:T(8,128)(2,1)}, bf16[32,64,128]{2,1,0:T(8,128)(2,1)S(1)}, u32[]{:S(2)}, u32[]{:S(2)}) collective-permute-start(bf16[32,64,128]{2,1,0:T(8,128)(2,1)} %refs_8_.1), channel_id=1, source_target_pairs={{0,1},{1,0},{2,3},{3,2},{4,5},{5,4},{6,7},{7,6},{8,9},{9,8},{10,11... | collective-permute-start | bytes 1572872 | tf_op jit(solution)/shard_map/ppermute | solution.py:98
  0.5 2.6 %collective-permute-start.5 = (bf16[2,32,128]{2,1,0:T(8,128)(2,1)}, bf16[2,32,128]{2,1,0:T(8,128)(2,1)S(1)}, u32[]{:S(2)}, u32[]{:S(2)}) collective-permute-start(bf16[2,32,128]{2,1,0:T(8,128)(2,1)} %refs_0_.1), channel_id=1, source_target_pairs={{0,4},{2,6},{4,8},{6,10},{8,12},{10,14},{12,0},{14,2},{1,5},{3,7},... | collective-permute-start | bytes 49160 | tf_op jit(solution)/shard_map/ppermute | solution.py:92
  3.1 2.5 %collective-permute-start.4 = (bf16[2,32,128]{2,1,0:T(8,128)(2,1)}, bf16[2,32,128]{2,1,0:T(8,128)(2,1)S(1)}, u32[]{:S(2)}, u32[]{:S(2)}) collective-permute-start(bf16[2,32,128]{2,1,0:T(8,128)(2,1)} %refs_0_.1), channel_id=1, source_target_pairs={{0,6},{2,8},{4,10},{6,12},{8,14},{10,0},{12,2},{14,4},{1,7},{3,9},... | collective-permute-start | bytes 49160 | tf_op jit(solution)/shard_map/ppermute | solution.py:92
  5.6 1.2 %collective-permute-start.3 = (bf16[2,32,128]{2,1,0:T(8,128)(2,1)}, bf16[2,32,128]{2,1,0:T(8,128)(2,1)S(1)}, u32[]{:S(2)}, u32[]{:S(2)}) collective-permute-start(bf16[2,32,128]{2,1,0:T(8,128)(2,1)} %refs_0_.1), channel_id=1, source_target_pairs={{0,8},{2,10},{4,12},{6,14},{8,0},{10,2},{12,4},{14,6},{1,9},{3,11}... | collective-permute-start | bytes 49160 | tf_op jit(solution)/shard_map/ppermute | solution.py:92
  6.8 2.7 %collective-permute-start.2 = (bf16[2,32,128]{2,1,0:T(8,128)(2,1)}, bf16[2,32,128]{2,1,0:T(8,128)(2,1)S(1)}, u32[]{:S(2)}, u32[]{:S(2)}) collective-permute-start(bf16[2,32,128]{2,1,0:T(8,128)(2,1)} %refs_0_.1), channel_id=1, source_target_pairs={{0,10},{2,12},{4,14},{6,0},{8,2},{10,4},{12,6},{14,8},{1,11},{3,13... | collective-permute-start | bytes 49160 | tf_op jit(solution)/shard_map/ppermute | solution.py:92
  9.5 0.0 collective-permute-done.5.refs_6_
  9.5 1.3 %collective-permute-start.1 = (bf16[2,32,128]{2,1,0:T(8,128)(2,1)}, bf16[2,32,128]{2,1,0:T(8,128)(2,1)S(1)}, u32[]{:S(2)}, u32[]{:S(2)}) collective-permute-start(bf16[2,32,128]{2,1,0:T(8,128)(2,1)} %refs_0_.1), channel_id=1, source_target_pairs={{0,12},{2,14},{4,0},{6,2},{8,4},{10,6},{12,8},{14,10},{1,13},{3,15... | collective-permute-start | bytes 49160 | tf_op jit(solution)/shard_map/ppermute | solution.py:92
  10.8 0.0 collective-permute-done.4.refs_5_
  10.8 1.4 %collective-permute-start = (bf16[2,32,128]{2,1,0:T(8,128)(2,1)}, bf16[2,32,128]{2,1,0:T(8,128)(2,1)S(1)}, u32[]{:S(2)}, u32[]{:S(2)}) collective-permute-start(bf16[2,32,128]{2,1,0:T(8,128)(2,1)} %refs_0_.1), channel_id=1, source_target_pairs={{0,14},{2,0},{4,2},{6,4},{8,6},{10,8},{12,10},{14,12},{1,15},{3,1}... | collective-permute-start | bytes 49160 | tf_op jit(solution)/shard_map/ppermute | solution.py:92
  12.2 0.0 collective-permute-done.3.refs_4_
  12.2 0.7 %collective-permute-start.6 = (bf16[2,32,128]{2,1,0:T(8,128)(2,1)}, bf16[2,32,128]{2,1,0:T(8,128)(2,1)S(1)}, u32[]{:S(2)}, u32[]{:S(2)}) collective-permute-start(bf16[2,32,128]{2,1,0:T(8,128)(2,1)} %refs_0_.1), channel_id=1, source_target_pairs={{0,2},{2,4},{4,6},{6,8},{8,10},{10,12},{12,14},{14,0},{1,3},{3,5},... | collective-permute-start | bytes 49160 | tf_op jit(solution)/shard_map/ppermute | solution.py:92
  12.9 0.0 collective-permute-done.2.refs_3_
  12.9 0.6 %collective-permute-done.1.refs_2_ = bf16[2,32,128]{2,1,0:T(8,128)(2,1)S(1)} collective-permute-done((bf16[2,32,128]{2,1,0:T(8,128)(2,1)}, bf16[2,32,128]{2,1,0:T(8,128)(2,1)S(1)}, u32[]{:S(2)}, u32[]{:S(2)}) %collective-permute-start.1) | collective-permute-done | bytes 16416 | tf_op jit(solution)/shard_map/ppermute | solution.py:92
  13.4 1.4 %collective-permute-done.refs_1_ = bf16[2,32,128]{2,1,0:T(8,128)(2,1)S(1)} collective-permute-done((bf16[2,32,128]{2,1,0:T(8,128)(2,1)}, bf16[2,32,128]{2,1,0:T(8,128)(2,1)S(1)}, u32[]{:S(2)}, u32[]{:S(2)}) %collective-permute-start) | collective-permute-done | bytes 16416 | tf_op jit(solution)/shard_map/ppermute | solution.py:92
  14.8 4.1 %collective-permute-done.6.refs_7_ = bf16[2,32,128]{2,1,0:T(8,128)(2,1)S(1)} collective-permute-done((bf16[2,32,128]{2,1,0:T(8,128)(2,1)}, bf16[2,32,128]{2,1,0:T(8,128)(2,1)S(1)}, u32[]{:S(2)}, u32[]{:S(2)}) %collective-permute-start.6) | collective-permute-done | bytes 16416 | tf_op jit(solution)/shard_map/ppermute | solution.py:92
  18.9 0.0 collective-permute-done.7.refs_9_
  18.9 1.0 %copy-done = bf16[32,64,128]{2,1,0:T(8,128)(2,1)S(1)} copy-done((bf16[32,64,128]{2,1,0:T(8,128)(2,1)S(1)}, bf16[32,64,128]{2,1,0:T(8,128)(2,1)}, u32[]{:S(2)}) %copy-start) | copy-done | bytes 524312
  19.9 4.7 %score.1 = (f32[2,32]{1,0:T(2,128)S(1)}, f32[2,32]{1,0:T(2,128)S(1)}, f32[2,32]{1,0:T(2,128)S(1)}, f32[2,32]{1,0:T(2,128)S(1)}, f32[2,32]{1,0:T(2,128)S(1)}, /*i...) custom-call(s32[1]{0:T(128)} %bitcast.1.me_ref, s32[32]{0:T(128)S(1)} %copy-done.3, ...), custom_call_target="tpu_custom_call" | custom-call | tf_op jit(solution)/shard_map/score/pallas_call | solution.py:103
  24.6 0.1 collective-permute-start.8
  24.7 0.5 %copy-done.2 = f32[2,32]{1,0:T(2,128)} copy-done((f32[2,32]{1,0:T(2,128)}, f32[2,32]{1,0:T(2,128)S(1)}, u32[]{:S(2)}) %copy-start.2) | copy-done | bytes 280
  25.2 0.0 collective-permute-start.9
  25.2 1.3 %collective-permute-start.10 = (f32[2,32]{1,0:T(2,128)S(1)}, f32[2,32]{1,0:T(2,128)S(1)}, u32[]{:S(2)}, u32[]{:S(2)}) collective-permute-start(f32[2,32]{1,0:T(2,128)S(1)} %get-tuple-element.16), channel_id=1, source_target_pairs={{0,10},{2,12},{4,14},{6,0},{8,2},{10,4},{12,6},{14,8},{1,11},{3,13... | collective-permute-start | bytes 776 | tf_op jit(solution)/shard_map/ppermute | solution.py:92
  26.5 2.6 %collective-permute-start.11 = (f32[2,32]{1,0:T(2,128)S(1)}, f32[2,32]{1,0:T(2,128)S(1)}, u32[]{:S(2)}, u32[]{:S(2)}) collective-permute-start(f32[2,32]{1,0:T(2,128)S(1)} %get-tuple-element.17), channel_id=1, source_target_pairs={{0,8},{2,10},{4,12},{6,14},{8,0},{10,2},{12,4},{14,6},{1,9},{3,11}... | collective-permute-start | bytes 776 | tf_op jit(solution)/shard_map/ppermute | solution.py:92
  29.1 0.0 collective-permute-start.12
  29.1 0.0 collective-permute-done.8.refs_1_
  29.1 2.1 %collective-permute-start.13 = (f32[2,32]{1,0:T(2,128)S(1)}, f32[2,32]{1,0:T(2,128)S(1)}, u32[]{:S(2)}, u32[]{:S(2)}) collective-permute-start(f32[2,32]{1,0:T(2,128)S(1)} %get-tuple-element.19), channel_id=1, source_target_pairs={{0,4},{2,6},{4,8},{6,10},{8,12},{10,14},{12,0},{14,2},{1,5},{3,7},... | collective-permute-start | bytes 776 | tf_op jit(solution)/shard_map/ppermute | solution.py:92
  31.2 1.5 %collective-permute-start.14 = (f32[2,32]{1,0:T(2,128)S(1)}, f32[2,32]{1,0:T(2,128)S(1)}, u32[]{:S(2)}, u32[]{:S(2)}) collective-permute-start(f32[2,32]{1,0:T(2,128)S(1)} %get-tuple-element.20), channel_id=1, source_target_pairs={{0,2},{2,4},{4,6},{6,8},{8,10},{10,12},{12,14},{14,0},{1,3},{3,5},... | collective-permute-start | bytes 776 | tf_op jit(solution)/shard_map/ppermute | solution.py:92
  32.6 1.8 %collective-permute-done.12.refs_5_ = f32[2,32]{1,0:T(2,128)S(1)} collective-permute-done((f32[2,32]{1,0:T(2,128)S(1)}, f32[2,32]{1,0:T(2,128)S(1)}, u32[]{:S(2)}, u32[]{:S(2)}) %collective-permute-start.12) | collective-permute-done | bytes 288 | tf_op jit(solution)/shard_map/ppermute | solution.py:92
  34.4 0.5 %collective-permute-done.13.refs_6_ = f32[2,32]{1,0:T(2,128)S(1)} collective-permute-done((f32[2,32]{1,0:T(2,128)S(1)}, f32[2,32]{1,0:T(2,128)S(1)}, u32[]{:S(2)}, u32[]{:S(2)}) %collective-permute-start.13) | collective-permute-done | bytes 288 | tf_op jit(solution)/shard_map/ppermute | solution.py:92
  35.0 2.5 %collective-permute-done.14.refs_7_ = f32[2,32]{1,0:T(2,128)S(1)} collective-permute-done((f32[2,32]{1,0:T(2,128)S(1)}, f32[2,32]{1,0:T(2,128)S(1)}, u32[]{:S(2)}, u32[]{:S(2)}) %collective-permute-start.14) | collective-permute-done | bytes 288 | tf_op jit(solution)/shard_map/ppermute | solution.py:92
  37.5 0.6 %copy-done.10 = f32[2,32]{1,0:T(2,128)} copy-done((f32[2,32]{1,0:T(2,128)}, f32[2,32]{1,0:T(2,128)S(1)}, u32[]{:S(2)}) %copy-start.10) | copy-done | bytes 280
  38.1 1.5 %pick.1 = f32[2,1000]{1,0:T(2,128)} custom-call(s32[1]{0:T(128)} %bitcast.base_ref, s32[2,1000]{1,0:T(2,128)} %cand_ref.1, f32[2,32]{1,0:T(2,128)} %copy-done.2, f32[2,32]{1,0:T(2,128)} %copy-done.4, f32[2,32]{1,0:T(2,128)} %copy-done.5, f32[2,32]{1,0:T(2,128)} %copy-done.6, f32[2,32]{1,0:T(2,128)} %copy-done.7, f32[2,32]{1,0:T(2,128)} %copy-done.8, ...), custom_call_target="tpu_custom_call" | custom-call | tf_op jit(solution)/shard_map/pick/pallas_call | solution.py:128
  (22 shorter events, 0.0 us)
Async XLA Ops:
  0.0 18.9 %copy-start.1 = (bf16[2,32,128]{2,1,0:T(8,128)(2,1)S(1)}, bf16[2,32,128]{2,1,0:T(8,128)(2,1)}, u32[]{:S(2)}) copy-start(bf16[2,32,128]{2,1,0:T(8,128)(2,1)} %refs_0_.1) | copy-start | bytes 49156
  0.0 18.9 %collective-permute-start.7 = (bf16[32,64,128]{2,1,0:T(8,128)(2,1)}, bf16[32,64,128]{2,1,0:T(8,128)(2,1)S(1)}, u32[]{:S(2)}, u32[]{:S(2)}) collective-permute-start(bf16[32,64,128]{2,1,0:T(8,128)(2,1)} %refs_8_.1), channel_id=1, source_target_pairs={{0,1},{1,0},{2,3},{3,2},{4,5},{5,4},{6,7},{7,6},{8,9},{9,8},{10,11... | collective-permute-start | bytes 1572872 | tf_op jit(solution)/shard_map/ppermute | solution.py:98
  0.5 9.0 %collective-permute-start.5 = (bf16[2,32,128]{2,1,0:T(8,128)(2,1)}, bf16[2,32,128]{2,1,0:T(8,128)(2,1)S(1)}, u32[]{:S(2)}, u32[]{:S(2)}) collective-permute-start(bf16[2,32,128]{2,1,0:T(8,128)(2,1)} %refs_0_.1), channel_id=1, source_target_pairs={{0,4},{2,6},{4,8},{6,10},{8,12},{10,14},{12,0},{14,2},{1,5},{3,7},... | collective-permute-start | bytes 49160 | tf_op jit(solution)/shard_map/ppermute | solution.py:92
  3.1 7.8 %collective-permute-start.4 = (bf16[2,32,128]{2,1,0:T(8,128)(2,1)}, bf16[2,32,128]{2,1,0:T(8,128)(2,1)S(1)}, u32[]{:S(2)}, u32[]{:S(2)}) collective-permute-start(bf16[2,32,128]{2,1,0:T(8,128)(2,1)} %refs_0_.1), channel_id=1, source_target_pairs={{0,6},{2,8},{4,10},{6,12},{8,14},{10,0},{12,2},{14,4},{1,7},{3,9},... | collective-permute-start | bytes 49160 | tf_op jit(solution)/shard_map/ppermute | solution.py:92
  5.6 6.6 %collective-permute-start.3 = (bf16[2,32,128]{2,1,0:T(8,128)(2,1)}, bf16[2,32,128]{2,1,0:T(8,128)(2,1)S(1)}, u32[]{:S(2)}, u32[]{:S(2)}) collective-permute-start(bf16[2,32,128]{2,1,0:T(8,128)(2,1)} %refs_0_.1), channel_id=1, source_target_pairs={{0,8},{2,10},{4,12},{6,14},{8,0},{10,2},{12,4},{14,6},{1,9},{3,11}... | collective-permute-start | bytes 49160 | tf_op jit(solution)/shard_map/ppermute | solution.py:92
  6.8 6.1 %collective-permute-start.2 = (bf16[2,32,128]{2,1,0:T(8,128)(2,1)}, bf16[2,32,128]{2,1,0:T(8,128)(2,1)S(1)}, u32[]{:S(2)}, u32[]{:S(2)}) collective-permute-start(bf16[2,32,128]{2,1,0:T(8,128)(2,1)} %refs_0_.1), channel_id=1, source_target_pairs={{0,10},{2,12},{4,14},{6,0},{8,2},{10,4},{12,6},{14,8},{1,11},{3,13... | collective-permute-start | bytes 49160 | tf_op jit(solution)/shard_map/ppermute | solution.py:92
  9.5 4.0 %collective-permute-start.1 = (bf16[2,32,128]{2,1,0:T(8,128)(2,1)}, bf16[2,32,128]{2,1,0:T(8,128)(2,1)S(1)}, u32[]{:S(2)}, u32[]{:S(2)}) collective-permute-start(bf16[2,32,128]{2,1,0:T(8,128)(2,1)} %refs_0_.1), channel_id=1, source_target_pairs={{0,12},{2,14},{4,0},{6,2},{8,4},{10,6},{12,8},{14,10},{1,13},{3,15... | collective-permute-start | bytes 49160 | tf_op jit(solution)/shard_map/ppermute | solution.py:92
  10.8 4.0 %collective-permute-start = (bf16[2,32,128]{2,1,0:T(8,128)(2,1)}, bf16[2,32,128]{2,1,0:T(8,128)(2,1)S(1)}, u32[]{:S(2)}, u32[]{:S(2)}) collective-permute-start(bf16[2,32,128]{2,1,0:T(8,128)(2,1)} %refs_0_.1), channel_id=1, source_target_pairs={{0,14},{2,0},{4,2},{6,4},{8,6},{10,8},{12,10},{14,12},{1,15},{3,1}... | collective-permute-start | bytes 49160 | tf_op jit(solution)/shard_map/ppermute | solution.py:92
  12.2 6.6 %collective-permute-start.6 = (bf16[2,32,128]{2,1,0:T(8,128)(2,1)}, bf16[2,32,128]{2,1,0:T(8,128)(2,1)S(1)}, u32[]{:S(2)}, u32[]{:S(2)}) collective-permute-start(bf16[2,32,128]{2,1,0:T(8,128)(2,1)} %refs_0_.1), channel_id=1, source_target_pairs={{0,2},{2,4},{4,6},{6,8},{8,10},{10,12},{12,14},{14,0},{1,3},{3,5},... | collective-permute-start | bytes 49160 | tf_op jit(solution)/shard_map/ppermute | solution.py:92
  12.9 6.0 %copy-start.3 = (s32[32]{0:T(128)S(1)}, s32[32]{0:T(128)}, u32[]{:S(2)}) copy-start(s32[32]{0:T(128)} %lens_ref.1) | copy-start | bytes 388
  18.9 1.0 %copy-start = (bf16[32,64,128]{2,1,0:T(8,128)(2,1)S(1)}, bf16[32,64,128]{2,1,0:T(8,128)(2,1)}, u32[]{:S(2)}) copy-start(bf16[32,64,128]{2,1,0:T(8,128)(2,1)} %refs_8_.1) | copy-start | bytes 1572868
  24.6 0.6 %copy-start.2 = (f32[2,32]{1,0:T(2,128)}, f32[2,32]{1,0:T(2,128)S(1)}, u32[]{:S(2)}) copy-start(f32[2,32]{1,0:T(2,128)S(1)} %get-tuple-element.13.refs_0_) | copy-start | bytes 772
  24.6 4.5 %collective-permute-start.8 = (f32[2,32]{1,0:T(2,128)S(1)}, f32[2,32]{1,0:T(2,128)S(1)}, u32[]{:S(2)}, u32[]{:S(2)}) collective-permute-start(f32[2,32]{1,0:T(2,128)S(1)} %get-tuple-element.14), channel_id=1, source_target_pairs={{0,14},{2,0},{4,2},{6,4},{8,6},{10,8},{12,10},{14,12},{1,15},{3,1}... | collective-permute-start | bytes 776 | tf_op jit(solution)/shard_map/ppermute | solution.py:92
  25.2 6.0 %collective-permute-start.9 = (f32[2,32]{1,0:T(2,128)S(1)}, f32[2,32]{1,0:T(2,128)S(1)}, u32[]{:S(2)}, u32[]{:S(2)}) collective-permute-start(f32[2,32]{1,0:T(2,128)S(1)} %get-tuple-element.15), channel_id=1, source_target_pairs={{0,12},{2,14},{4,0},{6,2},{8,4},{10,6},{12,8},{14,10},{1,13},{3,15... | collective-permute-start | bytes 776 | tf_op jit(solution)/shard_map/ppermute | solution.py:92
  25.2 7.4 %collective-permute-start.10 = (f32[2,32]{1,0:T(2,128)S(1)}, f32[2,32]{1,0:T(2,128)S(1)}, u32[]{:S(2)}, u32[]{:S(2)}) collective-permute-start(f32[2,32]{1,0:T(2,128)S(1)} %get-tuple-element.16), channel_id=1, source_target_pairs={{0,10},{2,12},{4,14},{6,0},{8,2},{10,4},{12,6},{14,8},{1,11},{3,13... | collective-permute-start | bytes 776 | tf_op jit(solution)/shard_map/ppermute | solution.py:92
  26.5 6.2 %collective-permute-start.11 = (f32[2,32]{1,0:T(2,128)S(1)}, f32[2,32]{1,0:T(2,128)S(1)}, u32[]{:S(2)}, u32[]{:S(2)}) collective-permute-start(f32[2,32]{1,0:T(2,128)S(1)} %get-tuple-element.17), channel_id=1, source_target_pairs={{0,8},{2,10},{4,12},{6,14},{8,0},{10,2},{12,4},{14,6},{1,9},{3,11}... | collective-permute-start | bytes 776 | tf_op jit(solution)/shard_map/ppermute | solution.py:92
  29.1 5.4 %collective-permute-start.12 = (f32[2,32]{1,0:T(2,128)S(1)}, f32[2,32]{1,0:T(2,128)S(1)}, u32[]{:S(2)}, u32[]{:S(2)}) collective-permute-start(f32[2,32]{1,0:T(2,128)S(1)} %get-tuple-element.18), channel_id=1, source_target_pairs={{0,6},{2,8},{4,10},{6,12},{8,14},{10,0},{12,2},{14,4},{1,7},{3,9},... | collective-permute-start | bytes 776 | tf_op jit(solution)/shard_map/ppermute | solution.py:92
  29.1 2.1 %copy-start.4 = (f32[2,32]{1,0:T(2,128)}, f32[2,32]{1,0:T(2,128)S(1)}, u32[]{:S(2)}) copy-start(f32[2,32]{1,0:T(2,128)S(1)} %collective-permute-done.8.refs_1_) | copy-start | bytes 772
  29.1 5.9 %collective-permute-start.13 = (f32[2,32]{1,0:T(2,128)S(1)}, f32[2,32]{1,0:T(2,128)S(1)}, u32[]{:S(2)}, u32[]{:S(2)}) collective-permute-start(f32[2,32]{1,0:T(2,128)S(1)} %get-tuple-element.19), channel_id=1, source_target_pairs={{0,4},{2,6},{4,8},{6,10},{8,12},{10,14},{12,0},{14,2},{1,5},{3,7},... | collective-permute-start | bytes 776 | tf_op jit(solution)/shard_map/ppermute | solution.py:92
  31.2 1.5 %copy-start.5 = (f32[2,32]{1,0:T(2,128)}, f32[2,32]{1,0:T(2,128)S(1)}, u32[]{:S(2)}) copy-start(f32[2,32]{1,0:T(2,128)S(1)} %collective-permute-done.9.refs_2_) | copy-start | bytes 772
  31.2 6.3 %collective-permute-start.14 = (f32[2,32]{1,0:T(2,128)S(1)}, f32[2,32]{1,0:T(2,128)S(1)}, u32[]{:S(2)}, u32[]{:S(2)}) collective-permute-start(f32[2,32]{1,0:T(2,128)S(1)} %get-tuple-element.20), channel_id=1, source_target_pairs={{0,2},{2,4},{4,6},{6,8},{8,10},{10,12},{12,14},{14,0},{1,3},{3,5},... | collective-permute-start | bytes 776 | tf_op jit(solution)/shard_map/ppermute | solution.py:92
  32.6 4.9 %copy-start.6 = (f32[2,32]{1,0:T(2,128)}, f32[2,32]{1,0:T(2,128)S(1)}, u32[]{:S(2)}) copy-start(f32[2,32]{1,0:T(2,128)S(1)} %collective-permute-done.10.refs_3_) | copy-start | bytes 772
  32.6 4.9 %copy-start.7 = (f32[2,32]{1,0:T(2,128)}, f32[2,32]{1,0:T(2,128)S(1)}, u32[]{:S(2)}) copy-start(f32[2,32]{1,0:T(2,128)S(1)} %collective-permute-done.11.refs_4_) | copy-start | bytes 772
  34.4 3.1 %copy-start.8 = (f32[2,32]{1,0:T(2,128)}, f32[2,32]{1,0:T(2,128)S(1)}, u32[]{:S(2)}) copy-start(f32[2,32]{1,0:T(2,128)S(1)} %collective-permute-done.12.refs_5_) | copy-start | bytes 772
  35.0 2.5 %copy-start.9 = (f32[2,32]{1,0:T(2,128)}, f32[2,32]{1,0:T(2,128)S(1)}, u32[]{:S(2)}) copy-start(f32[2,32]{1,0:T(2,128)S(1)} %collective-permute-done.13.refs_6_) | copy-start | bytes 772
  37.5 0.6 %copy-start.10 = (f32[2,32]{1,0:T(2,128)}, f32[2,32]{1,0:T(2,128)S(1)}, u32[]{:S(2)}) copy-start(f32[2,32]{1,0:T(2,128)S(1)} %collective-permute-done.14.refs_7_) | copy-start | bytes 772

commit v2 on v0

v2 whole, which is shorter than its diff:
```python
import functools

import jax
import jax.numpy as jnp
from jax import lax
from jax.experimental import pallas as pl
from jax.experimental.pallas import tpu as pltpu
from jax.sharding import PartitionSpec as P

INDEX_AXES = ("shard", "qgrp")
ALL_AXES = ("shard", "qgrp", "dim")
LOW = -1e30
LANES = 128
BLOCK = 256


def bits_of(size):
    return size.bit_length() - 1


def score_kernel(n_pieces, me_ref, lens_ref, *refs):
    piece_refs = refs[:n_pieces]
    own_ref, other_ref = refs[n_pieces: n_pieces + 2]
    out_refs = refs[n_pieces + 2: -2]
    flat_ref, max_ref = refs[-2:]
    core = me_ref[0]
    q_tokens, width = piece_refs[0].shape[1:]
    count, half, _ = own_ref.shape
    total = flat_ref.shape[0]
    firsts = n_pieces - len(out_refs) + 1
    at = 0
    for k in range(firsts - 1, n_pieces):
        rows = piece_refs[k].shape[0] * q_tokens
        piece = piece_refs[k][...].reshape(rows, width)
        if k == firsts - 1 and firsts == 2:
            piece = jnp.where(core == 0, piece_refs[0][...].reshape(rows, width), piece)
        flat_ref[pl.ds(at, rows), :] = piece
        at += rows
    block = min(total, BLOCK)
    step = min(count, 8)
    rows = lax.broadcasted_iota(jnp.int32, (half, block), 0)
    own_at = core * half

    def group(g, _):
        start = g * step
        for at in range(0, total, block):
            flat = flat_ref[pl.ds(at, block), :]
            scores = []
            for ref in (own_ref, other_ref):
                docs = ref[pl.ds(start, step)].reshape(step * half, width)
                scores.append(lax.dot_general(
                    docs, flat, (((1,), (1,)), ((), ())), preferred_element_type=jnp.float32
                ))
            for k in range(step):
                length = lens_ref[start + k]
                one = jnp.where(rows < length - own_at, scores[0][k * half: (k + 1) * half], LOW)
                two = jnp.where(rows < length - (half - own_at), scores[1][k * half: (k + 1) * half], LOW)
                best = jnp.max(jnp.maximum(one, two), axis=0, keepdims=True)
                max_ref[pl.ds(start + k, 1), pl.ds(at, block)] = best
        return 0

    lax.fori_loop(0, count // step, group, 0)
    summed = jnp.sum(max_ref[...].T.reshape(total // q_tokens, q_tokens, count), axis=1)
    q_each = out_refs[0].shape[0]
    for r, out_ref in enumerate(out_refs):
        out_ref[...] = summed[r * q_each: (r + 1) * q_each]


def score(core, doc_lens, pieces, doc_tokens, other, outs):
    smem = pl.BlockSpec(memory_space=pltpu.SMEM)
    vmem = pl.BlockSpec(memory_space=pltpu.VMEM)
    count = doc_tokens.shape[0]
    used = pieces if len(pieces) <= outs else pieces[1:]
    queries = sum(p.shape[0] for p in used)
    q_tokens, width = pieces[0].shape[1:]
    return pl.pallas_call(
        functools.partial(score_kernel, len(pieces)),
        out_shape=[jax.ShapeDtypeStruct((queries // outs, count), jnp.float32)] * outs,
        in_specs=[smem, smem] + [vmem] * (len(pieces) + 2),
        out_specs=[vmem] * outs,
        scratch_shapes=[
            pltpu.VMEM((queries * q_tokens, width), jnp.bfloat16),
            pltpu.VMEM((count, queries * q_tokens), jnp.float32),
        ],
        compiler_params=pltpu.CompilerParams(vmem_limit_bytes=24 * 1024 * 1024),
        name="score",
    )(core.reshape(1), doc_lens, *pieces, doc_tokens, other)


def pick_kernel(n_pieces, place, where_ref, cand_ref, *refs):
    piece_refs, out_ref = refs[:n_pieces], refs[n_pieces]
    parts = [ref[...] for ref in piece_refs]
    table = jnp.concatenate(parts, axis=1) if len(parts) > 1 else parts[0]
    size = table.shape[1]
    cand = cand_ref[...]
    rows, width = cand.shape
    spot = place(cand, where_ref)
    for at in range(0, width, LANES):
        wide = min(LANES, width - at)
        index = spot[:, at: at + wide]
        if wide < LANES:
            index = jnp.concatenate([index, jnp.zeros((rows, LANES - wide), jnp.int32)], axis=1)
        low = jnp.bitwise_and(index, LANES - 1)
        high = lax.shift_right_logical(index, bits_of(LANES))
        value = jnp.zeros((rows, LANES), jnp.float32)
        for t in range(0, size, LANES):
            found = jnp.take_along_axis(table[:, t: t + LANES], low, axis=1, mode="promise_in_bounds")
            value = jnp.where(high == t // LANES, found, value)
        out_ref[:, pl.ds(at, wide)] = value[:, :wide]


def pick(place, where, candidates, pieces):
    smem = pl.BlockSpec(memory_space=pltpu.SMEM)
    vmem = pl.BlockSpec(memory_space=pltpu.VMEM)
    return pl.pallas_call(
        functools.partial(pick_kernel, len(pieces), place),
        out_shape=jax.ShapeDtypeStruct(candidates.shape, jnp.float32),
        in_specs=[smem, vmem] + [vmem] * len(pieces),
        out_specs=vmem,
        name="pick",
    )(where, candidates, *pieces)


def two_columns(queries, doc_tokens, other, doc_lens, candidates, n_z, core):
    count = doc_tokens.shape[0]

    def flat(z, x, d):
        return ((z % n_z) * 2 + x) * 2 + d

    def to_scorer(array, r):
        pairs = [(flat(z + r, x ^ d, d), flat(z, x, d)) for z in range(n_z) for x in range(2) for d in range(2)]
        return lax.ppermute(array, ALL_AXES, [pair for pair in pairs if pair[0] != pair[1]])

    def to_owner(array, r):
        pairs = [(flat(z, x, d), flat(z + r, x ^ d, d)) for z in range(n_z) for x in range(2) for d in range(2)]
        return lax.ppermute(array, ALL_AXES, [pair for pair in pairs if pair[0] != pair[1]])

    def to_core(array):
        return lax.ppermute(array, "dim", [(0, 1), (1, 0)])

    pieces = [queries] + [to_scorer(queries, r) for r in range(n_z)]
    blocks = score(core, doc_lens, pieces, doc_tokens, other, n_z)
    moved = [to_owner(block, r) for r, block in enumerate(blocks)]
    moved[0] = jnp.where(core == 0, blocks[0], moved[0])
    crossed = [to_core(block) for block in moved]

    def place(cand, where_ref):
        p = jnp.bitwise_and(cand, count - 1)
        chip = lax.shift_right_logical(cand, bits_of(count))
        r = jnp.bitwise_and(where_ref[0] - lax.shift_right_logical(chip, 1), n_z - 1)
        side = jnp.bitwise_and(jnp.bitwise_xor(chip, where_ref[1]), 1)
        return (side * n_z + r) * count + p

    where = jnp.stack([lax.axis_index("shard"), lax.axis_index("qgrp") ^ core])
    return pick(place, where, candidates, moved + crossed)


def any_columns(queries, doc_tokens, other, doc_lens, candidates, n, core):
    q_owned = candidates.shape[0]
    count = doc_tokens.shape[0]
    gathered = lax.all_gather(queries, INDEX_AXES, axis=0, tiled=True)
    block = score(core, doc_lens, [gathered], doc_tokens, other, 1)[0]
    moved = lax.all_to_all(
        block.reshape(n, q_owned, count), INDEX_AXES, split_axis=0, concat_axis=0, tiled=True
    )
    table = moved.transpose(1, 0, 2).reshape(q_owned, n * count)
    return pick(lambda cand, where_ref: cand, jnp.zeros((1,), jnp.int32), candidates, [table])


def per_device(queries, doc_tokens, doc_lens, candidates):
    n_z, n_x, cores = (lax.axis_size(axis) for axis in ALL_AXES)
    count = doc_tokens.shape[0]
    core = lax.axis_index("dim")
    other = lax.ppermute(doc_tokens, "dim", [(s, cores - 1 - s) for s in range(cores)])
    power = count & (count - 1) == 0 and n_z & (n_z - 1) == 0
    if n_x == 2 and cores == 2 and n_z <= 8 and power:
        return two_columns(queries, doc_tokens, other, doc_lens, candidates, n_z, core)
    return any_columns(queries, doc_tokens, other, doc_lens, candidates, n_z * n_x, core)


def solution(mesh):
    in_specs = (
        P(("groups",) + INDEX_AXES, None, None),
        P(("groups",) + INDEX_AXES, "dim", None),
        P(("groups",) + INDEX_AXES),
        P(("groups",) + INDEX_AXES, None),
    )
    out_specs = P(("groups",) + INDEX_AXES, None)
    return jax.shard_map(
        per_device, mesh=mesh, in_specs=in_specs, out_specs=out_specs, check_vma=False
    )
```

time: 113 us -> 29.4 us (0.26)
  blocking collectives: 32.6 us -> 0 us
  local copies, waits for them, and re-layouts: 27.8 us -> 2.1 us
  waiting for transfers between devices: 25.7 us -> 4.92 us
  between operations: 13.4 us -> 0.09 us
  starting transfers between devices: 5.9 us -> 17.9 us
  matrix products: 4.87 us -> 0 us
  Pallas kernels: 0 us -> 3.5 us
  other arithmetic: 1.73 us -> 0.58 us
    all_gather x1 -> x0, blocking collectives: 32.6 us -> none  [per_device(): lax.all_gather(queries, ('shard', 'qgrp'), axis=0, tiled=True)]
    gather x3 -> x0, local copies, waits for them, and re-layouts: 25.8 us -> none  [per_device(): return jnp.take_along_axis(passage_score, candidates, axis=1)]
    pmax x1 -> x0, waiting for transfers between devices: 19.3 us -> none  [per_device(): maxima = lax.pmax(maxima, 'dim')]
    ppermute x0 -> x13, starting transfers between devices: none -> 17.9 us  [the longest x4 6.45 us: to_scorer(): lax.ppermute(array, ALL_AXES, [pair for pair in pairs if pair[0] != pair[...]
    all_to_all x1 -> x0, waiting for transfers between devices: 6.41 us -> none  [per_device(): lax.all_to_all(block.reshape(n_shard * n_qgrp, q_owned, 1, local_pas), ('...]
    all_to_all x1 -> x0, starting transfers between devices: 5.9 us -> none  [per_device(): lax.all_to_all(block.reshape(n_shard * n_qgrp, q_owned, 1, local_pas), ('...]
    ppermute x0 -> x13, waiting for transfers between devices: none -> 4.92 us  [the longest x4 4.73 us: to_scorer(): lax.ppermute(array, ALL_AXES, [pair for pair in pairs if pair[0] != pair[...]
    dot_general x4 -> x0, matrix products: 4.87 us -> none  [one_tile(): jnp.dot(flat_queries, tile.T, preferred_element_type=jnp.float32)]
  transfers between devices with their start and end apart: 2 -> 13, of which waited for: 2 -> 4; matrix products, arithmetic and copies ran while one was open for 0% -> 2% of each run, Pallas kernels for 0% -> 0%
where the time goes in v2:
time: 29.4 us; the launch traced here: 29.1 us
  starting transfers between devices  17.9 us (61%)
  waiting for transfers between devices  4.92 us (17%)
  Pallas kernels  3.5 us (12%)
  local copies, waits for them, and re-layouts  2.1 us (7%)
  other arithmetic  0.58 us (2%)
    ppermute x4, starting transfers between devices, to_scorer(): lax.ppermute(array, ALL_AXES, [pair for pair in pairs if pair[0] != pair[...  6.45 us
    ppermute x4, starting transfers between devices, to_core(): return lax.ppermute(array, 'dim', [(0, 1), (1, 0)])  5.97 us
    ppermute x4, starting transfers between devices, to_owner(): lax.ppermute(array, ALL_AXES, [pair for pair in pairs if pair[0] != pair[...  5.07 us
    ppermute x4, waiting for transfers between devices, to_scorer(): lax.ppermute(array, ALL_AXES, [pair for pair in pairs if pair[0] != pair[...  4.73 us
    unnamed x22, local copies, waits for them, and re-layouts  2.1 us
    pallas_call x1, Pallas kernels, score(): pl.pallas_call(functools.partial(score_kernel, len(pieces)), out_shape=[j...  1.92 us
    pallas_call x1, Pallas kernels, pick(): pl.pallas_call(functools.partial(pick_kernel, len(pieces), place), out_sh...  1.58 us
  transfers between devices with their start and end apart: 13, of which 4 were waited for; matrix products, arithmetic and copies ran while one was open for 2% of the time, Pallas kernels for 0%

profile of v2, /device:TPU:0, one launch (start us, length us, event | category | flops | bytes accessed | tf_op | source)
XLA Modules:
  0.0 29.1 jit_solution(10408639143438479884)
XLA Ops:
  0.0 0.5 %collective-permute-start.4 = (bf16[32,64,128]{2,1,0:T(8,128)(2,1)}, bf16[32,64,128]{2,1,0:T(8,128)(2,1)S(1)}, u32[]{:S(2)}, u32[]{:S(2)}) collective-permute-start(bf16[32,64,128]{2,1,0:T(8,128)(2,1)} %refs_5_.1), channel_id=1, source_target_pairs={{0,1},{1,0},{2,3},{3,2},{4,5},{5,4},{6,7},{7,6},{8,9},{9,8},{10,11... | collective-permute-start | bytes 1572872 | tf_op jit(solution)/shard_map/ppermute | solution.py:174
  0.5 0.7 %collective-permute-start = (bf16[2,32,128]{2,1,0:T(8,128)(2,1)}, bf16[2,32,128]{2,1,0:T(8,128)(2,1)S(1)}, u32[]{:S(2)}, u32[]{:S(2)}) collective-permute-start(bf16[2,32,128]{2,1,0:T(8,128)(2,1)} %refs_0_.1), channel_id=1, source_target_pairs={{3,1},{1,3},{7,5},{5,7},{11,9},{9,11},{15,13},{13,15},{19,17},{17,... | collective-permute-start | bytes 49160 | tf_op jit(solution)/shard_map/ppermute | solution.py:132
  1.1 4.8 %collective-permute-start.1 = (bf16[2,32,128]{2,1,0:T(8,128)(2,1)}, bf16[2,32,128]{2,1,0:T(8,128)(2,1)S(1)}, u32[]{:S(2)}, u32[]{:S(2)}) collective-permute-start(bf16[2,32,128]{2,1,0:T(8,128)(2,1)} %refs_0_.1), channel_id=1, source_target_pairs={{4,0},{7,1},{6,2},{5,3},{8,4},{11,5},{10,6},{9,7},{12,8},{15,9},{1... | collective-permute-start | bytes 49160 | tf_op jit(solution)/shard_map/ppermute | solution.py:132
  5.9 0.0 collective-permute-start.2
  5.9 1.0 %collective-permute-start.3 = (bf16[2,32,128]{2,1,0:T(8,128)(2,1)}, bf16[2,32,128]{2,1,0:T(8,128)(2,1)S(1)}, u32[]{:S(2)}, u32[]{:S(2)}) collective-permute-start(bf16[2,32,128]{2,1,0:T(8,128)(2,1)} %refs_0_.1), channel_id=1, source_target_pairs={{12,0},{15,1},{14,2},{13,3},{0,4},{3,5},{2,6},{1,7},{4,8},{7,9},{6... | collective-permute-start | bytes 49160 | tf_op jit(solution)/shard_map/ppermute | solution.py:132
  6.9 0.0 collective-permute-done.refs_1_
  6.9 0.6 %collective-permute-done.1.refs_2_ = bf16[2,32,128]{2,1,0:T(8,128)(2,1)S(1)} collective-permute-done((bf16[2,32,128]{2,1,0:T(8,128)(2,1)}, bf16[2,32,128]{2,1,0:T(8,128)(2,1)S(1)}, u32[]{:S(2)}, u32[]{:S(2)}) %collective-permute-start.1) | collective-permute-done | bytes 16416 | tf_op jit(solution)/shard_map/ppermute | solution.py:132
  7.6 3.2 %collective-permute-done.2.refs_3_ = bf16[2,32,128]{2,1,0:T(8,128)(2,1)S(1)} collective-permute-done((bf16[2,32,128]{2,1,0:T(8,128)(2,1)}, bf16[2,32,128]{2,1,0:T(8,128)(2,1)S(1)}, u32[]{:S(2)}, u32[]{:S(2)}) %collective-permute-start.2) | collective-permute-done | bytes 16416 | tf_op jit(solution)/shard_map/ppermute | solution.py:132
  10.8 0.9 %collective-permute-done.3.refs_4_ = bf16[2,32,128]{2,1,0:T(8,128)(2,1)S(1)} collective-permute-done((bf16[2,32,128]{2,1,0:T(8,128)(2,1)}, bf16[2,32,128]{2,1,0:T(8,128)(2,1)S(1)}, u32[]{:S(2)}, u32[]{:S(2)}) %collective-permute-start.3) | collective-permute-done | bytes 16416 | tf_op jit(solution)/shard_map/ppermute | solution.py:132
  11.7 0.0 collective-permute-done.4.refs_6_
  11.7 1.0 %copy-done = bf16[32,64,128]{2,1,0:T(8,128)(2,1)S(1)} copy-done((bf16[32,64,128]{2,1,0:T(8,128)(2,1)S(1)}, bf16[32,64,128]{2,1,0:T(8,128)(2,1)}, u32[]{:S(2)}) %copy-start) | copy-done | bytes 524312
  12.7 1.9 %score.1 = (f32[2,32]{1,0:T(2,128)S(1)}, f32[2,32]{1,0:T(2,128)S(1)}, f32[2,32]{1,0:T(2,128)S(1)}, f32[2,32]{1,0:T(2,128)S(1)}) custom-call(s32[1]{0:T(128)} %bitcast.2.me_ref, s32[32]{0:T(128)S(1)} %copy-done.2, bf16[2,32,128]{2,1,0:T(8,128)(2,1)S(1)} %copy-done.1, bf16[2,32,128]{2,1,0:T(8,128)(2,1)S(1)} %collective-permute-done.refs_1_, ...), custom_call_target="tpu_custom_call" | custom-call | tf_op jit(solution)/shard_map/score/pallas_call | solution.py:76
  14.6 0.7 %collective-permute-start.5 = (f32[2,32]{1,0:T(2,128)S(1)}, f32[2,32]{1,0:T(2,128)S(1)}, u32[]{:S(2)}, u32[]{:S(2)}) collective-permute-start(f32[2,32]{1,0:T(2,128)S(1)} %get-tuple-element.9), channel_id=1, source_target_pairs={{1,3},{3,1},{5,7},{7,5},{9,11},{11,9},{13,15},{15,13},{17,19},{19,... | collective-permute-start | bytes 776 | tf_op jit(solution)/shard_map/ppermute | solution.py:136
  15.3 0.1 collective-permute-start.6
  15.4 1.5 %collective-permute-start.7 = (f32[2,32]{1,0:T(2,128)S(1)}, f32[2,32]{1,0:T(2,128)S(1)}, u32[]{:S(2)}, u32[]{:S(2)}) collective-permute-start(f32[2,32]{1,0:T(2,128)S(1)} %get-tuple-element.11), channel_id=1, source_target_pairs={{0,8},{1,11},{2,10},{3,9},{4,12},{5,15},{6,14},{7,13},{8,0},{9,3},... | collective-permute-start | bytes 776 | tf_op jit(solution)/shard_map/ppermute | solution.py:136
  16.9 2.8 %collective-permute-start.8 = (f32[2,32]{1,0:T(2,128)S(1)}, f32[2,32]{1,0:T(2,128)S(1)}, u32[]{:S(2)}, u32[]{:S(2)}) collective-permute-start(f32[2,32]{1,0:T(2,128)S(1)} %get-tuple-element.12), channel_id=1, source_target_pairs={{0,12},{1,15},{2,14},{3,13},{4,0},{5,3},{6,2},{7,1},{8,4},{9,7},{1... | collective-permute-start | bytes 776 | tf_op jit(solution)/shard_map/ppermute | solution.py:136
  19.7 0.0 collective-permute-done.5
  19.7 5.2 %collective-permute-start.9 = (f32[2,32]{1,0:T(2,128)S(1)}, f32[2,32]{1,0:T(2,128)S(1)}, u32[]{:S(2)}, u32[]{:S(2)}) collective-permute-start(f32[2,32]{1,0:T(2,128)S(1)} %broadcast_select_fusion.refs_0_), channel_id=1, source_target_pairs={{0,1},{1,0},{2,3},{3,2},{4,5},{5,4},{6,7},{7,6},{8,9},{9,8},{10,11... | collective-permute-start | bytes 776 | tf_op jit(solution)/shard_map/ppermute | solution.py:139
  24.9 0.0 collective-permute-done.6.refs_1_
  24.9 0.3 %collective-permute-start.10 = (f32[2,32]{1,0:T(2,128)S(1)}, f32[2,32]{1,0:T(2,128)S(1)}, u32[]{:S(2)}, u32[]{:S(2)}) collective-permute-start(f32[2,32]{1,0:T(2,128)S(1)} %collective-permute-done.6.refs_1_), channel_id=1, source_target_pairs={{0,1},{1,0},{2,3},{3,2},{4,5},{5,4},{6,7},{7,6},{8,9},{9,8},{10,11... | collective-permute-start | bytes 776 | tf_op jit(solution)/shard_map/ppermute | solution.py:139
  25.2 0.0 collective-permute-done.7.refs_2_
  25.2 0.2 collective-permute-start.11
  25.4 0.0 collective-permute-done.8.refs_3_
  25.4 0.3 %collective-permute-start.12 = (f32[2,32]{1,0:T(2,128)S(1)}, f32[2,32]{1,0:T(2,128)S(1)}, u32[]{:S(2)}, u32[]{:S(2)}) collective-permute-start(f32[2,32]{1,0:T(2,128)S(1)} %collective-permute-done.8.refs_3_), channel_id=1, source_target_pairs={{0,1},{1,0},{2,3},{3,2},{4,5},{5,4},{6,7},{7,6},{8,9},{9,8},{10,11... | collective-permute-start | bytes 776 | tf_op jit(solution)/shard_map/ppermute | solution.py:139
  25.7 0.1 copy-done.5
  25.8 0.6 %pad_add_fusion.where_ref = s32[2]{0:T(128)} fusion(s32[1]{0:T(128)} %bitcast.1, s32[1]{0:T(128)} %bitcast), kind=kLoop, calls=%fused_computation.1 | loop fusion | flops 2 | bytes 16 | tf_op jit(solution)/shard_map/stack | solution.py:154
  26.4 0.0 collective-permute-done.9.refs_4_
  26.4 0.0 collective-permute-done.11.refs_6_
  26.4 0.2 collective-permute-done.12.refs_7_
  26.6 0.4 %copy-done.7 = f32[2,32]{1,0:T(2,128)} copy-done((f32[2,32]{1,0:T(2,128)}, f32[2,32]{1,0:T(2,128)S(1)}, u32[]{:S(2)}) %copy-start.7) | copy-done | bytes 280
  27.0 0.6 %copy-done.10 = f32[2,32]{1,0:T(2,128)} copy-done((f32[2,32]{1,0:T(2,128)}, f32[2,32]{1,0:T(2,128)S(1)}, u32[]{:S(2)}) %copy-start.10) | copy-done | bytes 280
  27.6 1.6 %pick.1 = f32[2,1000]{1,0:T(2,128)} custom-call(s32[2]{0:T(128)} %pad_add_fusion.where_ref, s32[2,1000]{1,0:T(2,128)} %cand_ref.1, f32[2,32]{1,0:T(2,128)} %copy-done.3, f32[2,32]{1,0:T(2,128)} %copy-done.4, f32[2,32]{1,0:T(2,128)} %copy-done.5, f32[2,32]{1,0:T(2,128)} %copy-done.6, f32[2,32]{1,0:T(2,128)} %copy-done.7, f32[2,32]{1,0:T(2,128)} %copy-done.8, ...), custom_call_target="tpu_custom_call" | custom-call | tf_op jit(solution)/shard_map/pick/pallas_call | solution.py:115
  (20 shorter events, 0.0 us)
Async XLA Ops:
  0.0 11.7 %copy-start.1 = (bf16[2,32,128]{2,1,0:T(8,128)(2,1)S(1)}, bf16[2,32,128]{2,1,0:T(8,128)(2,1)}, u32[]{:S(2)}) copy-start(bf16[2,32,128]{2,1,0:T(8,128)(2,1)} %refs_0_.1) | copy-start | bytes 49156
  0.0 11.7 %collective-permute-start.4 = (bf16[32,64,128]{2,1,0:T(8,128)(2,1)}, bf16[32,64,128]{2,1,0:T(8,128)(2,1)S(1)}, u32[]{:S(2)}, u32[]{:S(2)}) collective-permute-start(bf16[32,64,128]{2,1,0:T(8,128)(2,1)} %refs_5_.1), channel_id=1, source_target_pairs={{0,1},{1,0},{2,3},{3,2},{4,5},{5,4},{6,7},{7,6},{8,9},{9,8},{10,11... | collective-permute-start | bytes 1572872 | tf_op jit(solution)/shard_map/ppermute | solution.py:174
  0.5 6.5 %collective-permute-start = (bf16[2,32,128]{2,1,0:T(8,128)(2,1)}, bf16[2,32,128]{2,1,0:T(8,128)(2,1)S(1)}, u32[]{:S(2)}, u32[]{:S(2)}) collective-permute-start(bf16[2,32,128]{2,1,0:T(8,128)(2,1)} %refs_0_.1), channel_id=1, source_target_pairs={{3,1},{1,3},{7,5},{5,7},{11,9},{9,11},{15,13},{13,15},{19,17},{17,... | collective-permute-start | bytes 49160 | tf_op jit(solution)/shard_map/ppermute | solution.py:132
  1.1 6.4 %collective-permute-start.1 = (bf16[2,32,128]{2,1,0:T(8,128)(2,1)}, bf16[2,32,128]{2,1,0:T(8,128)(2,1)S(1)}, u32[]{:S(2)}, u32[]{:S(2)}) collective-permute-start(bf16[2,32,128]{2,1,0:T(8,128)(2,1)} %refs_0_.1), channel_id=1, source_target_pairs={{4,0},{7,1},{6,2},{5,3},{8,4},{11,5},{10,6},{9,7},{12,8},{15,9},{1... | collective-permute-start | bytes 49160 | tf_op jit(solution)/shard_map/ppermute | solution.py:132
  5.9 4.8 %collective-permute-start.2 = (bf16[2,32,128]{2,1,0:T(8,128)(2,1)}, bf16[2,32,128]{2,1,0:T(8,128)(2,1)S(1)}, u32[]{:S(2)}, u32[]{:S(2)}) collective-permute-start(bf16[2,32,128]{2,1,0:T(8,128)(2,1)} %refs_0_.1), channel_id=1, source_target_pairs={{8,0},{11,1},{10,2},{9,3},{12,4},{15,5},{14,6},{13,7},{0,8},{3,9},... | collective-permute-start | bytes 49160 | tf_op jit(solution)/shard_map/ppermute | solution.py:132
  5.9 5.7 %collective-permute-start.3 = (bf16[2,32,128]{2,1,0:T(8,128)(2,1)}, bf16[2,32,128]{2,1,0:T(8,128)(2,1)S(1)}, u32[]{:S(2)}, u32[]{:S(2)}) collective-permute-start(bf16[2,32,128]{2,1,0:T(8,128)(2,1)} %refs_0_.1), channel_id=1, source_target_pairs={{12,0},{15,1},{14,2},{13,3},{0,4},{3,5},{2,6},{1,7},{4,8},{7,9},{6... | collective-permute-start | bytes 49160 | tf_op jit(solution)/shard_map/ppermute | solution.py:132
  6.9 4.7 %copy-start.2 = (s32[32]{0:T(128)S(1)}, s32[32]{0:T(128)}, u32[]{:S(2)}) copy-start(s32[32]{0:T(128)} %lens_ref.1) | copy-start | bytes 388
  11.7 1.0 %copy-start = (bf16[32,64,128]{2,1,0:T(8,128)(2,1)S(1)}, bf16[32,64,128]{2,1,0:T(8,128)(2,1)}, u32[]{:S(2)}) copy-start(bf16[32,64,128]{2,1,0:T(8,128)(2,1)} %refs_5_.1) | copy-start | bytes 1572868
  14.6 5.1 %collective-permute-start.5 = (f32[2,32]{1,0:T(2,128)S(1)}, f32[2,32]{1,0:T(2,128)S(1)}, u32[]{:S(2)}, u32[]{:S(2)}) collective-permute-start(f32[2,32]{1,0:T(2,128)S(1)} %get-tuple-element.9), channel_id=1, source_target_pairs={{1,3},{3,1},{5,7},{7,5},{9,11},{11,9},{13,15},{15,13},{17,19},{19,... | collective-permute-start | bytes 776 | tf_op jit(solution)/shard_map/ppermute | solution.py:136
  15.3 9.6 %collective-permute-start.6 = (f32[2,32]{1,0:T(2,128)S(1)}, f32[2,32]{1,0:T(2,128)S(1)}, u32[]{:S(2)}, u32[]{:S(2)}) collective-permute-start(f32[2,32]{1,0:T(2,128)S(1)} %get-tuple-element.10), channel_id=1, source_target_pairs={{0,4},{1,7},{2,6},{3,5},{4,8},{5,11},{6,10},{7,9},{8,12},{9,15},{1... | collective-permute-start | bytes 776 | tf_op jit(solution)/shard_map/ppermute | solution.py:136
  15.4 9.8 %collective-permute-start.7 = (f32[2,32]{1,0:T(2,128)S(1)}, f32[2,32]{1,0:T(2,128)S(1)}, u32[]{:S(2)}, u32[]{:S(2)}) collective-permute-start(f32[2,32]{1,0:T(2,128)S(1)} %get-tuple-element.11), channel_id=1, source_target_pairs={{0,8},{1,11},{2,10},{3,9},{4,12},{5,15},{6,14},{7,13},{8,0},{9,3},... | collective-permute-start | bytes 776 | tf_op jit(solution)/shard_map/ppermute | solution.py:136
  16.9 8.5 %collective-permute-start.8 = (f32[2,32]{1,0:T(2,128)S(1)}, f32[2,32]{1,0:T(2,128)S(1)}, u32[]{:S(2)}, u32[]{:S(2)}) collective-permute-start(f32[2,32]{1,0:T(2,128)S(1)} %get-tuple-element.12), channel_id=1, source_target_pairs={{0,12},{1,15},{2,14},{3,13},{4,0},{5,3},{6,2},{7,1},{8,4},{9,7},{1... | collective-permute-start | bytes 776 | tf_op jit(solution)/shard_map/ppermute | solution.py:136
  19.7 6.0 %copy-start.3 = (f32[2,32]{1,0:T(2,128)}, f32[2,32]{1,0:T(2,128)S(1)}, u32[]{:S(2)}) copy-start(f32[2,32]{1,0:T(2,128)S(1)} %broadcast_select_fusion.refs_0_) | copy-start | bytes 772
  19.7 6.6 %collective-permute-start.9 = (f32[2,32]{1,0:T(2,128)S(1)}, f32[2,32]{1,0:T(2,128)S(1)}, u32[]{:S(2)}, u32[]{:S(2)}) collective-permute-start(f32[2,32]{1,0:T(2,128)S(1)} %broadcast_select_fusion.refs_0_), channel_id=1, source_target_pairs={{0,1},{1,0},{2,3},{3,2},{4,5},{5,4},{6,7},{7,6},{8,9},{9,8},{10,11... | collective-permute-start | bytes 776 | tf_op jit(solution)/shard_map/ppermute | solution.py:139
  24.9 0.8 %copy-start.4 = (f32[2,32]{1,0:T(2,128)}, f32[2,32]{1,0:T(2,128)S(1)}, u32[]{:S(2)}) copy-start(f32[2,32]{1,0:T(2,128)S(1)} %collective-permute-done.6.refs_1_) | copy-start | bytes 772
  24.9 1.5 %collective-permute-start.10 = (f32[2,32]{1,0:T(2,128)S(1)}, f32[2,32]{1,0:T(2,128)S(1)}, u32[]{:S(2)}, u32[]{:S(2)}) collective-permute-start(f32[2,32]{1,0:T(2,128)S(1)} %collective-permute-done.6.refs_1_), channel_id=1, source_target_pairs={{0,1},{1,0},{2,3},{3,2},{4,5},{5,4},{6,7},{7,6},{8,9},{9,8},{10,11... | collective-permute-start | bytes 776 | tf_op jit(solution)/shard_map/ppermute | solution.py:139
  25.2 0.6 %copy-start.5 = (f32[2,32]{1,0:T(2,128)}, f32[2,32]{1,0:T(2,128)S(1)}, u32[]{:S(2)}) copy-start(f32[2,32]{1,0:T(2,128)S(1)} %collective-permute-done.7.refs_2_) | copy-start | bytes 772
  25.2 1.2 %collective-permute-start.11 = (f32[2,32]{1,0:T(2,128)S(1)}, f32[2,32]{1,0:T(2,128)S(1)}, u32[]{:S(2)}, u32[]{:S(2)}) collective-permute-start(f32[2,32]{1,0:T(2,128)S(1)} %collective-permute-done.7.refs_2_), channel_id=1, source_target_pairs={{0,1},{1,0},{2,3},{3,2},{4,5},{5,4},{6,7},{7,6},{8,9},{9,8},{10,11... | collective-permute-start | bytes 776 | tf_op jit(solution)/shard_map/ppermute | solution.py:139
  25.4 1.1 %copy-start.6 = (f32[2,32]{1,0:T(2,128)}, f32[2,32]{1,0:T(2,128)S(1)}, u32[]{:S(2)}) copy-start(f32[2,32]{1,0:T(2,128)S(1)} %collective-permute-done.8.refs_3_) | copy-start | bytes 772
  25.4 1.1 %collective-permute-start.12 = (f32[2,32]{1,0:T(2,128)S(1)}, f32[2,32]{1,0:T(2,128)S(1)}, u32[]{:S(2)}, u32[]{:S(2)}) collective-permute-start(f32[2,32]{1,0:T(2,128)S(1)} %collective-permute-done.8.refs_3_), channel_id=1, source_target_pairs={{0,1},{1,0},{2,3},{3,2},{4,5},{5,4},{6,7},{7,6},{8,9},{9,8},{10,11... | collective-permute-start | bytes 776 | tf_op jit(solution)/shard_map/ppermute | solution.py:139
  26.4 0.6 %copy-start.7 = (f32[2,32]{1,0:T(2,128)}, f32[2,32]{1,0:T(2,128)S(1)}, u32[]{:S(2)}) copy-start(f32[2,32]{1,0:T(2,128)S(1)} %collective-permute-done.9.refs_4_) | copy-start | bytes 772
  26.4 0.6 %copy-start.8 = (f32[2,32]{1,0:T(2,128)}, f32[2,32]{1,0:T(2,128)S(1)}, u32[]{:S(2)}) copy-start(f32[2,32]{1,0:T(2,128)S(1)} %collective-permute-done.10.refs_5_) | copy-start | bytes 772
  26.4 0.6 %copy-start.9 = (f32[2,32]{1,0:T(2,128)}, f32[2,32]{1,0:T(2,128)S(1)}, u32[]{:S(2)}) copy-start(f32[2,32]{1,0:T(2,128)S(1)} %collective-permute-done.11.refs_6_) | copy-start | bytes 772
  27.0 0.6 %copy-start.10 = (f32[2,32]{1,0:T(2,128)}, f32[2,32]{1,0:T(2,128)S(1)}, u32[]{:S(2)}) copy-start(f32[2,32]{1,0:T(2,128)S(1)} %collective-permute-done.12.refs_7_) | copy-start | bytes 772

commit v3 on v2

v3 whole, which is shorter than its diff:
```python
import functools

import jax
import jax.numpy as jnp
from jax import lax
from jax.experimental import pallas as pl
from jax.experimental.pallas import tpu as pltpu
from jax.sharding import PartitionSpec as P

INDEX_AXES = ("shard", "qgrp")
ALL_AXES = ("shard", "qgrp", "dim")
LOW = -1e30
LANES = 128
BLOCK = 256


def score_kernel(n_pieces, me_ref, lens_ref, *refs):
    piece_refs = refs[:n_pieces]
    own_ref, other_ref = refs[n_pieces: n_pieces + 2]
    out_refs = refs[n_pieces + 2: -4]
    flat_ref, max_ref, held_ref, sem = refs[-4:]
    core = me_ref[0]
    q_tokens, width = piece_refs[0].shape[1:]
    count, half, _ = own_ref.shape
    total = flat_ref.shape[0]
    fetch = pltpu.make_async_copy(own_ref, held_ref, sem)
    fetch.start()
    at = 0
    for piece_ref in piece_refs:
        rows = piece_ref.shape[0] * q_tokens
        flat_ref[pl.ds(at, rows), :] = piece_ref[...].reshape(rows, width)
        at += rows
    block = min(total, BLOCK)
    step = min(count, 8)
    rows = lax.broadcasted_iota(jnp.int32, (half, block), 0)

    def best_of(ref, first, fold):
        def group(g, _):
            start = g * step
            docs = ref[pl.ds(start, step)].reshape(step * half, width)
            for at in range(0, total, block):
                flat = flat_ref[pl.ds(at, block), :]
                scores = lax.dot_general(
                    docs, flat, (((1,), (1,)), ((), ())), preferred_element_type=jnp.float32
                )
                for k in range(step):
                    part = scores[k * half: (k + 1) * half]
                    part = jnp.where(rows < lens_ref[start + k] - first, part, LOW)
                    best = jnp.max(part, axis=0, keepdims=True)
                    spot = pl.ds(start + k, 1), pl.ds(at, block)
                    max_ref[spot] = jnp.maximum(max_ref[spot], best) if fold else best
            return 0

        lax.fori_loop(0, count // step, group, 0)

    best_of(other_ref, (1 - core) * half, False)
    fetch.wait()
    best_of(held_ref, core * half, True)
    summed = jnp.sum(max_ref[...].T.reshape(total // q_tokens, q_tokens, count), axis=1)
    q_each = out_refs[0].shape[0]
    for r, out_ref in enumerate(out_refs):
        out_ref[...] = summed[r * q_each: (r + 1) * q_each]


def score(core, doc_lens, pieces, doc_tokens, other, outs):
    smem = pl.BlockSpec(memory_space=pltpu.SMEM)
    vmem = pl.BlockSpec(memory_space=pltpu.VMEM)
    hbm = pl.BlockSpec(memory_space=pltpu.HBM)
    count = doc_tokens.shape[0]
    queries = sum(p.shape[0] for p in pieces)
    q_tokens, width = pieces[0].shape[1:]
    return pl.pallas_call(
        functools.partial(score_kernel, len(pieces)),
        out_shape=[jax.ShapeDtypeStruct((queries // outs, count), jnp.float32)] * outs,
        in_specs=[smem, smem] + [vmem] * len(pieces) + [hbm, vmem],
        out_specs=[vmem] * outs,
        scratch_shapes=[
            pltpu.VMEM((queries * q_tokens, width), jnp.bfloat16),
            pltpu.VMEM((count, queries * q_tokens), jnp.float32),
            pltpu.VMEM(doc_tokens.shape, jnp.bfloat16),
            pltpu.SemaphoreType.DMA(()),
        ],
        compiler_params=pltpu.CompilerParams(vmem_limit_bytes=(8 + queries // 16) * 1024 * 1024),
        name="score",
    )(core.reshape(1), doc_lens, *pieces, doc_tokens, other)


def pick_kernel(n_pieces, base_ref, cand_ref, *refs):
    piece_refs, out_ref = refs[:n_pieces], refs[n_pieces]
    parts = [ref[...] for ref in piece_refs]
    table = jnp.concatenate(parts, axis=1) if len(parts) > 1 else parts[0]
    size = table.shape[1]
    rows, width = cand_ref.shape
    spot = jnp.bitwise_xor(cand_ref[...], base_ref[0])
    for at in range(0, width, LANES):
        wide = min(LANES, width - at)
        index = spot[:, at: at + wide]
        if wide < LANES:
            index = jnp.concatenate([index, jnp.zeros((rows, LANES - wide), jnp.int32)], axis=1)
        low = jnp.bitwise_and(index, LANES - 1)
        high = lax.shift_right_logical(index, LANES.bit_length() - 1)
        value = jnp.zeros((rows, LANES), jnp.float32)
        for t in range(0, size, LANES):
            found = jnp.take_along_axis(table[:, t: t + LANES], low, axis=1, mode="promise_in_bounds")
            value = jnp.where(high == t // LANES, found, value)
        out_ref[:, pl.ds(at, wide)] = value[:, :wide]


def pick(base, candidates, pieces):
    smem = pl.BlockSpec(memory_space=pltpu.SMEM)
    vmem = pl.BlockSpec(memory_space=pltpu.VMEM)
    return pl.pallas_call(
        functools.partial(pick_kernel, len(pieces)),
        out_shape=jax.ShapeDtypeStruct(candidates.shape, jnp.float32),
        in_specs=[smem, vmem] + [vmem] * len(pieces),
        out_specs=vmem,
        compiler_params=pltpu.CompilerParams(vmem_limit_bytes=4 * 1024 * 1024),
        name="pick",
    )(base.reshape(1), candidates, *pieces)


def two_columns(queries, doc_tokens, other, doc_lens, candidates, n_z, core):
    count = doc_tokens.shape[0]

    def exchange(array, r):
        pairs = [
            ((z * 2 + x) * 2 + d, ((z ^ r) * 2 + (x ^ d)) * 2 + d)
            for z in range(n_z) for x in range(2) for d in range(2)
        ]
        return lax.ppermute(array, ALL_AXES, pairs)

    pieces = [exchange(queries, r) for r in range(n_z)]
    blocks = score(core, doc_lens, pieces, doc_tokens, other, n_z)
    table = []
    for r in range(n_z):
        moved = exchange(blocks[r], r)
        table += [moved, lax.ppermute(moved, "dim", [(0, 1), (1, 0)])]
    base = (lax.axis_index("shard") * 2 + (lax.axis_index("qgrp") ^ core)) * count
    return pick(base, candidates, table)


def any_columns(queries, doc_tokens, other, doc_lens, candidates, n, core):
    q_owned = candidates.shape[0]
    count = doc_tokens.shape[0]
    gathered = lax.all_gather(queries, INDEX_AXES, axis=0, tiled=True)
    block = score(core, doc_lens, [gathered], doc_tokens, other, 1)[0]
    moved = lax.all_to_all(
        block.reshape(n, q_owned, count), INDEX_AXES, split_axis=0, concat_axis=0, tiled=True
    )
    table = moved.transpose(1, 0, 2).reshape(q_owned, n * count)
    return pick(jnp.int32(0), candidates, [table])


def per_device(queries, doc_tokens, doc_lens, candidates):
    n_z, n_x, cores = (lax.axis_size(axis) for axis in ALL_AXES)
    count = doc_tokens.shape[0]
    core = lax.axis_index("dim")
    other = lax.ppermute(doc_tokens, "dim", [(s, cores - 1 - s) for s in range(cores)])
    power = count & (count - 1) == 0 and n_z & (n_z - 1) == 0
    if n_x == 2 and cores == 2 and n_z <= 8 and power:
        return two_columns(queries, doc_tokens, other, doc_lens, candidates, n_z, core)
    return any_columns(queries, doc_tokens, other, doc_lens, candidates, n_z * n_x, core)


def solution(mesh):
    in_specs = (
        P(("groups",) + INDEX_AXES, None, None),
        P(("groups",) + INDEX_AXES, "dim", None),
        P(("groups",) + INDEX_AXES),
        P(("groups",) + INDEX_AXES, None),
    )
    out_specs = P(("groups",) + INDEX_AXES, None)
    return jax.shard_map(
        per_device, mesh=mesh, in_specs=in_specs, out_specs=out_specs, check_vma=False
    )
```

time: 29.4 us -> 29.5 us (level)
  starting transfers between devices: 17.9 us -> 19.1 us
  local copies, waits for them, and re-layouts: 2.1 us -> 1.05 us
  waiting for transfers between devices: 4.92 us -> 5.56 us
  other arithmetic: 0.58 us -> 0 us
    ppermute x12, starting transfers between devices: 17.5 us -> 18.7 us  [the longest x8 11.6 us: exchange(): return lax.ppermute(array, ALL_AXES, pairs)]
    unnamed x22 -> x6, local copies, waits for them, and re-layouts: 2.1 us -> 1.05 us
    pallas_call x1, Pallas kernels: 1.58 us -> 0.78 us  [pick(): pl.pallas_call(functools.partial(pick_kernel, len(pieces)), out_shape=jax...]
    pallas_call x1, Pallas kernels: 1.92 us -> 2.69 us  [score(): pl.pallas_call(functools.partial(score_kernel, len(pieces)), out_shape=[j...]
    ppermute x12, waiting for transfers between devices: 4.92 us -> 5.56 us  [the longest x8 4.75 us: exchange(): return lax.ppermute(array, ALL_AXES, pairs)]
    another operation x1 -> x0, other arithmetic: 0.58 us -> none  [two_columns(): where = jnp.stack([lax.axis_index('shard'), lax.axis_index('qgrp') ^ core])]
  transfers between devices with their start and end apart: 13 -> 13, of which waited for: 4 -> 3; matrix products, arithmetic and copies ran while one was open for 2% -> 0% of each run, Pallas kernels for 0% -> 0%
where the time goes in v3:
time: 29.5 us; the launch traced here: 29.3 us
  starting transfers between devices  19.1 us (65%)
  waiting for transfers between devices  5.56 us (19%)
  Pallas kernels  3.47 us (12%)
  local copies, waits for them, and re-layouts  1.05 us (4%)
    ppermute x8, starting transfers between devices, exchange(): return lax.ppermute(array, ALL_AXES, pairs)  11.6 us
    ppermute x4, starting transfers between devices, two_columns(): table += [moved, lax.ppermute(moved, 'dim', [(0, 1), (1, 0)])]  7.05 us
    ppermute x8, waiting for transfers between devices, exchange(): return lax.ppermute(array, ALL_AXES, pairs)  4.75 us
    pallas_call x1, Pallas kernels, score(): pl.pallas_call(functools.partial(score_kernel, len(pieces)), out_shape=[j...  2.69 us
    unnamed x6, local copies, waits for them, and re-layouts  1.05 us
    ppermute x4, waiting for transfers between devices, two_columns(): table += [moved, lax.ppermute(moved, 'dim', [(0, 1), (1, 0)])]  0.82 us
    pallas_call x1, Pallas kernels, pick(): pl.pallas_call(functools.partial(pick_kernel, len(pieces)), out_shape=jax...  0.78 us
  transfers between devices with their start and end apart: 13, of which 3 were waited for; matrix products, arithmetic and copies ran while one was open for 0% of the time, Pallas kernels for 0%

profile of v3, /device:TPU:0, one launch (start us, length us, event | category | flops | bytes accessed | tf_op | source)
XLA Modules:
  0.0 29.3 jit_solution(1995088073209187157)
XLA Ops:
  0.0 0.5 %collective-permute-start.4 = (bf16[32,64,128]{2,1,0:T(8,128)(2,1)}, bf16[32,64,128]{2,1,0:T(8,128)(2,1)S(1)}, u32[]{:S(2)}, u32[]{:S(2)}) collective-permute-start(bf16[32,64,128]{2,1,0:T(8,128)(2,1)} %refs_4_.1), channel_id=1, source_target_pairs={{0,1},{1,0},{2,3},{3,2},{4,5},{5,4},{6,7},{7,6},{8,9},{9,8},{10,11... | collective-permute-start | bytes 1572872 | tf_op jit(solution)/shard_map/ppermute | solution.py:158
  0.5 2.6 %collective-permute-start.1 = (bf16[2,32,128]{2,1,0:T(8,128)(2,1)}, bf16[2,32,128]{2,1,0:T(8,128)(2,1)S(1)}, u32[]{:S(2)}, u32[]{:S(2)}) collective-permute-start(bf16[2,32,128]{2,1,0:T(8,128)(2,1)} %param.4), channel_id=1, source_target_pairs={{0,4},{1,7},{2,6},{3,5},{4,0},{5,3},{6,2},{7,1},{8,12},{9,15},{10,... | collective-permute-start | bytes 49160 | tf_op jit(solution)/shard_map/ppermute | solution.py:130
  3.0 1.4 %collective-permute-start = (bf16[2,32,128]{2,1,0:T(8,128)(2,1)}, bf16[2,32,128]{2,1,0:T(8,128)(2,1)S(1)}, u32[]{:S(2)}, u32[]{:S(2)}) collective-permute-start(bf16[2,32,128]{2,1,0:T(8,128)(2,1)} %param.4), channel_id=1, source_target_pairs={{0,0},{1,3},{2,2},{3,1},{4,4},{5,7},{6,6},{7,5},{8,8},{9,11},{10,1... | collective-permute-start | bytes 49160 | tf_op jit(solution)/shard_map/ppermute | solution.py:130
  4.4 2.5 %collective-permute-start.3 = (bf16[2,32,128]{2,1,0:T(8,128)(2,1)}, bf16[2,32,128]{2,1,0:T(8,128)(2,1)S(1)}, u32[]{:S(2)}, u32[]{:S(2)}) collective-permute-start(bf16[2,32,128]{2,1,0:T(8,128)(2,1)} %param.4), channel_id=1, source_target_pairs={{0,12},{1,15},{2,14},{3,13},{4,8},{5,11},{6,10},{7,9},{8,4},{9,7},... | collective-permute-start | bytes 49160 | tf_op jit(solution)/shard_map/ppermute | solution.py:130
  6.9 0.1 collective-permute-start.2
  7.0 0.0 collective-permute-done.1.refs_1_
  7.0 0.0 collective-permute-done.refs_0_
  7.0 3.1 %collective-permute-done.3.refs_3_ = bf16[2,32,128]{2,1,0:T(8,128)(2,1)S(1)} collective-permute-done((bf16[2,32,128]{2,1,0:T(8,128)(2,1)}, bf16[2,32,128]{2,1,0:T(8,128)(2,1)S(1)}, u32[]{:S(2)}, u32[]{:S(2)}) %collective-permute-start.3) | collective-permute-done | bytes 16416 | tf_op jit(solution)/shard_map/ppermute | solution.py:130
  10.1 1.6 %collective-permute-done.2.refs_2_ = bf16[2,32,128]{2,1,0:T(8,128)(2,1)S(1)} collective-permute-done((bf16[2,32,128]{2,1,0:T(8,128)(2,1)}, bf16[2,32,128]{2,1,0:T(8,128)(2,1)S(1)}, u32[]{:S(2)}, u32[]{:S(2)}) %collective-permute-start.2) | collective-permute-done | bytes 16416 | tf_op jit(solution)/shard_map/ppermute | solution.py:130
  11.7 0.0 collective-permute-done.4.refs_5_
  11.7 0.0 copy-done.2
  11.7 1.0 %copy-done = bf16[32,64,128]{2,1,0:T(8,128)(2,1)S(1)} copy-done((bf16[32,64,128]{2,1,0:T(8,128)(2,1)S(1)}, bf16[32,64,128]{2,1,0:T(8,128)(2,1)}, u32[]{:S(2)}) %copy-start) | copy-done | bytes 524312
  12.8 2.7 %score.1 = (f32[2,32]{1,0:T(2,128)S(1)}, f32[2,32]{1,0:T(2,128)S(1)}, f32[2,32]{1,0:T(2,128)S(1)}, f32[2,32]{1,0:T(2,128)S(1)}) custom-call(s32[1]{0:T(128)} %bitcast.1.me_ref, s32[32]{0:T(128)S(1)} %copy-done.2, bf16[2,32,128]{2,1,0:T(8,128)(2,1)S(1)} %collective-permute-done.refs_0_, bf16[2,32,128]{2,1,0:T(8,128)(2,1)S(1)} %collective-permute-done.1.refs_1_, ...), custom_call_target="tpu_custom_call" | custom-call | tf_op jit(solution)/shard_map/score/pallas_call | solution.py:72
  15.5 0.0 copy-start.1
  15.5 0.7 %collective-permute-start.5 = (f32[2,32]{1,0:T(2,128)S(1)}, f32[2,32]{1,0:T(2,128)S(1)}, u32[]{:S(2)}, u32[]{:S(2)}) collective-permute-start(f32[2,32]{1,0:T(2,128)S(1)} %get-tuple-element.9), channel_id=1, source_target_pairs={{0,0},{1,3},{2,2},{3,1},{4,4},{5,7},{6,6},{7,5},{8,8},{9,11},{10,1... | collective-permute-start | bytes 776 | tf_op jit(solution)/shard_map/ppermute | solution.py:130
  16.2 0.8 %collective-permute-start.7 = (f32[2,32]{1,0:T(2,128)S(1)}, f32[2,32]{1,0:T(2,128)S(1)}, u32[]{:S(2)}, u32[]{:S(2)}) collective-permute-start(f32[2,32]{1,0:T(2,128)S(1)} %get-tuple-element.10), channel_id=1, source_target_pairs={{0,4},{1,7},{2,6},{3,5},{4,0},{5,3},{6,2},{7,1},{8,12},{9,15},{10,... | collective-permute-start | bytes 776 | tf_op jit(solution)/shard_map/ppermute | solution.py:130
  16.9 1.2 %collective-permute-start.9 = (f32[2,32]{1,0:T(2,128)S(1)}, f32[2,32]{1,0:T(2,128)S(1)}, u32[]{:S(2)}, u32[]{:S(2)}) collective-permute-start(f32[2,32]{1,0:T(2,128)S(1)} %get-tuple-element.11), channel_id=1, source_target_pairs={{0,8},{1,11},{2,10},{3,9},{4,12},{5,15},{6,14},{7,13},{8,0},{9,3},... | collective-permute-start | bytes 776 | tf_op jit(solution)/shard_map/ppermute | solution.py:130
  18.1 2.5 %collective-permute-start.11 = (f32[2,32]{1,0:T(2,128)S(1)}, f32[2,32]{1,0:T(2,128)S(1)}, u32[]{:S(2)}, u32[]{:S(2)}) collective-permute-start(f32[2,32]{1,0:T(2,128)S(1)} %get-tuple-element.12), channel_id=1, source_target_pairs={{0,12},{1,15},{2,14},{3,13},{4,8},{5,11},{6,10},{7,9},{8,4},{9,7},... | collective-permute-start | bytes 776 | tf_op jit(solution)/shard_map/ppermute | solution.py:130
  20.6 0.0 collective-permute-done.5.refs_0_
  20.6 4.9 %collective-permute-start.6 = (f32[2,32]{1,0:T(2,128)S(1)}, f32[2,32]{1,0:T(2,128)S(1)}, u32[]{:S(2)}, u32[]{:S(2)}) collective-permute-start(f32[2,32]{1,0:T(2,128)S(1)} %collective-permute-done.5.refs_0_), channel_id=1, source_target_pairs={{0,1},{1,0},{2,3},{3,2},{4,5},{5,4},{6,7},{7,6},{8,9},{9,8},{10,11... | collective-permute-start | bytes 776 | tf_op jit(solution)/shard_map/ppermute | solution.py:137
  25.5 0.0 collective-permute-done.7.refs_2_
  25.5 0.1 collective-permute-start.8
  25.6 0.0 collective-permute-done.9.refs_4_
  25.6 0.4 %collective-permute-start.10 = (f32[2,32]{1,0:T(2,128)S(1)}, f32[2,32]{1,0:T(2,128)S(1)}, u32[]{:S(2)}, u32[]{:S(2)}) collective-permute-start(f32[2,32]{1,0:T(2,128)S(1)} %collective-permute-done.9.refs_4_), channel_id=1, source_target_pairs={{0,1},{1,0},{2,3},{3,2},{4,5},{5,4},{6,7},{7,6},{8,9},{9,8},{10,11... | collective-permute-start | bytes 776 | tf_op jit(solution)/shard_map/ppermute | solution.py:137
  26.0 0.0 collective-permute-done.11.refs_6_
  26.0 1.7 %collective-permute-start.12 = (f32[2,32]{1,0:T(2,128)S(1)}, f32[2,32]{1,0:T(2,128)S(1)}, u32[]{:S(2)}, u32[]{:S(2)}) collective-permute-start(f32[2,32]{1,0:T(2,128)S(1)} %collective-permute-done.11.refs_6_), channel_id=1, source_target_pairs={{0,1},{1,0},{2,3},{3,2},{4,5},{5,4},{6,7},{7,6},{8,9},{9,8},{10,11... | collective-permute-start | bytes 776 | tf_op jit(solution)/shard_map/ppermute | solution.py:137
  27.7 0.0 collective-permute-done.6.refs_1_
  27.7 0.0 collective-permute-done.8.refs_3_
  27.7 0.0 collective-permute-done.10.refs_5_
  27.7 0.8 %collective-permute-done.12.refs_7_ = f32[2,32]{1,0:T(2,128)S(1)} collective-permute-done((f32[2,32]{1,0:T(2,128)S(1)}, f32[2,32]{1,0:T(2,128)S(1)}, u32[]{:S(2)}, u32[]{:S(2)}) %collective-permute-start.12) | collective-permute-done | bytes 288 | tf_op jit(solution)/shard_map/ppermute | solution.py:137
  28.5 0.0 copy-done.1
  28.5 0.8 %pick.1 = f32[2,1000]{1,0:T(2,128)} custom-call(s32[1]{0:T(128)} %bitcast.base_ref, s32[2,1000]{1,0:T(2,128)S(1)} %copy-done.1, f32[2,32]{1,0:T(2,128)S(1)} %collective-permute-done.5.refs_0_, f32[2,32]{1,0:T(2,128)S(1)} %collective-permute-done.6.refs_1_, f32[2,32]{1,0:T(2,128)S(1)} %collective-permute-done.7.refs_2_, ...), custom_call_target="tpu_custom_call" | custom-call | tf_op jit(solution)/shard_map/pick/pallas_call | solution.py:112
  (2 shorter events, 0.0 us)
Async XLA Ops:
  0.0 11.7 %collective-permute-start.4 = (bf16[32,64,128]{2,1,0:T(8,128)(2,1)}, bf16[32,64,128]{2,1,0:T(8,128)(2,1)S(1)}, u32[]{:S(2)}, u32[]{:S(2)}) collective-permute-start(bf16[32,64,128]{2,1,0:T(8,128)(2,1)} %refs_4_.1), channel_id=1, source_target_pairs={{0,1},{1,0},{2,3},{3,2},{4,5},{5,4},{6,7},{7,6},{8,9},{9,8},{10,11... | collective-permute-start | bytes 1572872 | tf_op jit(solution)/shard_map/ppermute | solution.py:158
  0.5 6.5 %collective-permute-start.1 = (bf16[2,32,128]{2,1,0:T(8,128)(2,1)}, bf16[2,32,128]{2,1,0:T(8,128)(2,1)S(1)}, u32[]{:S(2)}, u32[]{:S(2)}) collective-permute-start(bf16[2,32,128]{2,1,0:T(8,128)(2,1)} %param.4), channel_id=1, source_target_pairs={{0,4},{1,7},{2,6},{3,5},{4,0},{5,3},{6,2},{7,1},{8,12},{9,15},{10,... | collective-permute-start | bytes 49160 | tf_op jit(solution)/shard_map/ppermute | solution.py:130
  3.0 4.0 %collective-permute-start = (bf16[2,32,128]{2,1,0:T(8,128)(2,1)}, bf16[2,32,128]{2,1,0:T(8,128)(2,1)S(1)}, u32[]{:S(2)}, u32[]{:S(2)}) collective-permute-start(bf16[2,32,128]{2,1,0:T(8,128)(2,1)} %param.4), channel_id=1, source_target_pairs={{0,0},{1,3},{2,2},{3,1},{4,4},{5,7},{6,6},{7,5},{8,8},{9,11},{10,1... | collective-permute-start | bytes 49160 | tf_op jit(solution)/shard_map/ppermute | solution.py:130
  4.4 5.8 %collective-permute-start.3 = (bf16[2,32,128]{2,1,0:T(8,128)(2,1)}, bf16[2,32,128]{2,1,0:T(8,128)(2,1)S(1)}, u32[]{:S(2)}, u32[]{:S(2)}) collective-permute-start(bf16[2,32,128]{2,1,0:T(8,128)(2,1)} %param.4), channel_id=1, source_target_pairs={{0,12},{1,15},{2,14},{3,13},{4,8},{5,11},{6,10},{7,9},{8,4},{9,7},... | collective-permute-start | bytes 49160 | tf_op jit(solution)/shard_map/ppermute | solution.py:130
  6.9 4.9 %collective-permute-start.2 = (bf16[2,32,128]{2,1,0:T(8,128)(2,1)}, bf16[2,32,128]{2,1,0:T(8,128)(2,1)S(1)}, u32[]{:S(2)}, u32[]{:S(2)}) collective-permute-start(bf16[2,32,128]{2,1,0:T(8,128)(2,1)} %param.4), channel_id=1, source_target_pairs={{0,8},{1,11},{2,10},{3,9},{4,12},{5,15},{6,14},{7,13},{8,0},{9,3},... | collective-permute-start | bytes 49160 | tf_op jit(solution)/shard_map/ppermute | solution.py:130
  7.0 4.7 %copy-start.2 = (s32[32]{0:T(128)S(1)}, s32[32]{0:T(128)}, u32[]{:S(2)}) copy-start(s32[32]{0:T(128)} %lens_ref.1) | copy-start | bytes 388
  11.7 1.0 %copy-start = (bf16[32,64,128]{2,1,0:T(8,128)(2,1)S(1)}, bf16[32,64,128]{2,1,0:T(8,128)(2,1)}, u32[]{:S(2)}) copy-start(bf16[32,64,128]{2,1,0:T(8,128)(2,1)} %refs_4_.1) | copy-start | bytes 1572868
  15.5 13.0 %copy-start.1 = (s32[2,1000]{1,0:T(2,128)S(1)}, s32[2,1000]{1,0:T(2,128)}, u32[]{:S(2)}) copy-start(s32[2,1000]{1,0:T(2,128)} %cand_ref.1) | copy-start | bytes 24004
  15.5 5.1 %collective-permute-start.5 = (f32[2,32]{1,0:T(2,128)S(1)}, f32[2,32]{1,0:T(2,128)S(1)}, u32[]{:S(2)}, u32[]{:S(2)}) collective-permute-start(f32[2,32]{1,0:T(2,128)S(1)} %get-tuple-element.9), channel_id=1, source_target_pairs={{0,0},{1,3},{2,2},{3,1},{4,4},{5,7},{6,6},{7,5},{8,8},{9,11},{10,1... | collective-permute-start | bytes 776 | tf_op jit(solution)/shard_map/ppermute | solution.py:130
  16.2 9.3 %collective-permute-start.7 = (f32[2,32]{1,0:T(2,128)S(1)}, f32[2,32]{1,0:T(2,128)S(1)}, u32[]{:S(2)}, u32[]{:S(2)}) collective-permute-start(f32[2,32]{1,0:T(2,128)S(1)} %get-tuple-element.10), channel_id=1, source_target_pairs={{0,4},{1,7},{2,6},{3,5},{4,0},{5,3},{6,2},{7,1},{8,12},{9,15},{10,... | collective-permute-start | bytes 776 | tf_op jit(solution)/shard_map/ppermute | solution.py:130
  16.9 8.6 %collective-permute-start.9 = (f32[2,32]{1,0:T(2,128)S(1)}, f32[2,32]{1,0:T(2,128)S(1)}, u32[]{:S(2)}, u32[]{:S(2)}) collective-permute-start(f32[2,32]{1,0:T(2,128)S(1)} %get-tuple-element.11), channel_id=1, source_target_pairs={{0,8},{1,11},{2,10},{3,9},{4,12},{5,15},{6,14},{7,13},{8,0},{9,3},... | collective-permute-start | bytes 776 | tf_op jit(solution)/shard_map/ppermute | solution.py:130
  18.1 7.9 %collective-permute-start.11 = (f32[2,32]{1,0:T(2,128)S(1)}, f32[2,32]{1,0:T(2,128)S(1)}, u32[]{:S(2)}, u32[]{:S(2)}) collective-permute-start(f32[2,32]{1,0:T(2,128)S(1)} %get-tuple-element.12), channel_id=1, source_target_pairs={{0,12},{1,15},{2,14},{3,13},{4,8},{5,11},{6,10},{7,9},{8,4},{9,7},... | collective-permute-start | bytes 776 | tf_op jit(solution)/shard_map/ppermute | solution.py:130
  20.6 7.1 %collective-permute-start.6 = (f32[2,32]{1,0:T(2,128)S(1)}, f32[2,32]{1,0:T(2,128)S(1)}, u32[]{:S(2)}, u32[]{:S(2)}) collective-permute-start(f32[2,32]{1,0:T(2,128)S(1)} %collective-permute-done.5.refs_0_), channel_id=1, source_target_pairs={{0,1},{1,0},{2,3},{3,2},{4,5},{5,4},{6,7},{7,6},{8,9},{9,8},{10,11... | collective-permute-start | bytes 776 | tf_op jit(solution)/shard_map/ppermute | solution.py:137
  25.5 2.2 %collective-permute-start.8 = (f32[2,32]{1,0:T(2,128)S(1)}, f32[2,32]{1,0:T(2,128)S(1)}, u32[]{:S(2)}, u32[]{:S(2)}) collective-permute-start(f32[2,32]{1,0:T(2,128)S(1)} %collective-permute-done.7.refs_2_), channel_id=1, source_target_pairs={{0,1},{1,0},{2,3},{3,2},{4,5},{5,4},{6,7},{7,6},{8,9},{9,8},{10,11... | collective-permute-start | bytes 776 | tf_op jit(solution)/shard_map/ppermute | solution.py:137
  25.6 2.1 %collective-permute-start.10 = (f32[2,32]{1,0:T(2,128)S(1)}, f32[2,32]{1,0:T(2,128)S(1)}, u32[]{:S(2)}, u32[]{:S(2)}) collective-permute-start(f32[2,32]{1,0:T(2,128)S(1)} %collective-permute-done.9.refs_4_), channel_id=1, source_target_pairs={{0,1},{1,0},{2,3},{3,2},{4,5},{5,4},{6,7},{7,6},{8,9},{9,8},{10,11... | collective-permute-start | bytes 776 | tf_op jit(solution)/shard_map/ppermute | solution.py:137
  26.0 2.5 %collective-permute-start.12 = (f32[2,32]{1,0:T(2,128)S(1)}, f32[2,32]{1,0:T(2,128)S(1)}, u32[]{:S(2)}, u32[]{:S(2)}) collective-permute-start(f32[2,32]{1,0:T(2,128)S(1)} %collective-permute-done.11.refs_6_), channel_id=1, source_target_pairs={{0,1},{1,0},{2,3},{3,2},{4,5},{5,4},{6,7},{7,6},{8,9},{9,8},{10,11... | collective-permute-start | bytes 776 | tf_op jit(solution)/shard_map/ppermute | solution.py:137

commit v4 on v3

--- a/solution.py
+++ b/solution.py
@@ -14,7 +14,7 @@
 BLOCK = 256
 
 
-def score_kernel(n_pieces, me_ref, lens_ref, *refs):
+def score_kernel(n_pieces, put, me_ref, lens_ref, *refs):
     piece_refs = refs[:n_pieces]
     own_ref, other_ref = refs[n_pieces: n_pieces + 2]
     out_refs = refs[n_pieces + 2: -4]
@@ -51,29 +51,27 @@
                     max_ref[spot] = jnp.maximum(max_ref[spot], best) if fold else best
             return 0
 
-        lax.fori_loop(0, count // step, group, 0)
+        lax.fori_loop(0, count // step, group, 0, unroll=total <= block)
 
     best_of(other_ref, (1 - core) * half, False)
     fetch.wait()
     best_of(held_ref, core * half, True)
-    summed = jnp.sum(max_ref[...].T.reshape(total // q_tokens, q_tokens, count), axis=1)
-    q_each = out_refs[0].shape[0]
-    for r, out_ref in enumerate(out_refs):
-        out_ref[...] = summed[r * q_each: (r + 1) * q_each]
-
-
-def score(core, doc_lens, pieces, doc_tokens, other, outs):
+    put(jnp.sum(max_ref[...].T.reshape(total // q_tokens, q_tokens, count), axis=1), core, out_refs)
+
+
+def score(core, doc_lens, pieces, doc_tokens, other, put, out_shapes):
     smem = pl.BlockSpec(memory_space=pltpu.SMEM)
     vmem = pl.BlockSpec(memory_space=pltpu.VMEM)
     hbm = pl.BlockSpec(memory_space=pltpu.HBM)
     count = doc_tokens.shape[0]
     queries = sum(p.shape[0] for p in pieces)
     q_tokens, width = pieces[0].shape[1:]
+    doc_tokens = pltpu.with_memory_space_constraint(doc_tokens, pltpu.HBM)
     return pl.pallas_call(
-        functools.partial(score_kernel, len(pieces)),
-        out_shape=[jax.ShapeDtypeStruct((queries // outs, count), jnp.float32)] * outs,
+        functools.partial(score_kernel, len(pieces), put),
+        out_shape=[jax.ShapeDtypeStruct(shape, jnp.float32) for shape in out_shapes],
         in_specs=[smem, smem] + [vmem] * len(pieces) + [hbm, vmem],
-        out_specs=[vmem] * outs,
+        out_specs=[vmem] * len(out_shapes),
         scratch_shapes=[
             pltpu.VMEM((queries * q_tokens, width), jnp.bfloat16),
             pltpu.VMEM((count, queries * q_tokens), jnp.float32),
@@ -85,9 +83,11 @@
     )(core.reshape(1), doc_lens, *pieces, doc_tokens, other)
 
 
-def pick_kernel(n_pieces, base_ref, cand_ref, *refs):
+def pick_kernel(n_pieces, wide, base_ref, cand_ref, *refs):
     piece_refs, out_ref = refs[:n_pieces], refs[n_pieces]
     parts = [ref[...] for ref in piece_refs]
+    parts = [part[:, t: t + wide] for group in zip(*[iter(parts)] * min(2, n_pieces))
+             for t in range(0, parts[0].shape[1], wide) for part in group]
     table = jnp.concatenate(parts, axis=1) if len(parts) > 1 else parts[0]
     size = table.shape[1]
     rows, width = cand_ref.shape
@@ -106,11 +106,11 @@
         out_ref[:, pl.ds(at, wide)] = value[:, :wide]
 
 
-def pick(base, candidates, pieces):
+def pick(base, candidates, pieces, wide):
     smem = pl.BlockSpec(memory_space=pltpu.SMEM)
     vmem = pl.BlockSpec(memory_space=pltpu.VMEM)
     return pl.pallas_call(
-        functools.partial(pick_kernel, len(pieces)),
+        functools.partial(pick_kernel, len(pieces), wide),
         out_shape=jax.ShapeDtypeStruct(candidates.shape, jnp.float32),
         in_specs=[smem, vmem] + [vmem] * len(pieces),
         out_specs=vmem,
@@ -119,47 +119,84 @@
     )(base.reshape(1), candidates, *pieces)
 
 
-def two_columns(queries, doc_tokens, other, doc_lens, candidates, n_z, core):
-    count = doc_tokens.shape[0]
-
-    def exchange(array, r):
-        pairs = [
-            ((z * 2 + x) * 2 + d, ((z ^ r) * 2 + (x ^ d)) * 2 + d)
-            for z in range(n_z) for x in range(2) for d in range(2)
-        ]
+SELF, NEAR, FAR = (0, 0), (1, 0), (2, 0)
+NEAR_ACROSS, FAR_ACROSS = (1, 1), (2, 1)
+
+
+def put_two_levels(scores, core, out_refs):
+    kept_near_ref, kept_far_ref, lent_ref = out_refs
+    q_each = kept_near_ref.shape[0]
+    block = [scores[k * q_each: (k + 1) * q_each] for k in range(4)]
+    zero = jnp.zeros_like(block[0])
+
+    def left(x):
+        return jnp.concatenate([x, zero], axis=1)
+
+    def right(x):
+        return jnp.concatenate([zero, x], axis=1)
+
+    kept_near_ref[...] = jnp.where(core == 0, left(block[0]), right(block[0]))
+    kept_far_ref[...] = left(block[1])
+    lent_ref[pl.ds(0, q_each), :] = jnp.where(core == 0, right(block[2]), left(block[2]))
+    lent_ref[pl.ds(q_each, q_each), :] = right(block[3])
+
+
+def two_columns(queries, doc_tokens, doc_lens, candidates, core):
+    q_owned = queries.shape[0]
+    count = doc_tokens.shape[0]
+
+    def exchange(array, step0, step1):
+        pairs = []
+        for z in range(4):
+            for x in range(2):
+                for d, (dz, dx) in enumerate((step0, step1)):
+                    pairs.append(((z * 2 + x) * 2 + d, ((z ^ dz) * 2 + (x ^ dx)) * 2 + d))
         return lax.ppermute(array, ALL_AXES, pairs)
 
-    pieces = [exchange(queries, r) for r in range(n_z)]
-    blocks = score(core, doc_lens, pieces, doc_tokens, other, n_z)
-    table = []
-    for r in range(n_z):
-        moved = exchange(blocks[r], r)
-        table += [moved, lax.ppermute(moved, "dim", [(0, 1), (1, 0)])]
+    def cross(array):
+        return lax.ppermute(array, "dim", [(0, 1), (1, 0)])
+
+    far = exchange(queries, FAR, FAR_ACROSS)
+    near = exchange(queries, SELF, NEAR_ACROSS)
+    first = jnp.concatenate([near, far], axis=0)
+    first, docs_out = lax.optimization_barrier((first, doc_tokens))
+    second = exchange(first, NEAR, NEAR)
+    other = cross(docs_out)
+    pair = (q_owned, 2 * count)
+    kept_near, kept_far, lent = score(
+        core, doc_lens, [first, second], doc_tokens, other, put_two_levels, [pair, pair, (2 * q_owned, 2 * count)]
+    )
+    brought = exchange(lent, NEAR, NEAR)
+    far = exchange(kept_far + brought[q_owned:], FAR, FAR_ACROSS)
+    near = exchange(kept_near + brought[:q_owned], SELF, NEAR_ACROSS)
     base = (lax.axis_index("shard") * 2 + (lax.axis_index("qgrp") ^ core)) * count
-    return pick(base, candidates, table)
-
-
-def any_columns(queries, doc_tokens, other, doc_lens, candidates, n, core):
+    return pick(base, candidates, [near, cross(near), far, cross(far)], count)
+
+
+def any_columns(queries, doc_tokens, doc_lens, candidates, n, cores, core):
     q_owned = candidates.shape[0]
     count = doc_tokens.shape[0]
     gathered = lax.all_gather(queries, INDEX_AXES, axis=0, tiled=True)
-    block = score(core, doc_lens, [gathered], doc_tokens, other, 1)[0]
+    other = lax.ppermute(doc_tokens, "dim", [(s, cores - 1 - s) for s in range(cores)])
+
+    def put(scores, core, out_refs):
+        out_refs[0][...] = scores
+
+    block = score(core, doc_lens, [gathered], doc_tokens, other, put, [(n * q_owned, count)])[0]
     moved = lax.all_to_all(
         block.reshape(n, q_owned, count), INDEX_AXES, split_axis=0, concat_axis=0, tiled=True
     )
     table = moved.transpose(1, 0, 2).reshape(q_owned, n * count)
-    return pick(jnp.int32(0), candidates, [table])
+    return pick(jnp.int32(0), candidates, [table], n * count)
 
 
 def per_device(queries, doc_tokens, doc_lens, candidates):
-    n_z, n_x, cores = (lax.axis_size(axis) for axis in ALL_AXES)
+    sizes = n_z, n_x, cores = tuple(lax.axis_size(axis) for axis in ALL_AXES)
     count = doc_tokens.shape[0]
     core = lax.axis_index("dim")
-    other = lax.ppermute(doc_tokens, "dim", [(s, cores - 1 - s) for s in range(cores)])
-    power = count & (count - 1) == 0 and n_z & (n_z - 1) == 0
-    if n_x == 2 and cores == 2 and n_z <= 8 and power:
-        return two_columns(queries, doc_tokens, other, doc_lens, candidates, n_z, core)
-    return any_columns(queries, doc_tokens, other, doc_lens, candidates, n_z * n_x, core)
+    if sizes == (4, 2, 2) and count & (count - 1) == 0:
+        return two_columns(queries, doc_tokens, doc_lens, candidates, core)
+    return any_columns(queries, doc_tokens, doc_lens, candidates, n_z * n_x, cores, core)
 
 
 def solution(mesh):

time: 29.5 us -> 27 us (0.915)
  starting transfers between devices: 19.1 us -> 14.2 us
  waiting for transfers between devices: 5.56 us -> 9.24 us
  local copies, waits for them, and re-layouts: 1.05 us -> 0.01 us
    ppermute x8 -> x6, waiting for transfers between devices: 4.75 us -> 8.42 us  [exchange(): return lax.ppermute(array, ALL_AXES, pairs)]
    ppermute x5 -> x3, starting transfers between devices: 7.51 us -> 4.59 us  [cross(): return lax.ppermute(array, 'dim', [(0, 1), (1, 0)])]
    ppermute x8 -> x6, starting transfers between devices: 11.6 us -> 9.6 us  [exchange(): return lax.ppermute(array, ALL_AXES, pairs)]
    unnamed x6 -> x4, local copies, waits for them, and re-layouts: 1.05 us -> 0.01 us
    ppermute x5 -> x3, waiting for transfers between devices: 0.82 us -> 0.82 us  [cross(): return lax.ppermute(array, 'dim', [(0, 1), (1, 0)])]
  transfers between devices with their start and end apart: 13 -> 9, of which waited for: 3 -> 6; matrix products, arithmetic and copies ran while one was open for 0% -> 0% of each run, Pallas kernels for 0% -> 0%
where the time goes in v4:
time: 27 us; the launch traced here: 26.7 us
  starting transfers between devices  14.2 us (53%)
  waiting for transfers between devices  9.24 us (34%)
  Pallas kernels  3.24 us (12%)
    ppermute x6, starting transfers between devices, exchange(): return lax.ppermute(array, ALL_AXES, pairs)  9.6 us
    ppermute x6, waiting for transfers between devices, exchange(): return lax.ppermute(array, ALL_AXES, pairs)  8.42 us
    ppermute x3, starting transfers between devices, cross(): return lax.ppermute(array, 'dim', [(0, 1), (1, 0)])  4.59 us
    pallas_call x1, Pallas kernels, score(): pl.pallas_call(functools.partial(score_kernel, len(pieces), put), out_sha...  2.47 us
    ppermute x3, waiting for transfers between devices, cross(): return lax.ppermute(array, 'dim', [(0, 1), (1, 0)])  0.82 us
    pallas_call x1, Pallas kernels, pick(): pl.pallas_call(functools.partial(pick_kernel, len(pieces), wide), out_sha...  0.78 us
  transfers between devices with their start and end apart: 9, of which 6 were waited for; matrix products, arithmetic and copies ran while one was open for 0% of the time, Pallas kernels for 0%

profile of v4, /device:TPU:0, one launch (start us, length us, event | category | flops | bytes accessed | tf_op | source)
XLA Modules:
  0.0 26.7 jit_solution(12314037351889763230)
XLA Ops:
  0.0 4.0 %collective-permute-start.1 = (bf16[2,32,128]{2,1,0:T(8,128)(2,1)}, bf16[2,32,128]{2,1,0:T(8,128)(2,1)S(1)}, u32[]{:S(2)}, u32[]{:S(2)}) collective-permute-start(bf16[2,32,128]{2,1,0:T(8,128)(2,1)} %param.4), channel_id=1, source_target_pairs={{0,8},{1,11},{2,10},{3,9},{4,12},{5,15},{6,14},{7,13},{8,0},{9,3},... | collective-permute-start | bytes 49160 | tf_op jit(solution)/shard_map/ppermute | solution.py:154
  4.0 1.4 %collective-permute-start = (bf16[2,32,128]{2,1,0:T(8,128)(2,1)}, bf16[2,32,128]{2,1,0:T(8,128)(2,1)S(1)}, u32[]{:S(2)}, u32[]{:S(2)}) collective-permute-start(bf16[2,32,128]{2,1,0:T(8,128)(2,1)} %param.4), channel_id=1, source_target_pairs={{0,0},{1,7},{2,2},{3,5},{4,4},{5,3},{6,6},{7,1},{8,8},{9,15},{10,1... | collective-permute-start | bytes 49160 | tf_op jit(solution)/shard_map/ppermute | solution.py:154
  5.4 0.6 %collective-permute-done.1 = bf16[2,32,128]{2,1,0:T(8,128)(2,1)S(1)} collective-permute-done((bf16[2,32,128]{2,1,0:T(8,128)(2,1)}, bf16[2,32,128]{2,1,0:T(8,128)(2,1)S(1)}, u32[]{:S(2)}, u32[]{:S(2)}) %collective-permute-start.1) | collective-permute-done | bytes 16416 | tf_op jit(solution)/shard_map/ppermute | solution.py:154
  6.0 0.0 collective-permute-done
  6.0 4.1 %collective-permute-start.3 = (bf16[32,64,128]{2,1,0:T(8,128)(2,1)}, bf16[32,64,128]{2,1,0:T(8,128)(2,1)S(1)}, u32[]{:S(2)}, u32[]{:S(2)}) collective-permute-start(bf16[32,64,128]{2,1,0:T(8,128)(2,1)} %refs_2_.1), channel_id=1, source_target_pairs={{0,1},{1,0},{2,3},{3,2},{4,5},{5,4},{6,7},{7,6},{8,9},{9,8},{10,11... | collective-permute-start | bytes 1572872 | tf_op jit(solution)/shard_map/ppermute | solution.py:157
  10.1 1.6 %collective-permute-start.2 = (bf16[4,32,128]{2,1,0:T(8,128)(2,1)S(1)}, bf16[4,32,128]{2,1,0:T(8,128)(2,1)S(1)}, u32[]{:S(2)}, u32[]{:S(2)}) collective-permute-start(bf16[4,32,128]{2,1,0:T(8,128)(2,1)S(1)} %pad_maximum_fusion.refs_0_), channel_id=1, source_target_pairs={{0,4},{1,5},{2,6},{3,7},{4,0},{5,1},{6,2},{7,3},{8,12},{9,13},{10,... | collective-permute-start | bytes 98312 | tf_op jit(solution)/shard_map/ppermute | solution.py:154
  11.7 0.0 copy-start.1
  11.7 2.3 %collective-permute-done.2.refs_1_ = bf16[4,32,128]{2,1,0:T(8,128)(2,1)S(1)} collective-permute-done((bf16[4,32,128]{2,1,0:T(8,128)(2,1)S(1)}, bf16[4,32,128]{2,1,0:T(8,128)(2,1)S(1)}, u32[]{:S(2)}, u32[]{:S(2)}) %collective-permute-start.2) | collective-permute-done | bytes 32800 | tf_op jit(solution)/shard_map/ppermute | solution.py:154
  14.0 0.0 collective-permute-done.3.refs_3_
  14.0 0.0 copy-done.1
  14.0 2.5 %score.1 = (f32[2,64]{1,0:T(2,128)S(1)}, f32[2,64]{1,0:T(2,128)S(1)}, f32[4,64]{1,0:T(4,128)S(1)}) custom-call(s32[1]{0:T(128)} %bitcast.1.me_ref, s32[32]{0:T(128)S(1)} %copy-done.1, bf16[4,32,128]{2,1,0:T(8,128)(2,1)S(1)} %pad_maximum_fusion.refs_0_, bf16[4,32,128]{2,1,0:T(8,128)(2,1)S(1)} %collective-permute-done.2.refs_1_, bf16[32,64,128]{2,1,0:T(8,128)(2,1)} %refs_2_.1, ...), custom_call_target="tpu_custom_call" | custom-call | tf_op jit(solution)/shard_map/score/pallas_call | solution.py:70
  16.5 1.6 %collective-permute-start.4 = (f32[4,64]{1,0:T(4,128)S(1)}, f32[4,64]{1,0:T(4,128)S(1)}, u32[]{:S(2)}, u32[]{:S(2)}) collective-permute-start(f32[4,64]{1,0:T(4,128)S(1)} %get-tuple-element.13), channel_id=1, source_target_pairs={{0,4},{1,5},{2,6},{3,7},{4,0},{5,1},{6,2},{7,3},{8,12},{9,13},{10,... | collective-permute-start | bytes 3080 | tf_op jit(solution)/shard_map/ppermute | solution.py:154
  18.1 2.0 %collective-permute-done.4 = f32[4,64]{1,0:T(4,128)S(1)} collective-permute-done((f32[4,64]{1,0:T(4,128)S(1)}, f32[4,64]{1,0:T(4,128)S(1)}, u32[]{:S(2)}, u32[]{:S(2)}) %collective-permute-start.4) | collective-permute-done | bytes 1056 | tf_op jit(solution)/shard_map/ppermute | solution.py:154
  20.2 0.3 %collective-permute-start.7 = (f32[2,64]{1,0:T(2,128)S(1)}, f32[2,64]{1,0:T(2,128)S(1)}, u32[]{:S(2)}, u32[]{:S(2)}) collective-permute-start(f32[2,64]{1,0:T(2,128)S(1)} %get-tuple-element.15), channel_id=1, source_target_pairs={{0,8},{1,11},{2,10},{3,9},{4,12},{5,15},{6,14},{7,13},{8,0},{9,3},... | collective-permute-start | bytes 1544 | tf_op jit(solution)/shard_map/ppermute | solution.py:154
  20.5 0.6 %collective-permute-start.5 = (f32[2,64]{1,0:T(2,128)S(1)}, f32[2,64]{1,0:T(2,128)S(1)}, u32[]{:S(2)}, u32[]{:S(2)}) collective-permute-start(f32[2,64]{1,0:T(2,128)S(1)} %get-tuple-element.16), channel_id=1, source_target_pairs={{0,0},{1,7},{2,2},{3,5},{4,4},{5,3},{6,6},{7,1},{8,8},{9,15},{10,1... | collective-permute-start | bytes 1544 | tf_op jit(solution)/shard_map/ppermute | solution.py:154
  21.2 0.0 copy-start
  21.2 3.5 %collective-permute-done.7.refs_2_ = f32[2,64]{1,0:T(2,128)S(1)} collective-permute-done((f32[2,64]{1,0:T(2,128)S(1)}, f32[2,64]{1,0:T(2,128)S(1)}, u32[]{:S(2)}, u32[]{:S(2)}) %collective-permute-start.7) | collective-permute-done | bytes 544 | tf_op jit(solution)/shard_map/ppermute | solution.py:154
  24.6 0.0 collective-permute-start.8
  24.6 0.0 collective-permute-done.5.refs_0_
  24.6 0.5 %collective-permute-start.6 = (f32[2,64]{1,0:T(2,128)S(1)}, f32[2,64]{1,0:T(2,128)S(1)}, u32[]{:S(2)}, u32[]{:S(2)}) collective-permute-start(f32[2,64]{1,0:T(2,128)S(1)} %collective-permute-done.5.refs_0_), channel_id=1, source_target_pairs={{0,1},{1,0},{2,3},{3,2},{4,5},{5,4},{6,7},{7,6},{8,9},{9,8},{10,11... | collective-permute-start | bytes 1544 | tf_op jit(solution)/shard_map/ppermute | solution.py:157
  25.1 0.6 %collective-permute-done.8.refs_3_ = f32[2,64]{1,0:T(2,128)S(1)} collective-permute-done((f32[2,64]{1,0:T(2,128)S(1)}, f32[2,64]{1,0:T(2,128)S(1)}, u32[]{:S(2)}, u32[]{:S(2)}) %collective-permute-start.8) | collective-permute-done | bytes 544 | tf_op jit(solution)/shard_map/ppermute | solution.py:157
  25.8 0.2 collective-permute-done.6.refs_1_
  26.0 0.0 copy-done
  26.0 0.8 %pick.1 = f32[2,1000]{1,0:T(2,128)} custom-call(s32[1]{0:T(128)} %bitcast.base_ref, s32[2,1000]{1,0:T(2,128)S(1)} %copy-done, f32[2,64]{1,0:T(2,128)S(1)} %collective-permute-done.5.refs_0_, f32[2,64]{1,0:T(2,128)S(1)} %collective-permute-done.6.refs_1_, f32[2,64]{1,0:T(2,128)S(1)} %collective-permute-done.7.refs_2_, f32[2,64]{1,0:T(2,128)S(1)} %collective-permute-done.8.refs_3_), custom_call_target="tpu_custom_call" | custom-call | tf_op jit(solution)/shard_map/pick/pallas_call | solution.py:112
  (2 shorter events, 0.0 us)
Async XLA Ops:
  0.0 6.0 %collective-permute-start.1 = (bf16[2,32,128]{2,1,0:T(8,128)(2,1)}, bf16[2,32,128]{2,1,0:T(8,128)(2,1)S(1)}, u32[]{:S(2)}, u32[]{:S(2)}) collective-permute-start(bf16[2,32,128]{2,1,0:T(8,128)(2,1)} %param.4), channel_id=1, source_target_pairs={{0,8},{1,11},{2,10},{3,9},{4,12},{5,15},{6,14},{7,13},{8,0},{9,3},... | collective-permute-start | bytes 49160 | tf_op jit(solution)/shard_map/ppermute | solution.py:154
  4.0 2.0 %collective-permute-start = (bf16[2,32,128]{2,1,0:T(8,128)(2,1)}, bf16[2,32,128]{2,1,0:T(8,128)(2,1)S(1)}, u32[]{:S(2)}, u32[]{:S(2)}) collective-permute-start(bf16[2,32,128]{2,1,0:T(8,128)(2,1)} %param.4), channel_id=1, source_target_pairs={{0,0},{1,7},{2,2},{3,5},{4,4},{5,3},{6,6},{7,1},{8,8},{9,15},{10,1... | collective-permute-start | bytes 49160 | tf_op jit(solution)/shard_map/ppermute | solution.py:154
  6.0 8.0 %collective-permute-start.3 = (bf16[32,64,128]{2,1,0:T(8,128)(2,1)}, bf16[32,64,128]{2,1,0:T(8,128)(2,1)S(1)}, u32[]{:S(2)}, u32[]{:S(2)}) collective-permute-start(bf16[32,64,128]{2,1,0:T(8,128)(2,1)} %refs_2_.1), channel_id=1, source_target_pairs={{0,1},{1,0},{2,3},{3,2},{4,5},{5,4},{6,7},{7,6},{8,9},{9,8},{10,11... | collective-permute-start | bytes 1572872 | tf_op jit(solution)/shard_map/ppermute | solution.py:157
  10.1 3.9 %collective-permute-start.2 = (bf16[4,32,128]{2,1,0:T(8,128)(2,1)S(1)}, bf16[4,32,128]{2,1,0:T(8,128)(2,1)S(1)}, u32[]{:S(2)}, u32[]{:S(2)}) collective-permute-start(bf16[4,32,128]{2,1,0:T(8,128)(2,1)S(1)} %pad_maximum_fusion.refs_0_), channel_id=1, source_target_pairs={{0,4},{1,5},{2,6},{3,7},{4,0},{5,1},{6,2},{7,3},{8,12},{9,13},{10,... | collective-permute-start | bytes 98312 | tf_op jit(solution)/shard_map/ppermute | solution.py:154
  11.7 2.3 %copy-start.1 = (s32[32]{0:T(128)S(1)}, s32[32]{0:T(128)}, u32[]{:S(2)}) copy-start(s32[32]{0:T(128)} %lens_ref.1) | copy-start | bytes 388
  16.5 3.7 %collective-permute-start.4 = (f32[4,64]{1,0:T(4,128)S(1)}, f32[4,64]{1,0:T(4,128)S(1)}, u32[]{:S(2)}, u32[]{:S(2)}) collective-permute-start(f32[4,64]{1,0:T(4,128)S(1)} %get-tuple-element.13), channel_id=1, source_target_pairs={{0,4},{1,5},{2,6},{3,7},{4,0},{5,1},{6,2},{7,3},{8,12},{9,13},{10,... | collective-permute-start | bytes 3080 | tf_op jit(solution)/shard_map/ppermute | solution.py:154
  20.2 4.5 %collective-permute-start.7 = (f32[2,64]{1,0:T(2,128)S(1)}, f32[2,64]{1,0:T(2,128)S(1)}, u32[]{:S(2)}, u32[]{:S(2)}) collective-permute-start(f32[2,64]{1,0:T(2,128)S(1)} %get-tuple-element.15), channel_id=1, source_target_pairs={{0,8},{1,11},{2,10},{3,9},{4,12},{5,15},{6,14},{7,13},{8,0},{9,3},... | collective-permute-start | bytes 1544 | tf_op jit(solution)/shard_map/ppermute | solution.py:154
  20.5 4.1 %collective-permute-start.5 = (f32[2,64]{1,0:T(2,128)S(1)}, f32[2,64]{1,0:T(2,128)S(1)}, u32[]{:S(2)}, u32[]{:S(2)}) collective-permute-start(f32[2,64]{1,0:T(2,128)S(1)} %get-tuple-element.16), channel_id=1, source_target_pairs={{0,0},{1,7},{2,2},{3,5},{4,4},{5,3},{6,6},{7,1},{8,8},{9,15},{10,1... | collective-permute-start | bytes 1544 | tf_op jit(solution)/shard_map/ppermute | solution.py:154
  21.2 4.8 %copy-start = (s32[2,1000]{1,0:T(2,128)S(1)}, s32[2,1000]{1,0:T(2,128)}, u32[]{:S(2)}) copy-start(s32[2,1000]{1,0:T(2,128)} %cand_ref.1) | copy-start | bytes 24004
  24.6 1.1 %collective-permute-start.8 = (f32[2,64]{1,0:T(2,128)S(1)}, f32[2,64]{1,0:T(2,128)S(1)}, u32[]{:S(2)}, u32[]{:S(2)}) collective-permute-start(f32[2,64]{1,0:T(2,128)S(1)} %collective-permute-done.7.refs_2_), channel_id=1, source_target_pairs={{0,1},{1,0},{2,3},{3,2},{4,5},{5,4},{6,7},{7,6},{8,9},{9,8},{10,11... | collective-permute-start | bytes 1544 | tf_op jit(solution)/shard_map/ppermute | solution.py:157
  24.6 1.3 %collective-permute-start.6 = (f32[2,64]{1,0:T(2,128)S(1)}, f32[2,64]{1,0:T(2,128)S(1)}, u32[]{:S(2)}, u32[]{:S(2)}) collective-permute-start(f32[2,64]{1,0:T(2,128)S(1)} %collective-permute-done.5.refs_0_), channel_id=1, source_target_pairs={{0,1},{1,0},{2,3},{3,2},{4,5},{5,4},{6,7},{7,6},{8,9},{9,8},{10,11... | collective-permute-start | bytes 1544 | tf_op jit(solution)/shard_map/ppermute | solution.py:157

commit v5 on v4

--- a/solution.py
+++ b/solution.py
@@ -56,7 +56,7 @@
     best_of(other_ref, (1 - core) * half, False)
     fetch.wait()
     best_of(held_ref, core * half, True)
-    put(jnp.sum(max_ref[...].T.reshape(total // q_tokens, q_tokens, count), axis=1), core, out_refs)
+    put(jnp.sum(max_ref[...].T.reshape(total // q_tokens, q_tokens, count), axis=1), out_refs)
 
 
 def score(core, doc_lens, pieces, doc_tokens, other, put, out_shapes):
@@ -119,11 +119,11 @@
     )(base.reshape(1), candidates, *pieces)
 
 
-SELF, NEAR, FAR = (0, 0), (1, 0), (2, 0)
+NEAR, FAR = (1, 0), (2, 0)
 NEAR_ACROSS, FAR_ACROSS = (1, 1), (2, 1)
 
 
-def put_two_levels(scores, core, out_refs):
+def put_two_levels(scores, out_refs):
     kept_near_ref, kept_far_ref, lent_ref = out_refs
     q_each = kept_near_ref.shape[0]
     block = [scores[k * q_each: (k + 1) * q_each] for k in range(4)]
@@ -135,9 +135,9 @@
     def right(x):
         return jnp.concatenate([zero, x], axis=1)
 
-    kept_near_ref[...] = jnp.where(core == 0, left(block[0]), right(block[0]))
+    kept_near_ref[...] = right(block[0])
     kept_far_ref[...] = left(block[1])
-    lent_ref[pl.ds(0, q_each), :] = jnp.where(core == 0, right(block[2]), left(block[2]))
+    lent_ref[pl.ds(0, q_each), :] = left(block[2])
     lent_ref[pl.ds(q_each, q_each), :] = right(block[3])
 
 
@@ -157,7 +157,7 @@
         return lax.ppermute(array, "dim", [(0, 1), (1, 0)])
 
     far = exchange(queries, FAR, FAR_ACROSS)
-    near = exchange(queries, SELF, NEAR_ACROSS)
+    near = exchange(queries, NEAR, NEAR_ACROSS)
     first = jnp.concatenate([near, far], axis=0)
     first, docs_out = lax.optimization_barrier((first, doc_tokens))
     second = exchange(first, NEAR, NEAR)
@@ -168,7 +168,7 @@
     )
     brought = exchange(lent, NEAR, NEAR)
     far = exchange(kept_far + brought[q_owned:], FAR, FAR_ACROSS)
-    near = exchange(kept_near + brought[:q_owned], SELF, NEAR_ACROSS)
+    near = exchange(kept_near + brought[:q_owned], NEAR, NEAR_ACROSS)
     base = (lax.axis_index("shard") * 2 + (lax.axis_index("qgrp") ^ core)) * count
     return pick(base, candidates, [near, cross(near), far, cross(far)], count)
 
@@ -179,7 +179,7 @@
     gathered = lax.all_gather(queries, INDEX_AXES, axis=0, tiled=True)
     other = lax.ppermute(doc_tokens, "dim", [(s, cores - 1 - s) for s in range(cores)])
 
-    def put(scores, core, out_refs):
+    def put(scores, out_refs):
         out_refs[0][...] = scores
 
     block = score(core, doc_lens, [gathered], doc_tokens, other, put, [(n * q_owned, count)])[0]

time: 27 us -> 25 us (0.926)
  starting transfers between devices: 14.2 us -> 12.2 us
    ppermute x3, starting transfers between devices: 4.59 us -> 0.74 us  [cross(): return lax.ppermute(array, 'dim', [(0, 1), (1, 0)])]
    ppermute x6, starting transfers between devices: 9.6 us -> 11.4 us  [exchange(): return lax.ppermute(array, ALL_AXES, pairs)]
  transfers between devices with their start and end apart: 9 -> 9, of which waited for: 6 -> 7; matrix products, arithmetic and copies ran while one was open for 0% -> 0% of each run, Pallas kernels for 0% -> 0%
where the time goes in v5:
time: 25 us; the launch traced here: 24.9 us
  starting transfers between devices  12.2 us (49%)
  waiting for transfers between devices  9.41 us (38%)
  Pallas kernels  3.24 us (13%)
    ppermute x6, starting transfers between devices, exchange(): return lax.ppermute(array, ALL_AXES, pairs)  11.4 us
    ppermute x6, waiting for transfers between devices, exchange(): return lax.ppermute(array, ALL_AXES, pairs)  8.58 us
    pallas_call x1, Pallas kernels, score(): pl.pallas_call(functools.partial(score_kernel, len(pieces), put), out_sha...  2.47 us
    ppermute x3, waiting for transfers between devices, cross(): return lax.ppermute(array, 'dim', [(0, 1), (1, 0)])  0.82 us
    pallas_call x1, Pallas kernels, pick(): pl.pallas_call(functools.partial(pick_kernel, len(pieces), wide), out_sha...  0.78 us
    ppermute x3, starting transfers between devices, cross(): return lax.ppermute(array, 'dim', [(0, 1), (1, 0)])  0.74 us
  transfers between devices with their start and end apart: 9, of which 7 were waited for; matrix products, arithmetic and copies ran while one was open for 0% of the time, Pallas kernels for 0%

profile of v5, /device:TPU:0, one launch (start us, length us, event | category | flops | bytes accessed | tf_op | source)
XLA Modules:
  0.0 24.9 jit_solution(2935436609344097572)
XLA Ops:
  0.0 4.0 %collective-permute-start.1 = (bf16[2,32,128]{2,1,0:T(8,128)(2,1)}, bf16[2,32,128]{2,1,0:T(8,128)(2,1)S(1)}, u32[]{:S(2)}, u32[]{:S(2)}) collective-permute-start(bf16[2,32,128]{2,1,0:T(8,128)(2,1)} %param.4), channel_id=1, source_target_pairs={{0,8},{1,11},{2,10},{3,9},{4,12},{5,15},{6,14},{7,13},{8,0},{9,3},... | collective-permute-start | bytes 49160 | tf_op jit(solution)/shard_map/ppermute | solution.py:154
  4.0 1.6 %collective-permute-start = (bf16[2,32,128]{2,1,0:T(8,128)(2,1)}, bf16[2,32,128]{2,1,0:T(8,128)(2,1)S(1)}, u32[]{:S(2)}, u32[]{:S(2)}) collective-permute-start(bf16[2,32,128]{2,1,0:T(8,128)(2,1)} %param.4), channel_id=1, source_target_pairs={{0,4},{1,7},{2,6},{3,5},{4,0},{5,3},{6,2},{7,1},{8,12},{9,15},{10,... | collective-permute-start | bytes 49160 | tf_op jit(solution)/shard_map/ppermute | solution.py:154
  5.6 0.4 %collective-permute-done.1 = bf16[2,32,128]{2,1,0:T(8,128)(2,1)S(1)} collective-permute-done((bf16[2,32,128]{2,1,0:T(8,128)(2,1)}, bf16[2,32,128]{2,1,0:T(8,128)(2,1)S(1)}, u32[]{:S(2)}, u32[]{:S(2)}) %collective-permute-start.1) | collective-permute-done | bytes 16416 | tf_op jit(solution)/shard_map/ppermute | solution.py:154
  6.0 2.0 %collective-permute-done = bf16[2,32,128]{2,1,0:T(8,128)(2,1)S(1)} collective-permute-done((bf16[2,32,128]{2,1,0:T(8,128)(2,1)}, bf16[2,32,128]{2,1,0:T(8,128)(2,1)S(1)}, u32[]{:S(2)}, u32[]{:S(2)}) %collective-permute-start) | collective-permute-done | bytes 16416 | tf_op jit(solution)/shard_map/ppermute | solution.py:154
  8.0 0.2 collective-permute-start.3
  8.2 1.6 %collective-permute-start.2 = (bf16[4,32,128]{2,1,0:T(8,128)(2,1)S(1)}, bf16[4,32,128]{2,1,0:T(8,128)(2,1)S(1)}, u32[]{:S(2)}, u32[]{:S(2)}) collective-permute-start(bf16[4,32,128]{2,1,0:T(8,128)(2,1)S(1)} %pad_maximum_fusion.refs_0_), channel_id=1, source_target_pairs={{0,4},{1,5},{2,6},{3,7},{4,0},{5,1},{6,2},{7,3},{8,12},{9,13},{10,... | collective-permute-start | bytes 98312 | tf_op jit(solution)/shard_map/ppermute | solution.py:154
  9.8 0.0 copy-start.1
  9.8 2.3 %collective-permute-done.2.refs_1_ = bf16[4,32,128]{2,1,0:T(8,128)(2,1)S(1)} collective-permute-done((bf16[4,32,128]{2,1,0:T(8,128)(2,1)S(1)}, bf16[4,32,128]{2,1,0:T(8,128)(2,1)S(1)}, u32[]{:S(2)}, u32[]{:S(2)}) %collective-permute-start.2) | collective-permute-done | bytes 32800 | tf_op jit(solution)/shard_map/ppermute | solution.py:154
  12.1 0.0 collective-permute-done.3.refs_3_
  12.1 0.0 copy-done.1
  12.1 2.5 %score.1 = (f32[2,64]{1,0:T(2,128)S(1)}, f32[2,64]{1,0:T(2,128)S(1)}, f32[4,64]{1,0:T(4,128)S(1)}) custom-call(s32[1]{0:T(128)} %bitcast.1.me_ref, s32[32]{0:T(128)S(1)} %copy-done.1, bf16[4,32,128]{2,1,0:T(8,128)(2,1)S(1)} %pad_maximum_fusion.refs_0_, bf16[4,32,128]{2,1,0:T(8,128)(2,1)S(1)} %collective-permute-done.2.refs_1_, bf16[32,64,128]{2,1,0:T(8,128)(2,1)} %refs_2_.1, ...), custom_call_target="tpu_custom_call" | custom-call | tf_op jit(solution)/shard_map/score/pallas_call | solution.py:70
  14.6 1.6 %collective-permute-start.4 = (f32[4,64]{1,0:T(4,128)S(1)}, f32[4,64]{1,0:T(4,128)S(1)}, u32[]{:S(2)}, u32[]{:S(2)}) collective-permute-start(f32[4,64]{1,0:T(4,128)S(1)} %get-tuple-element.13), channel_id=1, source_target_pairs={{0,4},{1,5},{2,6},{3,7},{4,0},{5,1},{6,2},{7,3},{8,12},{9,13},{10,... | collective-permute-start | bytes 3080 | tf_op jit(solution)/shard_map/ppermute | solution.py:154
  16.3 2.0 %collective-permute-done.4 = f32[4,64]{1,0:T(4,128)S(1)} collective-permute-done((f32[4,64]{1,0:T(4,128)S(1)}, f32[4,64]{1,0:T(4,128)S(1)}, u32[]{:S(2)}, u32[]{:S(2)}) %collective-permute-start.4) | collective-permute-done | bytes 1056 | tf_op jit(solution)/shard_map/ppermute | solution.py:154
  18.3 0.8 %collective-permute-start.7 = (f32[2,64]{1,0:T(2,128)S(1)}, f32[2,64]{1,0:T(2,128)S(1)}, u32[]{:S(2)}, u32[]{:S(2)}) collective-permute-start(f32[2,64]{1,0:T(2,128)S(1)} %get-tuple-element.15), channel_id=1, source_target_pairs={{0,8},{1,11},{2,10},{3,9},{4,12},{5,15},{6,14},{7,13},{8,0},{9,3},... | collective-permute-start | bytes 1544 | tf_op jit(solution)/shard_map/ppermute | solution.py:154
  19.1 1.8 %collective-permute-start.5 = (f32[2,64]{1,0:T(2,128)S(1)}, f32[2,64]{1,0:T(2,128)S(1)}, u32[]{:S(2)}, u32[]{:S(2)}) collective-permute-start(f32[2,64]{1,0:T(2,128)S(1)} %get-tuple-element.16), channel_id=1, source_target_pairs={{0,4},{1,7},{2,6},{3,5},{4,0},{5,3},{6,2},{7,1},{8,12},{9,15},{10,... | collective-permute-start | bytes 1544 | tf_op jit(solution)/shard_map/ppermute | solution.py:154
  20.9 0.0 copy-start
  20.9 1.9 %collective-permute-done.7.refs_2_ = f32[2,64]{1,0:T(2,128)S(1)} collective-permute-done((f32[2,64]{1,0:T(2,128)S(1)}, f32[2,64]{1,0:T(2,128)S(1)}, u32[]{:S(2)}, u32[]{:S(2)}) %collective-permute-start.7) | collective-permute-done | bytes 544 | tf_op jit(solution)/shard_map/ppermute | solution.py:154
  22.7 0.0 collective-permute-start.8
  22.8 0.0 collective-permute-done.5.refs_0_
  22.8 0.5 %collective-permute-start.6 = (f32[2,64]{1,0:T(2,128)S(1)}, f32[2,64]{1,0:T(2,128)S(1)}, u32[]{:S(2)}, u32[]{:S(2)}) collective-permute-start(f32[2,64]{1,0:T(2,128)S(1)} %collective-permute-done.5.refs_0_), channel_id=1, source_target_pairs={{0,1},{1,0},{2,3},{3,2},{4,5},{5,4},{6,7},{7,6},{8,9},{9,8},{10,11... | collective-permute-start | bytes 1544 | tf_op jit(solution)/shard_map/ppermute | solution.py:157
  23.3 0.6 %collective-permute-done.8.refs_3_ = f32[2,64]{1,0:T(2,128)S(1)} collective-permute-done((f32[2,64]{1,0:T(2,128)S(1)}, f32[2,64]{1,0:T(2,128)S(1)}, u32[]{:S(2)}, u32[]{:S(2)}) %collective-permute-start.8) | collective-permute-done | bytes 544 | tf_op jit(solution)/shard_map/ppermute | solution.py:157
  23.9 0.2 collective-permute-done.6.refs_1_
  24.1 0.0 copy-done
  24.1 0.8 %pick.1 = f32[2,1000]{1,0:T(2,128)} custom-call(s32[1]{0:T(128)} %bitcast.base_ref, s32[2,1000]{1,0:T(2,128)S(1)} %copy-done, f32[2,64]{1,0:T(2,128)S(1)} %collective-permute-done.5.refs_0_, f32[2,64]{1,0:T(2,128)S(1)} %collective-permute-done.6.refs_1_, f32[2,64]{1,0:T(2,128)S(1)} %collective-permute-done.7.refs_2_, f32[2,64]{1,0:T(2,128)S(1)} %collective-permute-done.8.refs_3_), custom_call_target="tpu_custom_call" | custom-call | tf_op jit(solution)/shard_map/pick/pallas_call | solution.py:112
  (2 shorter events, 0.0 us)
Async XLA Ops:
  0.0 6.0 %collective-permute-start.1 = (bf16[2,32,128]{2,1,0:T(8,128)(2,1)}, bf16[2,32,128]{2,1,0:T(8,128)(2,1)S(1)}, u32[]{:S(2)}, u32[]{:S(2)}) collective-permute-start(bf16[2,32,128]{2,1,0:T(8,128)(2,1)} %param.4), channel_id=1, source_target_pairs={{0,8},{1,11},{2,10},{3,9},{4,12},{5,15},{6,14},{7,13},{8,0},{9,3},... | collective-permute-start | bytes 49160 | tf_op jit(solution)/shard_map/ppermute | solution.py:154
  4.0 3.9 %collective-permute-start = (bf16[2,32,128]{2,1,0:T(8,128)(2,1)}, bf16[2,32,128]{2,1,0:T(8,128)(2,1)S(1)}, u32[]{:S(2)}, u32[]{:S(2)}) collective-permute-start(bf16[2,32,128]{2,1,0:T(8,128)(2,1)} %param.4), channel_id=1, source_target_pairs={{0,4},{1,7},{2,6},{3,5},{4,0},{5,3},{6,2},{7,1},{8,12},{9,15},{10,... | collective-permute-start | bytes 49160 | tf_op jit(solution)/shard_map/ppermute | solution.py:154
  8.0 4.2 %collective-permute-start.3 = (bf16[32,64,128]{2,1,0:T(8,128)(2,1)}, bf16[32,64,128]{2,1,0:T(8,128)(2,1)S(1)}, u32[]{:S(2)}, u32[]{:S(2)}) collective-permute-start(bf16[32,64,128]{2,1,0:T(8,128)(2,1)} %refs_2_.1), channel_id=1, source_target_pairs={{0,1},{1,0},{2,3},{3,2},{4,5},{5,4},{6,7},{7,6},{8,9},{9,8},{10,11... | collective-permute-start | bytes 1572872 | tf_op jit(solution)/shard_map/ppermute | solution.py:157
  8.2 3.9 %collective-permute-start.2 = (bf16[4,32,128]{2,1,0:T(8,128)(2,1)S(1)}, bf16[4,32,128]{2,1,0:T(8,128)(2,1)S(1)}, u32[]{:S(2)}, u32[]{:S(2)}) collective-permute-start(bf16[4,32,128]{2,1,0:T(8,128)(2,1)S(1)} %pad_maximum_fusion.refs_0_), channel_id=1, source_target_pairs={{0,4},{1,5},{2,6},{3,7},{4,0},{5,1},{6,2},{7,3},{8,12},{9,13},{10,... | collective-permute-start | bytes 98312 | tf_op jit(solution)/shard_map/ppermute | solution.py:154
  9.8 2.3 %copy-start.1 = (s32[32]{0:T(128)S(1)}, s32[32]{0:T(128)}, u32[]{:S(2)}) copy-start(s32[32]{0:T(128)} %lens_ref.1) | copy-start | bytes 388
  14.6 3.7 %collective-permute-start.4 = (f32[4,64]{1,0:T(4,128)S(1)}, f32[4,64]{1,0:T(4,128)S(1)}, u32[]{:S(2)}, u32[]{:S(2)}) collective-permute-start(f32[4,64]{1,0:T(4,128)S(1)} %get-tuple-element.13), channel_id=1, source_target_pairs={{0,4},{1,5},{2,6},{3,7},{4,0},{5,1},{6,2},{7,3},{8,12},{9,13},{10,... | collective-permute-start | bytes 3080 | tf_op jit(solution)/shard_map/ppermute | solution.py:154
  18.3 4.5 %collective-permute-start.7 = (f32[2,64]{1,0:T(2,128)S(1)}, f32[2,64]{1,0:T(2,128)S(1)}, u32[]{:S(2)}, u32[]{:S(2)}) collective-permute-start(f32[2,64]{1,0:T(2,128)S(1)} %get-tuple-element.15), channel_id=1, source_target_pairs={{0,8},{1,11},{2,10},{3,9},{4,12},{5,15},{6,14},{7,13},{8,0},{9,3},... | collective-permute-start | bytes 1544 | tf_op jit(solution)/shard_map/ppermute | solution.py:154
  19.1 3.6 %collective-permute-start.5 = (f32[2,64]{1,0:T(2,128)S(1)}, f32[2,64]{1,0:T(2,128)S(1)}, u32[]{:S(2)}, u32[]{:S(2)}) collective-permute-start(f32[2,64]{1,0:T(2,128)S(1)} %get-tuple-element.16), channel_id=1, source_target_pairs={{0,4},{1,7},{2,6},{3,5},{4,0},{5,3},{6,2},{7,1},{8,12},{9,15},{10,... | collective-permute-start | bytes 1544 | tf_op jit(solution)/shard_map/ppermute | solution.py:154
  20.9 3.2 %copy-start = (s32[2,1000]{1,0:T(2,128)S(1)}, s32[2,1000]{1,0:T(2,128)}, u32[]{:S(2)}) copy-start(s32[2,1000]{1,0:T(2,128)} %cand_ref.1) | copy-start | bytes 24004
  22.7 1.1 %collective-permute-start.8 = (f32[2,64]{1,0:T(2,128)S(1)}, f32[2,64]{1,0:T(2,128)S(1)}, u32[]{:S(2)}, u32[]{:S(2)}) collective-permute-start(f32[2,64]{1,0:T(2,128)S(1)} %collective-permute-done.7.refs_2_), channel_id=1, source_target_pairs={{0,1},{1,0},{2,3},{3,2},{4,5},{5,4},{6,7},{7,6},{8,9},{9,8},{10,11... | collective-permute-start | bytes 1544 | tf_op jit(solution)/shard_map/ppermute | solution.py:157
  22.8 1.3 %collective-permute-start.6 = (f32[2,64]{1,0:T(2,128)S(1)}, f32[2,64]{1,0:T(2,128)S(1)}, u32[]{:S(2)}, u32[]{:S(2)}) collective-permute-start(f32[2,64]{1,0:T(2,128)S(1)} %collective-permute-done.5.refs_0_), channel_id=1, source_target_pairs={{0,1},{1,0},{2,3},{3,2},{4,5},{5,4},{6,7},{7,6},{8,9},{9,8},{10,11... | collective-permute-start | bytes 1544 | tf_op jit(solution)/shard_map/ppermute | solution.py:157

commit v6 on v5

v6 whole, which is shorter than its diff:
```python
import functools

import jax
import jax.numpy as jnp
from jax import lax
from jax.experimental import pallas as pl
from jax.experimental.pallas import tpu as pltpu
from jax.sharding import PartitionSpec as P

INDEX_AXES = ("shard", "qgrp")
ALL_AXES = ("shard", "qgrp", "dim")
LOW = -1e30
LANES = 128
BLOCK = 256


def score_kernel(n_pieces, with_own, put, me_ref, lens_ref, *refs):
    piece_refs = refs[:n_pieces]
    own_ref, other_ref = refs[n_pieces: n_pieces + 2]
    out_refs = refs[n_pieces + 2: -6]
    flat_ref, turned_ref, part_ref, max_ref, held_ref, sem = refs[-6:]
    core = me_ref[0]
    q_tokens, width = piece_refs[0].shape[1:]
    count, half, _ = own_ref.shape
    total = flat_ref.shape[0]
    fetch = pltpu.make_async_copy(own_ref, held_ref, sem)
    fetch.start()
    at = 0
    for k in range(n_pieces - int(with_own)):
        rows = piece_refs[k].shape[0] * q_tokens
        piece = piece_refs[k][...].reshape(rows, width)
        if with_own and k == n_pieces - 2:
            piece = jnp.where(core == 0, piece_refs[k + 1][...].reshape(rows, width), piece)
        flat_ref[pl.ds(at, rows), :] = piece
        at += rows
    turned_ref[...] = flat_ref[...].T
    block = min(total, BLOCK)
    step = min(count, 8)
    rows = lax.broadcasted_iota(jnp.int32, (half, LANES), 0)

    def best_of(ref, first, last):
        def group(g, _):
            start = g * step
            docs = ref[pl.ds(start, step)].reshape(step * half, width)
            for at in range(0, total, block):
                scores = jnp.dot(docs, turned_ref[:, pl.ds(at, block)], preferred_element_type=jnp.float32)
                for lane in range(0, block, LANES):
                    to = pl.ds(at + lane, LANES)
                    bests = []
                    for k in range(step):
                        part = scores[k * half: (k + 1) * half, lane: lane + LANES]
                        part = jnp.where(rows < lens_ref[start + k] - first, part, LOW)
                        best = jnp.max(part.reshape(half // 8, 8, LANES), axis=0)
                        spot = pl.ds(pl.multiple_of((start + k) * 8, 8), 8)
                        if last:
                            best = jnp.maximum(best, part_ref[spot, to])
                            bests.append(jnp.max(best, axis=0, keepdims=True))
                        else:
                            part_ref[spot, to] = best
                    if last:
                        max_ref[pl.ds(pl.multiple_of(start, step), step), to] = jnp.concatenate(bests, axis=0)
            return 0

        lax.fori_loop(0, count // step, group, 0, unroll=total <= block)

    best_of(other_ref, (1 - core) * half, False)
    fetch.wait()
    best_of(held_ref, core * half, True)
    put(jnp.sum(max_ref[...].T.reshape(total // q_tokens, q_tokens, count), axis=1), out_refs)


def score(core, doc_lens, pieces, doc_tokens, other, put, out_shapes, with_own):
    smem = pl.BlockSpec(memory_space=pltpu.SMEM)
    vmem = pl.BlockSpec(memory_space=pltpu.VMEM)
    hbm = pl.BlockSpec(memory_space=pltpu.HBM)
    count = doc_tokens.shape[0]
    queries = sum(p.shape[0] for p in pieces[int(with_own):])
    q_tokens, width = pieces[0].shape[1:]
    doc_tokens = pltpu.with_memory_space_constraint(doc_tokens, pltpu.HBM)
    return pl.pallas_call(
        functools.partial(score_kernel, len(pieces), with_own, put),
        out_shape=[jax.ShapeDtypeStruct(shape, jnp.float32) for shape in out_shapes],
        in_specs=[smem, smem] + [vmem] * len(pieces) + [hbm, vmem],
        out_specs=[vmem] * len(out_shapes),
        scratch_shapes=[
            pltpu.VMEM((queries * q_tokens, width), jnp.bfloat16),
            pltpu.VMEM((width, queries * q_tokens), jnp.bfloat16),
            pltpu.VMEM((count * 8, queries * q_tokens), jnp.float32),
            pltpu.VMEM((count, queries * q_tokens), jnp.float32),
            pltpu.VMEM(doc_tokens.shape, jnp.bfloat16),
            pltpu.SemaphoreType.DMA(()),
        ],
        compiler_params=pltpu.CompilerParams(vmem_limit_bytes=(8 + queries // 10) * 1024 * 1024),
        name="score",
    )(core.reshape(1), doc_lens, *pieces, doc_tokens, other)


def pick_kernel(n_pieces, wide, base_ref, cand_ref, *refs):
    piece_refs, out_ref = refs[:n_pieces], refs[n_pieces]
    parts = [ref[...] for ref in piece_refs]
    parts = [part[:, t: t + wide] for group in zip(*[iter(parts)] * min(2, n_pieces))
             for t in range(0, parts[0].shape[1], wide) for part in group]
    table = jnp.concatenate(parts, axis=1) if len(parts) > 1 else parts[0]
    size = table.shape[1]
    rows, width = cand_ref.shape
    spot = jnp.bitwise_xor(cand_ref[...], base_ref[0])
    for at in range(0, width, LANES):
        wide = min(LANES, width - at)
        index = spot[:, at: at + wide]
        if wide < LANES:
            index = jnp.concatenate([index, jnp.zeros((rows, LANES - wide), jnp.int32)], axis=1)
        low = jnp.bitwise_and(index, LANES - 1)
        high = lax.shift_right_logical(index, LANES.bit_length() - 1)
        value = jnp.zeros((rows, LANES), jnp.float32)
        for t in range(0, size, LANES):
            found = jnp.take_along_axis(table[:, t: t + LANES], low, axis=1, mode="promise_in_bounds")
            value = jnp.where(high == t // LANES, found, value)
        out_ref[:, pl.ds(at, wide)] = value[:, :wide]


def pick(base, candidates, pieces, wide):
    smem = pl.BlockSpec(memory_space=pltpu.SMEM)
    vmem = pl.BlockSpec(memory_space=pltpu.VMEM)
    return pl.pallas_call(
        functools.partial(pick_kernel, len(pieces), wide),
        out_shape=jax.ShapeDtypeStruct(candidates.shape, jnp.float32),
        in_specs=[smem, vmem] + [vmem] * len(pieces),
        out_specs=vmem,
        compiler_params=pltpu.CompilerParams(vmem_limit_bytes=4 * 1024 * 1024),
        name="pick",
    )(base.reshape(1), candidates, *pieces)


def two_columns(queries, doc_tokens, doc_lens, candidates, n_z, core):
    q_owned = queries.shape[0]
    count = doc_tokens.shape[0]

    def exchange(array, dz, dx0, dx1):
        pairs = [
            ((z * 2 + x) * 2 + d, ((z ^ dz) * 2 + (x ^ dx)) * 2 + d)
            for z in range(n_z) for x in range(2) for d, dx in enumerate((dx0, dx1))
        ]
        return lax.ppermute(array, ALL_AXES, pairs)

    def cross(array):
        return lax.ppermute(array, "dim", [(0, 1), (1, 0)])

    other = cross(doc_tokens)
    far_first = list(reversed(range(n_z)))
    pieces = [exchange(queries, dz, int(dz == 0), 1) for dz in far_first]

    def put(scores, out_refs):
        for k, out_ref in enumerate(out_refs):
            out_ref[...] = scores[k * q_owned: (k + 1) * q_owned]

    blocks = score(core, doc_lens, pieces + [queries], doc_tokens, other, put, [(q_owned, count)] * n_z, True)
    table = []
    for dz, block in zip(far_first, blocks):
        moved = exchange(block, dz, int(dz == 0), 1)
        if dz == 0:
            moved = jnp.where(core == 0, block, moved)
        table += [moved, cross(moved)]
    base = ((lax.axis_index("shard") ^ (n_z - 1)) * 2 + (lax.axis_index("qgrp") ^ core)) * count
    return pick(base, candidates, table, count)


def any_columns(queries, doc_tokens, doc_lens, candidates, n, cores, core):
    q_owned = candidates.shape[0]
    count = doc_tokens.shape[0]
    gathered = lax.all_gather(queries, INDEX_AXES, axis=0, tiled=True)
    other = lax.ppermute(doc_tokens, "dim", [(s, cores - 1 - s) for s in range(cores)])

    def put(scores, out_refs):
        out_refs[0][...] = scores

    block = score(core, doc_lens, [gathered], doc_tokens, other, put, [(n * q_owned, count)], False)[0]
    moved = lax.all_to_all(
        block.reshape(n, q_owned, count), INDEX_AXES, split_axis=0, concat_axis=0, tiled=True
    )
    table = moved.transpose(1, 0, 2).reshape(q_owned, n * count)
    return pick(jnp.int32(0), candidates, [table], n * count)


def per_device(queries, doc_tokens, doc_lens, candidates):
    sizes = n_z, n_x, cores = tuple(lax.axis_size(axis) for axis in ALL_AXES)
    count = doc_tokens.shape[0]
    core = lax.axis_index("dim")
    if sizes in ((4, 2, 2), (2, 2, 2)) and count & (count - 1) == 0:
        return two_columns(queries, doc_tokens, doc_lens, candidates, n_z, core)
    return any_columns(queries, doc_tokens, doc_lens, candidates, n_z * n_x, cores, core)


def solution(mesh):
    in_specs = (
        P(("groups",) + INDEX_AXES, None, None),
        P(("groups",) + INDEX_AXES, "dim", None),
        P(("groups",) + INDEX_AXES),
        P(("groups",) + INDEX_AXES, None),
    )
    out_specs = P(("groups",) + INDEX_AXES, None)
    return jax.shard_map(
        per_device, mesh=mesh, in_specs=in_specs, out_specs=out_specs, check_vma=False
    )
```

time: 25 us -> 24 us (0.960)
  waiting for transfers between devices: 9.41 us -> 6.86 us
  starting transfers between devices: 12.2 us -> 13.8 us
    ppermute x6 -> x8, waiting for transfers between devices: 8.58 us -> 6.04 us  [exchange(): return lax.ppermute(array, ALL_AXES, pairs)]
    ppermute x6 -> x8, starting transfers between devices: 11.4 us -> 12.5 us  [exchange(): return lax.ppermute(array, ALL_AXES, pairs)]
    ppermute x3 -> x5, starting transfers between devices: 0.74 us -> 1.32 us  [cross(): return lax.ppermute(array, 'dim', [(0, 1), (1, 0)])]
    ppermute x3 -> x5, waiting for transfers between devices: 0.82 us -> 0.82 us  [cross(): return lax.ppermute(array, 'dim', [(0, 1), (1, 0)])]
  transfers between devices with their start and end apart: 9 -> 13, of which waited for: 7 -> 4; matrix products, arithmetic and copies ran while one was open for 0% -> 0% of each run, Pallas kernels for 0% -> 0%
where the time goes in v6:
time: 24 us; the launch traced here: 23.9 us
  starting transfers between devices  13.8 us (58%)
  waiting for transfers between devices  6.86 us (29%)
  Pallas kernels  3.2 us (13%)
    ppermute x8, starting transfers between devices, exchange(): return lax.ppermute(array, ALL_AXES, pairs)  12.5 us
    ppermute x8, waiting for transfers between devices, exchange(): return lax.ppermute(array, ALL_AXES, pairs)  6.04 us
    pallas_call x1, Pallas kernels, score(): pl.pallas_call(functools.partial(score_kernel, len(pieces), with_own, put...  2.42 us
    ppermute x5, starting transfers between devices, cross(): return lax.ppermute(array, 'dim', [(0, 1), (1, 0)])  1.32 us
    ppermute x5, waiting for transfers between devices, cross(): return lax.ppermute(array, 'dim', [(0, 1), (1, 0)])  0.82 us
    pallas_call x1, Pallas kernels, pick(): pl.pallas_call(functools.partial(pick_kernel, len(pieces), wide), out_sha...  0.78 us
  transfers between devices with their start and end apart: 13, of which 4 were waited for; matrix products, arithmetic and copies ran while one was open for 0% of the time, Pallas kernels for 0%

profile of v6, /device:TPU:0, one launch (start us, length us, event | category | flops | bytes accessed | tf_op | source)
XLA Modules:
  0.0 23.9 jit_solution(11929051431060720871)
XLA Ops:
  0.0 0.5 %collective-permute-start.4 = (bf16[32,64,128]{2,1,0:T(8,128)(2,1)}, bf16[32,64,128]{2,1,0:T(8,128)(2,1)S(1)}, u32[]{:S(2)}, u32[]{:S(2)}) collective-permute-start(bf16[32,64,128]{2,1,0:T(8,128)(2,1)} %refs_5_.1), channel_id=1, source_target_pairs={{0,1},{1,0},{2,3},{3,2},{4,5},{5,4},{6,7},{7,6},{8,9},{9,8},{10,11... | collective-permute-start | bytes 1572872 | tf_op jit(solution)/shard_map/ppermute | solution.py:146
  0.5 4.7 %collective-permute-start = (bf16[2,32,128]{2,1,0:T(8,128)(2,1)}, bf16[2,32,128]{2,1,0:T(8,128)(2,1)S(1)}, u32[]{:S(2)}, u32[]{:S(2)}) collective-permute-start(bf16[2,32,128]{2,1,0:T(8,128)(2,1)} %refs_4_.1), channel_id=1, source_target_pairs={{0,12},{1,15},{2,14},{3,13},{4,8},{5,11},{6,10},{7,9},{8,4},{9,7},... | collective-permute-start | bytes 49160 | tf_op jit(solution)/shard_map/ppermute | solution.py:143
  5.1 0.0 collective-permute-start.1
  5.1 0.6 %collective-permute-start.2 = (bf16[2,32,128]{2,1,0:T(8,128)(2,1)}, bf16[2,32,128]{2,1,0:T(8,128)(2,1)S(1)}, u32[]{:S(2)}, u32[]{:S(2)}) collective-permute-start(bf16[2,32,128]{2,1,0:T(8,128)(2,1)} %refs_4_.1), channel_id=1, source_target_pairs={{0,4},{1,7},{2,6},{3,5},{4,0},{5,3},{6,2},{7,1},{8,12},{9,15},{10,... | collective-permute-start | bytes 49160 | tf_op jit(solution)/shard_map/ppermute | solution.py:143
  5.8 1.6 %collective-permute-start.3 = (bf16[2,32,128]{2,1,0:T(8,128)(2,1)}, bf16[2,32,128]{2,1,0:T(8,128)(2,1)S(1)}, u32[]{:S(2)}, u32[]{:S(2)}) collective-permute-start(bf16[2,32,128]{2,1,0:T(8,128)(2,1)} %refs_4_.1), channel_id=1, source_target_pairs={{0,2},{1,3},{2,0},{3,1},{4,6},{5,7},{6,4},{7,5},{8,10},{9,11},{10,... | collective-permute-start | bytes 49160 | tf_op jit(solution)/shard_map/ppermute | solution.py:143
  7.4 0.0 collective-permute-done.refs_0_
  7.4 2.6 %collective-permute-done.1.refs_1_ = bf16[2,32,128]{2,1,0:T(8,128)(2,1)S(1)} collective-permute-done((bf16[2,32,128]{2,1,0:T(8,128)(2,1)}, bf16[2,32,128]{2,1,0:T(8,128)(2,1)S(1)}, u32[]{:S(2)}, u32[]{:S(2)}) %collective-permute-start.1) | collective-permute-done | bytes 16416 | tf_op jit(solution)/shard_map/ppermute | solution.py:143
  10.0 0.0 collective-permute-done.2.refs_2_
  10.0 0.0 collective-permute-done.3.refs_3_
  10.0 0.0 collective-permute-done.4.refs_6_
  10.1 0.0 copy-done
  10.1 0.0 copy-done.2
  10.1 2.4 %score.1 = (f32[2,32]{1,0:T(2,128)S(1)}, f32[2,32]{1,0:T(2,128)S(1)}, f32[2,32]{1,0:T(2,128)S(1)}, f32[2,32]{1,0:T(2,128)S(1)}) custom-call(s32[1]{0:T(128)} %bitcast.1.me_ref, s32[32]{0:T(128)S(1)} %copy-done.2, bf16[2,32,128]{2,1,0:T(8,128)(2,1)S(1)} %collective-permute-done.refs_0_, bf16[2,32,128]{2,1,0:T(8,128)(2,1)S(1)} %collective-permute-done.1.refs_1_, ...), custom_call_target="tpu_custom_call" | custom-call | tf_op jit(solution)/shard_map/score/pallas_call | solution.py:80
  12.5 0.0 copy-start.1
  12.5 1.6 %collective-permute-start.11 = (f32[2,32]{1,0:T(2,128)S(1)}, f32[2,32]{1,0:T(2,128)S(1)}, u32[]{:S(2)}, u32[]{:S(2)}) collective-permute-start(f32[2,32]{1,0:T(2,128)S(1)} %get-tuple-element.12), channel_id=1, source_target_pairs={{0,2},{1,3},{2,0},{3,1},{4,6},{5,7},{6,4},{7,5},{8,10},{9,11},{10,... | collective-permute-start | bytes 776 | tf_op jit(solution)/shard_map/ppermute | solution.py:143
  14.1 1.0 %collective-permute-start.9 = (f32[2,32]{1,0:T(2,128)S(1)}, f32[2,32]{1,0:T(2,128)S(1)}, u32[]{:S(2)}, u32[]{:S(2)}) collective-permute-start(f32[2,32]{1,0:T(2,128)S(1)} %get-tuple-element.11), channel_id=1, source_target_pairs={{0,4},{1,7},{2,6},{3,5},{4,0},{5,3},{6,2},{7,1},{8,12},{9,15},{10,... | collective-permute-start | bytes 776 | tf_op jit(solution)/shard_map/ppermute | solution.py:143
  15.1 2.4 %collective-permute-start.5 = (f32[2,32]{1,0:T(2,128)S(1)}, f32[2,32]{1,0:T(2,128)S(1)}, u32[]{:S(2)}, u32[]{:S(2)}) collective-permute-start(f32[2,32]{1,0:T(2,128)S(1)} %get-tuple-element.9), channel_id=1, source_target_pairs={{0,12},{1,15},{2,14},{3,13},{4,8},{5,11},{6,10},{7,9},{8,4},{9,7},... | collective-permute-start | bytes 776 | tf_op jit(solution)/shard_map/ppermute | solution.py:143
  17.5 0.6 %collective-permute-start.7 = (f32[2,32]{1,0:T(2,128)S(1)}, f32[2,32]{1,0:T(2,128)S(1)}, u32[]{:S(2)}, u32[]{:S(2)}) collective-permute-start(f32[2,32]{1,0:T(2,128)S(1)} %get-tuple-element.10), channel_id=1, source_target_pairs={{0,8},{1,11},{2,10},{3,9},{4,12},{5,15},{6,14},{7,13},{8,0},{9,3},... | collective-permute-start | bytes 776 | tf_op jit(solution)/shard_map/ppermute | solution.py:143
  18.0 0.0 collective-permute-done.11
  18.0 0.1 collective-permute-start.12
  18.2 0.0 collective-permute-done.9.refs_4_
  18.2 0.4 %collective-permute-start.10 = (f32[2,32]{1,0:T(2,128)S(1)}, f32[2,32]{1,0:T(2,128)S(1)}, u32[]{:S(2)}, u32[]{:S(2)}) collective-permute-start(f32[2,32]{1,0:T(2,128)S(1)} %collective-permute-done.9.refs_4_), channel_id=1, source_target_pairs={{0,1},{1,0},{2,3},{3,2},{4,5},{5,4},{6,7},{7,6},{8,9},{9,8},{10,11... | collective-permute-start | bytes 776 | tf_op jit(solution)/shard_map/ppermute | solution.py:146
  18.6 1.9 %collective-permute-done.5.refs_0_ = f32[2,32]{1,0:T(2,128)S(1)} collective-permute-done((f32[2,32]{1,0:T(2,128)S(1)}, f32[2,32]{1,0:T(2,128)S(1)}, u32[]{:S(2)}, u32[]{:S(2)}) %collective-permute-start.5) | collective-permute-done | bytes 288 | tf_op jit(solution)/shard_map/ppermute | solution.py:143
  20.5 0.0 collective-permute-start.6
  20.5 1.5 %collective-permute-done.7.refs_2_ = f32[2,32]{1,0:T(2,128)S(1)} collective-permute-done((f32[2,32]{1,0:T(2,128)S(1)}, f32[2,32]{1,0:T(2,128)S(1)}, u32[]{:S(2)}, u32[]{:S(2)}) %collective-permute-start.7) | collective-permute-done | bytes 288 | tf_op jit(solution)/shard_map/ppermute | solution.py:143
  21.9 0.4 %collective-permute-start.8 = (f32[2,32]{1,0:T(2,128)S(1)}, f32[2,32]{1,0:T(2,128)S(1)}, u32[]{:S(2)}, u32[]{:S(2)}) collective-permute-start(f32[2,32]{1,0:T(2,128)S(1)} %collective-permute-done.7.refs_2_), channel_id=1, source_target_pairs={{0,1},{1,0},{2,3},{3,2},{4,5},{5,4},{6,7},{7,6},{8,9},{9,8},{10,11... | collective-permute-start | bytes 776 | tf_op jit(solution)/shard_map/ppermute | solution.py:146
  22.3 0.0 collective-permute-done.12.refs_7_
  22.3 0.0 collective-permute-done.10.refs_5_
  22.3 0.0 collective-permute-done.6.refs_1_
  22.3 0.8 %collective-permute-done.8.refs_3_ = f32[2,32]{1,0:T(2,128)S(1)} collective-permute-done((f32[2,32]{1,0:T(2,128)S(1)}, f32[2,32]{1,0:T(2,128)S(1)}, u32[]{:S(2)}, u32[]{:S(2)}) %collective-permute-start.8) | collective-permute-done | bytes 288 | tf_op jit(solution)/shard_map/ppermute | solution.py:146
  23.1 0.0 copy-done.1
  23.1 0.8 %pick.1 = f32[2,1000]{1,0:T(2,128)} custom-call(s32[1]{0:T(128)} %bitcast.base_ref, s32[2,1000]{1,0:T(2,128)S(1)} %copy-done.1, f32[2,32]{1,0:T(2,128)S(1)} %collective-permute-done.5.refs_0_, f32[2,32]{1,0:T(2,128)S(1)} %collective-permute-done.6.refs_1_, f32[2,32]{1,0:T(2,128)S(1)} %collective-permute-done.7.refs_2_, ...), custom_call_target="tpu_custom_call" | custom-call | tf_op jit(solution)/shard_map/pick/pallas_call | solution.py:124
  (3 shorter events, 0.0 us)
Async XLA Ops:
  0.0 10.1 %copy-start = (bf16[2,32,128]{2,1,0:T(8,128)(2,1)S(1)}, bf16[2,32,128]{2,1,0:T(8,128)(2,1)}, u32[]{:S(2)}) copy-start(bf16[2,32,128]{2,1,0:T(8,128)(2,1)} %refs_4_.1) | copy-start | bytes 49156
  0.0 10.0 %collective-permute-start.4 = (bf16[32,64,128]{2,1,0:T(8,128)(2,1)}, bf16[32,64,128]{2,1,0:T(8,128)(2,1)S(1)}, u32[]{:S(2)}, u32[]{:S(2)}) collective-permute-start(bf16[32,64,128]{2,1,0:T(8,128)(2,1)} %refs_5_.1), channel_id=1, source_target_pairs={{0,1},{1,0},{2,3},{3,2},{4,5},{5,4},{6,7},{7,6},{8,9},{9,8},{10,11... | collective-permute-start | bytes 1572872 | tf_op jit(solution)/shard_map/ppermute | solution.py:146
  0.5 6.9 %collective-permute-start = (bf16[2,32,128]{2,1,0:T(8,128)(2,1)}, bf16[2,32,128]{2,1,0:T(8,128)(2,1)S(1)}, u32[]{:S(2)}, u32[]{:S(2)}) collective-permute-start(bf16[2,32,128]{2,1,0:T(8,128)(2,1)} %refs_4_.1), channel_id=1, source_target_pairs={{0,12},{1,15},{2,14},{3,13},{4,8},{5,11},{6,10},{7,9},{8,4},{9,7},... | collective-permute-start | bytes 49160 | tf_op jit(solution)/shard_map/ppermute | solution.py:143
  5.1 4.9 %collective-permute-start.1 = (bf16[2,32,128]{2,1,0:T(8,128)(2,1)}, bf16[2,32,128]{2,1,0:T(8,128)(2,1)S(1)}, u32[]{:S(2)}, u32[]{:S(2)}) collective-permute-start(bf16[2,32,128]{2,1,0:T(8,128)(2,1)} %refs_4_.1), channel_id=1, source_target_pairs={{0,8},{1,11},{2,10},{3,9},{4,12},{5,15},{6,14},{7,13},{8,0},{9,3},... | collective-permute-start | bytes 49160 | tf_op jit(solution)/shard_map/ppermute | solution.py:143
  5.1 4.9 %collective-permute-start.2 = (bf16[2,32,128]{2,1,0:T(8,128)(2,1)}, bf16[2,32,128]{2,1,0:T(8,128)(2,1)S(1)}, u32[]{:S(2)}, u32[]{:S(2)}) collective-permute-start(bf16[2,32,128]{2,1,0:T(8,128)(2,1)} %refs_4_.1), channel_id=1, source_target_pairs={{0,4},{1,7},{2,6},{3,5},{4,0},{5,3},{6,2},{7,1},{8,12},{9,15},{10,... | collective-permute-start | bytes 49160 | tf_op jit(solution)/shard_map/ppermute | solution.py:143
  5.8 4.3 %collective-permute-start.3 = (bf16[2,32,128]{2,1,0:T(8,128)(2,1)}, bf16[2,32,128]{2,1,0:T(8,128)(2,1)S(1)}, u32[]{:S(2)}, u32[]{:S(2)}) collective-permute-start(bf16[2,32,128]{2,1,0:T(8,128)(2,1)} %refs_4_.1), channel_id=1, source_target_pairs={{0,2},{1,3},{2,0},{3,1},{4,6},{5,7},{6,4},{7,5},{8,10},{9,11},{10,... | collective-permute-start | bytes 49160 | tf_op jit(solution)/shard_map/ppermute | solution.py:143
  7.4 2.7 %copy-start.2 = (s32[32]{0:T(128)S(1)}, s32[32]{0:T(128)}, u32[]{:S(2)}) copy-start(s32[32]{0:T(128)} %lens_ref.1) | copy-start | bytes 388
  12.5 10.6 %copy-start.1 = (s32[2,1000]{1,0:T(2,128)S(1)}, s32[2,1000]{1,0:T(2,128)}, u32[]{:S(2)}) copy-start(s32[2,1000]{1,0:T(2,128)} %cand_ref.1) | copy-start | bytes 24004
  12.5 5.5 %collective-permute-start.11 = (f32[2,32]{1,0:T(2,128)S(1)}, f32[2,32]{1,0:T(2,128)S(1)}, u32[]{:S(2)}, u32[]{:S(2)}) collective-permute-start(f32[2,32]{1,0:T(2,128)S(1)} %get-tuple-element.12), channel_id=1, source_target_pairs={{0,2},{1,3},{2,0},{3,1},{4,6},{5,7},{6,4},{7,5},{8,10},{9,11},{10,... | collective-permute-start | bytes 776 | tf_op jit(solution)/shard_map/ppermute | solution.py:143
  14.1 4.1 %collective-permute-start.9 = (f32[2,32]{1,0:T(2,128)S(1)}, f32[2,32]{1,0:T(2,128)S(1)}, u32[]{:S(2)}, u32[]{:S(2)}) collective-permute-start(f32[2,32]{1,0:T(2,128)S(1)} %get-tuple-element.11), channel_id=1, source_target_pairs={{0,4},{1,7},{2,6},{3,5},{4,0},{5,3},{6,2},{7,1},{8,12},{9,15},{10,... | collective-permute-start | bytes 776 | tf_op jit(solution)/shard_map/ppermute | solution.py:143
  15.1 5.4 %collective-permute-start.5 = (f32[2,32]{1,0:T(2,128)S(1)}, f32[2,32]{1,0:T(2,128)S(1)}, u32[]{:S(2)}, u32[]{:S(2)}) collective-permute-start(f32[2,32]{1,0:T(2,128)S(1)} %get-tuple-element.9), channel_id=1, source_target_pairs={{0,12},{1,15},{2,14},{3,13},{4,8},{5,11},{6,10},{7,9},{8,4},{9,7},... | collective-permute-start | bytes 776 | tf_op jit(solution)/shard_map/ppermute | solution.py:143
  17.5 4.5 %collective-permute-start.7 = (f32[2,32]{1,0:T(2,128)S(1)}, f32[2,32]{1,0:T(2,128)S(1)}, u32[]{:S(2)}, u32[]{:S(2)}) collective-permute-start(f32[2,32]{1,0:T(2,128)S(1)} %get-tuple-element.10), channel_id=1, source_target_pairs={{0,8},{1,11},{2,10},{3,9},{4,12},{5,15},{6,14},{7,13},{8,0},{9,3},... | collective-permute-start | bytes 776 | tf_op jit(solution)/shard_map/ppermute | solution.py:143
  18.0 4.3 %collective-permute-start.12 = (f32[2,32]{1,0:T(2,128)S(1)}, f32[2,32]{1,0:T(2,128)S(1)}, u32[]{:S(2)}, u32[]{:S(2)}) collective-permute-start(f32[2,32]{1,0:T(2,128)S(1)} %broadcast_select_fusion.refs_6_), channel_id=1, source_target_pairs={{0,1},{1,0},{2,3},{3,2},{4,5},{5,4},{6,7},{7,6},{8,9},{9,8},{10,11... | collective-permute-start | bytes 776 | tf_op jit(solution)/shard_map/ppermute | solution.py:146
  18.2 4.1 %collective-permute-start.10 = (f32[2,32]{1,0:T(2,128)S(1)}, f32[2,32]{1,0:T(2,128)S(1)}, u32[]{:S(2)}, u32[]{:S(2)}) collective-permute-start(f32[2,32]{1,0:T(2,128)S(1)} %collective-permute-done.9.refs_4_), channel_id=1, source_target_pairs={{0,1},{1,0},{2,3},{3,2},{4,5},{5,4},{6,7},{7,6},{8,9},{9,8},{10,11... | collective-permute-start | bytes 776 | tf_op jit(solution)/shard_map/ppermute | solution.py:146
  20.5 1.8 %collective-permute-start.6 = (f32[2,32]{1,0:T(2,128)S(1)}, f32[2,32]{1,0:T(2,128)S(1)}, u32[]{:S(2)}, u32[]{:S(2)}) collective-permute-start(f32[2,32]{1,0:T(2,128)S(1)} %collective-permute-done.5.refs_0_), channel_id=1, source_target_pairs={{0,1},{1,0},{2,3},{3,2},{4,5},{5,4},{6,7},{7,6},{8,9},{9,8},{10,11... | collective-permute-start | bytes 776 | tf_op jit(solution)/shard_map/ppermute | solution.py:146
  21.9 1.2 %collective-permute-start.8 = (f32[2,32]{1,0:T(2,128)S(1)}, f32[2,32]{1,0:T(2,128)S(1)}, u32[]{:S(2)}, u32[]{:S(2)}) collective-permute-start(f32[2,32]{1,0:T(2,128)S(1)} %collective-permute-done.7.refs_2_), channel_id=1, source_target_pairs={{0,1},{1,0},{2,3},{3,2},{4,5},{5,4},{6,7},{7,6},{8,9},{9,8},{10,11... | collective-permute-start | bytes 776 | tf_op jit(solution)/shard_map/ppermute | solution.py:146

commit v7 on v6

--- a/solution.py
+++ b/solution.py
@@ -155,12 +155,10 @@
 
     blocks = score(core, doc_lens, pieces + [queries], doc_tokens, other, put, [(q_owned, count)] * n_z, True)
     table = []
-    for dz, block in zip(far_first, blocks):
-        moved = exchange(block, dz, int(dz == 0), 1)
-        if dz == 0:
-            moved = jnp.where(core == 0, block, moved)
+    for dz, block in zip(reversed(far_first), reversed(blocks)):
+        moved = jnp.where(core == -dz, block, exchange(block, dz, int(dz == 0), 1))
         table += [moved, cross(moved)]
-    base = ((lax.axis_index("shard") ^ (n_z - 1)) * 2 + (lax.axis_index("qgrp") ^ core)) * count
+    base = (lax.axis_index("shard") * 2 + (lax.axis_index("qgrp") ^ core)) * count
     return pick(base, candidates, table, count)
 
 

time: 24 us -> 23 us (0.958)
  waiting for transfers between devices: 6.86 us -> 4.99 us
  starting transfers between devices: 13.8 us -> 14.6 us
    ppermute x8, waiting for transfers between devices: 6.04 us -> 3.96 us  [exchange(): return lax.ppermute(array, ALL_AXES, pairs)]
    ppermute x8, starting transfers between devices: 12.5 us -> 12.9 us  [exchange(): return lax.ppermute(array, ALL_AXES, pairs)]
    ppermute x5, starting transfers between devices: 1.32 us -> 1.73 us  [cross(): return lax.ppermute(array, 'dim', [(0, 1), (1, 0)])]
  transfers between devices with their start and end apart: 13 -> 13, of which waited for: 4 -> 5; matrix products, arithmetic and copies ran while one was open for 0% -> 0% of each run, Pallas kernels for 0% -> 0%
where the time goes in v7:
time: 23 us; the launch traced here: 22.9 us
  starting transfers between devices  14.6 us (63%)
  waiting for transfers between devices  4.99 us (22%)
  Pallas kernels  3.2 us (14%)
    ppermute x8, starting transfers between devices, exchange(): return lax.ppermute(array, ALL_AXES, pairs)  12.9 us
    ppermute x8, waiting for transfers between devices, exchange(): return lax.ppermute(array, ALL_AXES, pairs)  3.96 us
    pallas_call x1, Pallas kernels, score(): pl.pallas_call(functools.partial(score_kernel, len(pieces), with_own, put...  2.42 us
    ppermute x5, starting transfers between devices, cross(): return lax.ppermute(array, 'dim', [(0, 1), (1, 0)])  1.73 us
    ppermute x5, waiting for transfers between devices, cross(): return lax.ppermute(array, 'dim', [(0, 1), (1, 0)])  1.03 us
    pallas_call x1, Pallas kernels, pick(): pl.pallas_call(functools.partial(pick_kernel, len(pieces), wide), out_sha...  0.78 us
  transfers between devices with their start and end apart: 13, of which 5 were waited for; matrix products, arithmetic and copies ran while one was open for 0% of the time, Pallas kernels for 0%

profile of v7, /device:TPU:0, one launch (start us, length us, event | category | flops | bytes accessed | tf_op | source)
XLA Modules:
  0.0 22.9 jit_solution(588723467974349373)
XLA Ops:
  0.0 0.0 copy-start
  0.0 0.5 %collective-permute-start.4 = (bf16[32,64,128]{2,1,0:T(8,128)(2,1)}, bf16[32,64,128]{2,1,0:T(8,128)(2,1)S(1)}, u32[]{:S(2)}, u32[]{:S(2)}) collective-permute-start(bf16[32,64,128]{2,1,0:T(8,128)(2,1)} %refs_5_.1), channel_id=1, source_target_pairs={{0,1},{1,0},{2,3},{3,2},{4,5},{5,4},{6,7},{7,6},{8,9},{9,8},{10,11... | collective-permute-start | bytes 1572872 | tf_op jit(solution)/shard_map/ppermute | solution.py:146
  0.5 4.7 %collective-permute-start = (bf16[2,32,128]{2,1,0:T(8,128)(2,1)}, bf16[2,32,128]{2,1,0:T(8,128)(2,1)S(1)}, u32[]{:S(2)}, u32[]{:S(2)}) collective-permute-start(bf16[2,32,128]{2,1,0:T(8,128)(2,1)} %refs_4_.1), channel_id=1, source_target_pairs={{0,12},{1,15},{2,14},{3,13},{4,8},{5,11},{6,10},{7,9},{8,4},{9,7},... | collective-permute-start | bytes 49160 | tf_op jit(solution)/shard_map/ppermute | solution.py:143
  5.1 0.0 collective-permute-start.1
  5.1 0.6 %collective-permute-start.2 = (bf16[2,32,128]{2,1,0:T(8,128)(2,1)}, bf16[2,32,128]{2,1,0:T(8,128)(2,1)S(1)}, u32[]{:S(2)}, u32[]{:S(2)}) collective-permute-start(bf16[2,32,128]{2,1,0:T(8,128)(2,1)} %refs_4_.1), channel_id=1, source_target_pairs={{0,4},{1,7},{2,6},{3,5},{4,0},{5,3},{6,2},{7,1},{8,12},{9,15},{10,... | collective-permute-start | bytes 49160 | tf_op jit(solution)/shard_map/ppermute | solution.py:143
  5.8 1.6 %collective-permute-start.3 = (bf16[2,32,128]{2,1,0:T(8,128)(2,1)}, bf16[2,32,128]{2,1,0:T(8,128)(2,1)S(1)}, u32[]{:S(2)}, u32[]{:S(2)}) collective-permute-start(bf16[2,32,128]{2,1,0:T(8,128)(2,1)} %refs_4_.1), channel_id=1, source_target_pairs={{0,2},{1,3},{2,0},{3,1},{4,6},{5,7},{6,4},{7,5},{8,10},{9,11},{10,... | collective-permute-start | bytes 49160 | tf_op jit(solution)/shard_map/ppermute | solution.py:143
  7.4 0.0 collective-permute-done.refs_0_
  7.4 2.6 %collective-permute-done.1.refs_1_ = bf16[2,32,128]{2,1,0:T(8,128)(2,1)S(1)} collective-permute-done((bf16[2,32,128]{2,1,0:T(8,128)(2,1)}, bf16[2,32,128]{2,1,0:T(8,128)(2,1)S(1)}, u32[]{:S(2)}, u32[]{:S(2)}) %collective-permute-start.1) | collective-permute-done | bytes 16416 | tf_op jit(solution)/shard_map/ppermute | solution.py:143
  10.0 0.0 collective-permute-done.2.refs_2_
  10.0 0.0 collective-permute-done.3.refs_3_
  10.0 0.0 collective-permute-done.4.refs_6_
  10.1 0.0 copy-done
  10.1 0.0 copy-done.2
  10.1 2.4 %score.1 = (f32[2,32]{1,0:T(2,128)S(1)}, f32[2,32]{1,0:T(2,128)S(1)}, f32[2,32]{1,0:T(2,128)S(1)}, f32[2,32]{1,0:T(2,128)S(1)}) custom-call(s32[1]{0:T(128)} %bitcast.1.me_ref, s32[32]{0:T(128)S(1)} %copy-done.2, bf16[2,32,128]{2,1,0:T(8,128)(2,1)S(1)} %collective-permute-done.refs_0_, bf16[2,32,128]{2,1,0:T(8,128)(2,1)S(1)} %collective-permute-done.1.refs_1_, ...), custom_call_target="tpu_custom_call" | custom-call | tf_op jit(solution)/shard_map/score/pallas_call | solution.py:80
  12.5 3.5 %collective-permute-start.11 = (f32[2,32]{1,0:T(2,128)S(1)}, f32[2,32]{1,0:T(2,128)S(1)}, u32[]{:S(2)}, u32[]{:S(2)}) collective-permute-start(f32[2,32]{1,0:T(2,128)S(1)} %get-tuple-element.12), channel_id=1, source_target_pairs={{0,12},{1,15},{2,14},{3,13},{4,8},{5,11},{6,10},{7,9},{8,4},{9,7},... | collective-permute-start | bytes 776 | tf_op jit(solution)/shard_map/ppermute | solution.py:143
  16.0 0.0 collective-permute-start.9
  16.0 1.0 %collective-permute-start.7 = (f32[2,32]{1,0:T(2,128)S(1)}, f32[2,32]{1,0:T(2,128)S(1)}, u32[]{:S(2)}, u32[]{:S(2)}) collective-permute-start(f32[2,32]{1,0:T(2,128)S(1)} %get-tuple-element.10), channel_id=1, source_target_pairs={{0,4},{1,7},{2,6},{3,5},{4,0},{5,3},{6,2},{7,1},{8,12},{9,15},{10,... | collective-permute-start | bytes 776 | tf_op jit(solution)/shard_map/ppermute | solution.py:143
  17.0 1.5 %collective-permute-start.5 = (f32[2,32]{1,0:T(2,128)S(1)}, f32[2,32]{1,0:T(2,128)S(1)}, u32[]{:S(2)}, u32[]{:S(2)}) collective-permute-start(f32[2,32]{1,0:T(2,128)S(1)} %get-tuple-element.9), channel_id=1, source_target_pairs={{0,2},{1,3},{2,0},{3,1},{4,6},{5,7},{6,4},{7,5},{8,10},{9,11},{10,... | collective-permute-start | bytes 776 | tf_op jit(solution)/shard_map/ppermute | solution.py:143
  18.4 0.0 collective-permute-done.11
  18.5 0.7 %collective-permute-start.12 = (f32[2,32]{1,0:T(2,128)S(1)}, f32[2,32]{1,0:T(2,128)S(1)}, u32[]{:S(2)}, u32[]{:S(2)}) collective-permute-start(f32[2,32]{1,0:T(2,128)S(1)} %broadcast_select_fusion.refs_6_), channel_id=1, source_target_pairs={{0,1},{1,0},{2,3},{3,2},{4,5},{5,4},{6,7},{7,6},{8,9},{9,8},{10,11... | collective-permute-start | bytes 776 | tf_op jit(solution)/shard_map/ppermute | solution.py:146
  19.1 1.3 %collective-permute-done.9 = f32[2,32]{1,0:T(2,128)S(1)} collective-permute-done((f32[2,32]{1,0:T(2,128)S(1)}, f32[2,32]{1,0:T(2,128)S(1)}, u32[]{:S(2)}, u32[]{:S(2)}) %collective-permute-start.9) | collective-permute-done | bytes 288 | tf_op jit(solution)/shard_map/ppermute | solution.py:143
  20.4 0.0 collective-permute-start.10
  20.4 0.0 collective-permute-done.7
  20.4 0.5 %collective-permute-start.8 = (f32[2,32]{1,0:T(2,128)S(1)}, f32[2,32]{1,0:T(2,128)S(1)}, u32[]{:S(2)}, u32[]{:S(2)}) collective-permute-start(f32[2,32]{1,0:T(2,128)S(1)} %broadcast_select_fusion.2.refs_2_), channel_id=1, source_target_pairs={{0,1},{1,0},{2,3},{3,2},{4,5},{5,4},{6,7},{7,6},{8,9},{9,8},{10,11... | collective-permute-start | bytes 776 | tf_op jit(solution)/shard_map/ppermute | solution.py:146
  20.9 0.0 collective-permute-done.5
  21.0 0.1 collective-permute-start.6
  21.1 0.0 collective-permute-done.12.refs_7_
  21.1 0.5 %collective-permute-done.10.refs_5_ = f32[2,32]{1,0:T(2,128)S(1)} collective-permute-done((f32[2,32]{1,0:T(2,128)S(1)}, f32[2,32]{1,0:T(2,128)S(1)}, u32[]{:S(2)}, u32[]{:S(2)}) %collective-permute-start.10) | collective-permute-done | bytes 288 | tf_op jit(solution)/shard_map/ppermute | solution.py:146
  21.6 0.2 collective-permute-done.8.refs_3_
  21.8 0.3 %collective-permute-done.6.refs_1_ = f32[2,32]{1,0:T(2,128)S(1)} collective-permute-done((f32[2,32]{1,0:T(2,128)S(1)}, f32[2,32]{1,0:T(2,128)S(1)}, u32[]{:S(2)}, u32[]{:S(2)}) %collective-permute-start.6) | collective-permute-done | bytes 288 | tf_op jit(solution)/shard_map/ppermute | solution.py:146
  22.1 0.0 copy-done.1
  22.1 0.8 %pick.1 = f32[2,1000]{1,0:T(2,128)} custom-call(s32[1]{0:T(128)} %bitcast.base_ref, s32[2,1000]{1,0:T(2,128)S(1)} %copy-done.1, f32[2,32]{1,0:T(2,128)S(1)} %broadcast_select_fusion.3.refs_0_, f32[2,32]{1,0:T(2,128)S(1)} %collective-permute-done.6.refs_1_, f32[2,32]{1,0:T(2,128)S(1)} %broadcast_select_fusion.2.refs_2_, ...), custom_call_target="tpu_custom_call" | custom-call | tf_op jit(solution)/shard_map/pick/pallas_call | solution.py:124
  (6 shorter events, 0.0 us)
Async XLA Ops:
  0.0 10.1 %copy-start = (bf16[2,32,128]{2,1,0:T(8,128)(2,1)S(1)}, bf16[2,32,128]{2,1,0:T(8,128)(2,1)}, u32[]{:S(2)}) copy-start(bf16[2,32,128]{2,1,0:T(8,128)(2,1)} %refs_4_.1) | copy-start | bytes 49156
  0.0 10.0 %collective-permute-start.4 = (bf16[32,64,128]{2,1,0:T(8,128)(2,1)}, bf16[32,64,128]{2,1,0:T(8,128)(2,1)S(1)}, u32[]{:S(2)}, u32[]{:S(2)}) collective-permute-start(bf16[32,64,128]{2,1,0:T(8,128)(2,1)} %refs_5_.1), channel_id=1, source_target_pairs={{0,1},{1,0},{2,3},{3,2},{4,5},{5,4},{6,7},{7,6},{8,9},{9,8},{10,11... | collective-permute-start | bytes 1572872 | tf_op jit(solution)/shard_map/ppermute | solution.py:146
  0.5 6.9 %collective-permute-start = (bf16[2,32,128]{2,1,0:T(8,128)(2,1)}, bf16[2,32,128]{2,1,0:T(8,128)(2,1)S(1)}, u32[]{:S(2)}, u32[]{:S(2)}) collective-permute-start(bf16[2,32,128]{2,1,0:T(8,128)(2,1)} %refs_4_.1), channel_id=1, source_target_pairs={{0,12},{1,15},{2,14},{3,13},{4,8},{5,11},{6,10},{7,9},{8,4},{9,7},... | collective-permute-start | bytes 49160 | tf_op jit(solution)/shard_map/ppermute | solution.py:143
  5.1 4.9 %collective-permute-start.1 = (bf16[2,32,128]{2,1,0:T(8,128)(2,1)}, bf16[2,32,128]{2,1,0:T(8,128)(2,1)S(1)}, u32[]{:S(2)}, u32[]{:S(2)}) collective-permute-start(bf16[2,32,128]{2,1,0:T(8,128)(2,1)} %refs_4_.1), channel_id=1, source_target_pairs={{0,8},{1,11},{2,10},{3,9},{4,12},{5,15},{6,14},{7,13},{8,0},{9,3},... | collective-permute-start | bytes 49160 | tf_op jit(solution)/shard_map/ppermute | solution.py:143
  5.1 4.9 %collective-permute-start.2 = (bf16[2,32,128]{2,1,0:T(8,128)(2,1)}, bf16[2,32,128]{2,1,0:T(8,128)(2,1)S(1)}, u32[]{:S(2)}, u32[]{:S(2)}) collective-permute-start(bf16[2,32,128]{2,1,0:T(8,128)(2,1)} %refs_4_.1), channel_id=1, source_target_pairs={{0,4},{1,7},{2,6},{3,5},{4,0},{5,3},{6,2},{7,1},{8,12},{9,15},{10,... | collective-permute-start | bytes 49160 | tf_op jit(solution)/shard_map/ppermute | solution.py:143
  5.8 4.3 %collective-permute-start.3 = (bf16[2,32,128]{2,1,0:T(8,128)(2,1)}, bf16[2,32,128]{2,1,0:T(8,128)(2,1)S(1)}, u32[]{:S(2)}, u32[]{:S(2)}) collective-permute-start(bf16[2,32,128]{2,1,0:T(8,128)(2,1)} %refs_4_.1), channel_id=1, source_target_pairs={{0,2},{1,3},{2,0},{3,1},{4,6},{5,7},{6,4},{7,5},{8,10},{9,11},{10,... | collective-permute-start | bytes 49160 | tf_op jit(solution)/shard_map/ppermute | solution.py:143
  7.4 2.7 %copy-start.2 = (s32[32]{0:T(128)S(1)}, s32[32]{0:T(128)}, u32[]{:S(2)}) copy-start(s32[32]{0:T(128)} %lens_ref.1) | copy-start | bytes 388
  12.5 5.9 %collective-permute-start.11 = (f32[2,32]{1,0:T(2,128)S(1)}, f32[2,32]{1,0:T(2,128)S(1)}, u32[]{:S(2)}, u32[]{:S(2)}) collective-permute-start(f32[2,32]{1,0:T(2,128)S(1)} %get-tuple-element.12), channel_id=1, source_target_pairs={{0,12},{1,15},{2,14},{3,13},{4,8},{5,11},{6,10},{7,9},{8,4},{9,7},... | collective-permute-start | bytes 776 | tf_op jit(solution)/shard_map/ppermute | solution.py:143
  16.0 4.5 %collective-permute-start.9 = (f32[2,32]{1,0:T(2,128)S(1)}, f32[2,32]{1,0:T(2,128)S(1)}, u32[]{:S(2)}, u32[]{:S(2)}) collective-permute-start(f32[2,32]{1,0:T(2,128)S(1)} %get-tuple-element.11), channel_id=1, source_target_pairs={{0,8},{1,11},{2,10},{3,9},{4,12},{5,15},{6,14},{7,13},{8,0},{9,3},... | collective-permute-start | bytes 776 | tf_op jit(solution)/shard_map/ppermute | solution.py:143
  16.0 4.5 %collective-permute-start.7 = (f32[2,32]{1,0:T(2,128)S(1)}, f32[2,32]{1,0:T(2,128)S(1)}, u32[]{:S(2)}, u32[]{:S(2)}) collective-permute-start(f32[2,32]{1,0:T(2,128)S(1)} %get-tuple-element.10), channel_id=1, source_target_pairs={{0,4},{1,7},{2,6},{3,5},{4,0},{5,3},{6,2},{7,1},{8,12},{9,15},{10,... | collective-permute-start | bytes 776 | tf_op jit(solution)/shard_map/ppermute | solution.py:143
  17.0 4.0 %collective-permute-start.5 = (f32[2,32]{1,0:T(2,128)S(1)}, f32[2,32]{1,0:T(2,128)S(1)}, u32[]{:S(2)}, u32[]{:S(2)}) collective-permute-start(f32[2,32]{1,0:T(2,128)S(1)} %get-tuple-element.9), channel_id=1, source_target_pairs={{0,2},{1,3},{2,0},{3,1},{4,6},{5,7},{6,4},{7,5},{8,10},{9,11},{10,... | collective-permute-start | bytes 776 | tf_op jit(solution)/shard_map/ppermute | solution.py:143
  18.5 3.6 %copy-start.1 = (s32[2,1000]{1,0:T(2,128)S(1)}, s32[2,1000]{1,0:T(2,128)}, u32[]{:S(2)}) copy-start(s32[2,1000]{1,0:T(2,128)} %cand_ref.1) | copy-start | bytes 24004
  18.5 2.6 %collective-permute-start.12 = (f32[2,32]{1,0:T(2,128)S(1)}, f32[2,32]{1,0:T(2,128)S(1)}, u32[]{:S(2)}, u32[]{:S(2)}) collective-permute-start(f32[2,32]{1,0:T(2,128)S(1)} %broadcast_select_fusion.refs_6_), channel_id=1, source_target_pairs={{0,1},{1,0},{2,3},{3,2},{4,5},{5,4},{6,7},{7,6},{8,9},{9,8},{10,11... | collective-permute-start | bytes 776 | tf_op jit(solution)/shard_map/ppermute | solution.py:146
  20.4 1.1 %collective-permute-start.10 = (f32[2,32]{1,0:T(2,128)S(1)}, f32[2,32]{1,0:T(2,128)S(1)}, u32[]{:S(2)}, u32[]{:S(2)}) collective-permute-start(f32[2,32]{1,0:T(2,128)S(1)} %broadcast_select_fusion.1.refs_4_), channel_id=1, source_target_pairs={{0,1},{1,0},{2,3},{3,2},{4,5},{5,4},{6,7},{7,6},{8,9},{9,8},{10,11... | collective-permute-start | bytes 776 | tf_op jit(solution)/shard_map/ppermute | solution.py:146
  20.4 1.3 %collective-permute-start.8 = (f32[2,32]{1,0:T(2,128)S(1)}, f32[2,32]{1,0:T(2,128)S(1)}, u32[]{:S(2)}, u32[]{:S(2)}) collective-permute-start(f32[2,32]{1,0:T(2,128)S(1)} %broadcast_select_fusion.2.refs_2_), channel_id=1, source_target_pairs={{0,1},{1,0},{2,3},{3,2},{4,5},{5,4},{6,7},{7,6},{8,9},{9,8},{10,11... | collective-permute-start | bytes 776 | tf_op jit(solution)/shard_map/ppermute | solution.py:146
  21.0 1.1 %collective-permute-start.6 = (f32[2,32]{1,0:T(2,128)S(1)}, f32[2,32]{1,0:T(2,128)S(1)}, u32[]{:S(2)}, u32[]{:S(2)}) collective-permute-start(f32[2,32]{1,0:T(2,128)S(1)} %broadcast_select_fusion.3.refs_0_), channel_id=1, source_target_pairs={{0,1},{1,0},{2,3},{3,2},{4,5},{5,4},{6,7},{7,6},{8,9},{9,8},{10,11... | collective-permute-start | bytes 776 | tf_op jit(solution)/shard_map/ppermute | solution.py:146

commit v8 on v7

v8 whole, which is shorter than its diff:
```python
import functools

import jax
import jax.numpy as jnp
from jax import lax
from jax.experimental import pallas as pl
from jax.experimental.pallas import tpu as pltpu
from jax.sharding import PartitionSpec as P

INDEX_AXES = ("shard", "qgrp")
ALL_AXES = ("shard", "qgrp", "dim")
LANES = 128
BLOCK = 256


def stage_kernel(core_ref, lens_ref, own_ref, other_ref, own_out, other_out, held_ref, sem):
    core = core_ref[0]
    count, half, width = own_ref.shape
    fetch = pltpu.make_async_copy(own_ref, held_ref, sem)
    fetch.start()
    fetch.wait()
    rows = lax.broadcasted_iota(jnp.int32, (half, width), 0)
    step = min(count, 4)

    def group(g, _):
        for k in range(step):
            p = g * step + k
            own = held_ref[p].astype(jnp.float32)
            other = other_ref[p].astype(jnp.float32)
            first = jnp.where(core == 0, own[:1], other[:1])
            length = lens_ref[p]
            own_out[p] = jnp.where(rows < length - core * half, own, first).astype(own_out.dtype)
            other_out[p] = jnp.where(rows < length - (1 - core) * half, other, first).astype(own_out.dtype)
        return 0

    lax.fori_loop(0, count // step, group, 0)


def stage(core, doc_lens, doc_tokens, other):
    smem = pl.BlockSpec(memory_space=pltpu.SMEM)
    vmem = pl.BlockSpec(memory_space=pltpu.VMEM)
    hbm = pl.BlockSpec(memory_space=pltpu.HBM)
    doc_tokens = pltpu.with_memory_space_constraint(doc_tokens, pltpu.HBM)
    return pl.pallas_call(
        stage_kernel,
        out_shape=[jax.ShapeDtypeStruct(doc_tokens.shape, doc_tokens.dtype)] * 2,
        in_specs=[smem, smem, hbm, vmem],
        out_specs=[vmem] * 2,
        scratch_shapes=[pltpu.VMEM(doc_tokens.shape, doc_tokens.dtype), pltpu.SemaphoreType.DMA(())],
        compiler_params=pltpu.CompilerParams(vmem_limit_bytes=8 * 1024 * 1024),
        cost_estimate=pl.CostEstimate(flops=4 * doc_tokens.size, bytes_accessed=8 * doc_tokens.size, transcendentals=0),
        name="stage",
    )(core.reshape(1), doc_lens, doc_tokens, other)


def score_kernel(n_pieces, put, *refs):
    piece_refs = refs[:n_pieces]
    own_ref, other_ref = refs[n_pieces: n_pieces + 2]
    out_refs = refs[n_pieces + 2: -3]
    flat_ref, turned_ref, max_ref = refs[-3:]
    q_tokens, width = piece_refs[0].shape[1:]
    count, half, _ = own_ref.shape
    total = flat_ref.shape[0]
    at = 0
    for piece_ref in piece_refs:
        rows = piece_ref.shape[0] * q_tokens
        flat_ref[pl.ds(at, rows), :] = piece_ref[...].reshape(rows, width)
        at += rows
    turned_ref[...] = flat_ref[...].T
    block = min(total, BLOCK)
    step = min(count, 8)

    def group(g, _):
        start = pl.multiple_of(g * step, step)
        for at in range(0, total, block):
            best = None
            for ref in (own_ref, other_ref):
                docs = ref[pl.ds(start, step)].reshape(step * half, width)
                part = jnp.dot(docs, turned_ref[:, pl.ds(at, block)], preferred_element_type=jnp.float32)
                part = jnp.max(part.reshape(step, half // 8, 8, block), axis=1)
                best = part if best is None else jnp.maximum(best, part)
            max_ref[pl.ds(start, step), pl.ds(at, block)] = jnp.max(best, axis=1)
        return 0

    lax.fori_loop(0, count // step, group, 0, unroll=total <= block)
    put(jnp.sum(max_ref[...].T.reshape(total // q_tokens, q_tokens, count), axis=1), out_refs)


def score(pieces, own, other, put, out_shapes):
    vmem = pl.BlockSpec(memory_space=pltpu.VMEM)
    count = own.shape[0]
    queries = sum(p.shape[0] for p in pieces)
    q_tokens, width = pieces[0].shape[1:]
    return pl.pallas_call(
        functools.partial(score_kernel, len(pieces), put),
        out_shape=[jax.ShapeDtypeStruct(shape, jnp.float32) for shape in out_shapes],
        in_specs=[vmem] * (len(pieces) + 2),
        out_specs=[vmem] * len(out_shapes),
        scratch_shapes=[
            pltpu.VMEM((queries * q_tokens, width), jnp.bfloat16),
            pltpu.VMEM((width, queries * q_tokens), jnp.bfloat16),
            pltpu.VMEM((count, queries * q_tokens), jnp.float32),
        ],
        compiler_params=pltpu.CompilerParams(vmem_limit_bytes=(8 + queries // 10) * 1024 * 1024),
        name="score",
    )(*pieces, own, other)


def pick_kernel(n_pieces, wide, spot_ref, *refs):
    piece_refs, out_ref = refs[:n_pieces], refs[n_pieces]
    parts = [ref[...] for ref in piece_refs]
    parts = [part[:, t: t + wide] for group in zip(*[iter(parts)] * min(2, n_pieces))
             for t in range(0, parts[0].shape[1], wide) for part in group]
    table = jnp.concatenate(parts, axis=1) if len(parts) > 1 else parts[0]
    size = table.shape[1]
    rows, width = spot_ref.shape
    spot = spot_ref[...]
    for at in range(0, width, LANES):
        wide = min(LANES, width - at)
        index = spot[:, at: at + wide]
        if wide < LANES:
            index = jnp.concatenate([index, jnp.zeros((rows, LANES - wide), jnp.int32)], axis=1)
        low = jnp.bitwise_and(index, LANES - 1)
        high = lax.shift_right_logical(index, LANES.bit_length() - 1)
        value = jnp.zeros((rows, LANES), jnp.float32)
        for t in range(0, size, LANES):
            found = jnp.take_along_axis(table[:, t: t + LANES], low, axis=1, mode="promise_in_bounds")
            value = jnp.where(high == t // LANES, found, value)
        out_ref[:, pl.ds(at, wide)] = value[:, :wide]


def pick(spots, pieces, wide):
    vmem = pl.BlockSpec(memory_space=pltpu.VMEM)
    return pl.pallas_call(
        functools.partial(pick_kernel, len(pieces), wide),
        out_shape=jax.ShapeDtypeStruct(spots.shape, jnp.float32),
        in_specs=[vmem] * (1 + len(pieces)),
        out_specs=vmem,
        compiler_params=pltpu.CompilerParams(vmem_limit_bytes=4 * 1024 * 1024),
        name="pick",
    )(spots, *pieces)


def two_columns(queries, doc_tokens, doc_lens, candidates, n_z, core):
    q_owned = queries.shape[0]
    count = doc_tokens.shape[0]

    def exchange(array, dz, dx0, dx1):
        pairs = [
            ((z * 2 + x) * 2 + d, ((z ^ dz) * 2 + (x ^ dx)) * 2 + d)
            for z in range(n_z) for x in range(2) for d, dx in enumerate((dx0, dx1))
        ]
        return lax.ppermute(array, ALL_AXES, pairs)

    def cross(array):
        return lax.ppermute(array, "dim", [(0, 1), (1, 0)])

    other = cross(doc_tokens)
    def from_column(array):
        pairs = []
        for z in range(n_z):
            for x in range(2):
                pairs.append(((z * 2 + x) * 2, (z * 2 + 1 - x) * 2 + 1))
                pairs.append(((z * 2 + x) * 2 + 1, (z * 2 + x) * 2))
        return lax.ppermute(array, ALL_AXES, pairs)

    far_first = list(reversed(range(n_z)))
    pieces = [exchange(queries, dz, 0, 1) for dz in far_first[:-1]] + [from_column(queries)]
    own, other = stage(core, doc_lens, doc_tokens, other)

    def put(scores, out_refs):
        for k, out_ref in enumerate(out_refs):
            out_ref[...] = scores[k * q_owned: (k + 1) * q_owned]

    blocks = score(pieces, own, other, put, [(q_owned, count)] * n_z)
    table = []
    for dz, block in zip(reversed(far_first), reversed(blocks)):
        moved = jnp.where(core == -dz, block, exchange(block, dz, int(dz == 0), 1))
        table += [moved, cross(moved)]
    base = (lax.axis_index("shard") * 2 + (lax.axis_index("qgrp") ^ core)) * count
    return pick(candidates ^ base, table, count)


def any_columns(queries, doc_tokens, doc_lens, candidates, n, cores, core):
    q_owned = candidates.shape[0]
    count = doc_tokens.shape[0]
    gathered = lax.all_gather(queries, INDEX_AXES, axis=0, tiled=True)
    other = lax.ppermute(doc_tokens, "dim", [(s, cores - 1 - s) for s in range(cores)])

    def put(scores, out_refs):
        out_refs[0][...] = scores

    own, other = stage(core, doc_lens, doc_tokens, other)
    block = score([gathered], own, other, put, [(n * q_owned, count)])[0]
    moved = lax.all_to_all(
        block.reshape(n, q_owned, count), INDEX_AXES, split_axis=0, concat_axis=0, tiled=True
    )
    table = moved.transpose(1, 0, 2).reshape(q_owned, n * count)
    return pick(candidates, [table], n * count)


def per_device(queries, doc_tokens, doc_lens, candidates):
    sizes = n_z, n_x, cores = tuple(lax.axis_size(axis) for axis in ALL_AXES)
    count = doc_tokens.shape[0]
    core = lax.axis_index("dim")
    if sizes in ((4, 2, 2), (2, 2, 2)) and count & (count - 1) == 0:
        return two_columns(queries, doc_tokens, doc_lens, candidates, n_z, core)
    return any_columns(queries, doc_tokens, doc_lens, candidates, n_z * n_x, cores, core)


def solution(mesh):
    in_specs = (
        P(("groups",) + INDEX_AXES, None, None),
        P(("groups",) + INDEX_AXES, "dim", None),
        P(("groups",) + INDEX_AXES),
        P(("groups",) + INDEX_AXES, None),
    )
    out_specs = P(("groups",) + INDEX_AXES, None)
    return jax.shard_map(
        per_device, mesh=mesh, in_specs=in_specs, out_specs=out_specs, check_vma=False
    )
```

time: 23 us -> 21.7 us (0.943)
  waiting for transfers between devices: 4.99 us -> 2.61 us
  local copies, waits for them, and re-layouts: 0.01 us -> 0.66 us
  Pallas kernels: 3.2 us -> 3.51 us
    ppermute x8 -> x7, waiting for transfers between devices: 3.96 us -> 1.61 us  [exchange(): return lax.ppermute(array, ALL_AXES, pairs)]
    ppermute x0 -> x1, starting transfers between devices: none -> 1.88 us  [from_column(): return lax.ppermute(array, ALL_AXES, pairs)]
    ppermute x8 -> x7, starting transfers between devices: 12.9 us -> 11.1 us  [exchange(): return lax.ppermute(array, ALL_AXES, pairs)]
    unnamed x6 -> x4, local copies, waits for them, and re-layouts: 0.01 us -> 0.66 us
    pallas_call x1 -> x2, Pallas kernels: 2.42 us -> 2.74 us  [the longest x1 1.87 us: stage(): pl.pallas_call(stage_kernel, out_shape=[jax.ShapeDtypeStruct(doc_tokens.s...]
  transfers between devices with their start and end apart: 13 -> 13, of which waited for: 5 -> 4; matrix products, arithmetic and copies ran while one was open for 0% -> 0% of each run, Pallas kernels for 0% -> 9%
where the time goes in v8:
time: 21.7 us; the launch traced here: 21.5 us
  starting transfers between devices  14.6 us (67%)
  Pallas kernels  3.51 us (16%)
  waiting for transfers between devices  2.61 us (12%)
  local copies, waits for them, and re-layouts  0.66 us (3%)
    ppermute x7, starting transfers between devices, exchange(): return lax.ppermute(array, ALL_AXES, pairs)  11.1 us
    ppermute x1, starting transfers between devices, from_column(): return lax.ppermute(array, ALL_AXES, pairs)  1.88 us
    pallas_call x1, Pallas kernels, stage(): pl.pallas_call(stage_kernel, out_shape=[jax.ShapeDtypeStruct(doc_tokens.s...  1.87 us
    ppermute x5, starting transfers between devices, cross(): return lax.ppermute(array, 'dim', [(0, 1), (1, 0)])  1.68 us
    ppermute x7, waiting for transfers between devices, exchange(): return lax.ppermute(array, ALL_AXES, pairs)  1.61 us
    ppermute x5, waiting for transfers between devices, cross(): return lax.ppermute(array, 'dim', [(0, 1), (1, 0)])  1 us
    pallas_call x1, Pallas kernels, score(): pl.pallas_call(functools.partial(score_kernel, len(pieces), put), out_sha...  0.86 us
    pallas_call x1, Pallas kernels, pick(): pl.pallas_call(functools.partial(pick_kernel, len(pieces), wide), out_sha...  0.78 us
  transfers between devices with their start and end apart: 13, of which 4 were waited for; matrix products, arithmetic and copies ran while one was open for 0% of the time, Pallas kernels for 9%

profile of v8, /device:TPU:0, one launch (start us, length us, event | category | flops | bytes accessed | tf_op | source)
XLA Modules:
  0.0 21.5 jit_solution(5952083553164112746)
XLA Ops:
  0.0 0.5 %collective-permute-start.4 = (bf16[32,64,128]{2,1,0:T(8,128)(2,1)}, bf16[32,64,128]{2,1,0:T(8,128)(2,1)S(1)}, u32[]{:S(2)}, u32[]{:S(2)}) collective-permute-start(bf16[32,64,128]{2,1,0:T(8,128)(2,1)} %own_ref.1), channel_id=1, source_target_pairs={{0,1},{1,0},{2,3},{3,2},{4,5},{5,4},{6,7},{7,6},{8,9},{9,8},{10,11... | collective-permute-start | bytes 1572872 | tf_op jit(solution)/shard_map/ppermute | solution.py:156
  0.5 4.6 %collective-permute-start = (bf16[2,32,128]{2,1,0:T(8,128)(2,1)}, bf16[2,32,128]{2,1,0:T(8,128)(2,1)S(1)}, u32[]{:S(2)}, u32[]{:S(2)}) collective-permute-start(bf16[2,32,128]{2,1,0:T(8,128)(2,1)} %param.4), channel_id=1, source_target_pairs={{0,12},{1,15},{2,14},{3,13},{4,8},{5,11},{6,10},{7,9},{8,4},{9,7},... | collective-permute-start | bytes 49160 | tf_op jit(solution)/shard_map/ppermute | solution.py:153
  5.1 0.0 collective-permute-start.1
  5.1 0.6 %collective-permute-start.2 = (bf16[2,32,128]{2,1,0:T(8,128)(2,1)}, bf16[2,32,128]{2,1,0:T(8,128)(2,1)S(1)}, u32[]{:S(2)}, u32[]{:S(2)}) collective-permute-start(bf16[2,32,128]{2,1,0:T(8,128)(2,1)} %param.4), channel_id=1, source_target_pairs={{0,4},{1,7},{2,6},{3,5},{4,0},{5,3},{6,2},{7,1},{8,12},{9,15},{10,... | collective-permute-start | bytes 49160 | tf_op jit(solution)/shard_map/ppermute | solution.py:153
  5.7 1.9 %collective-permute-start.3 = (bf16[2,32,128]{2,1,0:T(8,128)(2,1)}, bf16[2,32,128]{2,1,0:T(8,128)(2,1)S(1)}, u32[]{:S(2)}, u32[]{:S(2)}) collective-permute-start(bf16[2,32,128]{2,1,0:T(8,128)(2,1)} %param.4), channel_id=1, source_target_pairs={{0,3},{1,0},{2,1},{3,2},{4,7},{5,4},{6,5},{7,6},{8,11},{9,8},{10,9... | collective-permute-start | bytes 49160 | tf_op jit(solution)/shard_map/ppermute | solution.py:165
  7.6 0.0 copy-start
  7.6 0.0 collective-permute-done.4.other_ref
  7.6 0.7 %copy-done = s32[32]{0:T(128)S(1)} copy-done((s32[32]{0:T(128)S(1)}, s32[32]{0:T(128)}, u32[]{:S(2)}) %copy-start) | copy-done | bytes 152
  8.2 1.9 %stage.1 = (bf16[32,64,128]{2,1,0:T(8,128)(2,1)S(1)}, bf16[32,64,128]{2,1,0:T(8,128)(2,1)S(1)}) custom-call(s32[1]{0:T(128)} %bitcast.core_ref, s32[32]{0:T(128)S(1)} %copy-done, bf16[32,64,128]{2,1,0:T(8,128)(2,1)} %own_ref.1, bf16[32,64,128]{2,1,0:T(8,128)(2,1)S(1)} %collective-permute-done.4.other_ref), custom_call_target="tpu_custom_call" | custom-call | flops 1048576 | bytes 2097152 | tf_op jit(solution)/shard_map/stage/pallas_call | solution.py:44
  10.1 0.0 collective-permute-done.refs_0_
  10.1 0.0 collective-permute-done.1.refs_1_
  10.1 0.0 collective-permute-done.2.refs_2_
  10.1 0.0 collective-permute-done.3.refs_3_
  10.1 0.9 %score.1 = (f32[2,32]{1,0:T(2,128)S(1)}, f32[2,32]{1,0:T(2,128)S(1)}, f32[2,32]{1,0:T(2,128)S(1)}, f32[2,32]{1,0:T(2,128)S(1)}) custom-call(bf16[2,32,128]{2,1,0:T(8,128)(2,1)S(1)} %collective-permute-done.refs_0_, bf16[2,32,128]{2,1,0:T(8,128)(2,1)S(1)} %collective-permute-done.1.refs_1_, bf16[2,32,128]{2,1,0:T(8,128)(2,1)S(1)} %collective-permute-done.2.refs_2_, ...), custom_call_target="tpu_custom_call" | custom-call | tf_op jit(solution)/shard_map/score/pallas_call | solution.py:94
  11.0 3.6 %collective-permute-start.11 = (f32[2,32]{1,0:T(2,128)S(1)}, f32[2,32]{1,0:T(2,128)S(1)}, u32[]{:S(2)}, u32[]{:S(2)}) collective-permute-start(f32[2,32]{1,0:T(2,128)S(1)} %get-tuple-element.16), channel_id=1, source_target_pairs={{0,12},{1,15},{2,14},{3,13},{4,8},{5,11},{6,10},{7,9},{8,4},{9,7},... | collective-permute-start | bytes 776 | tf_op jit(solution)/shard_map/ppermute | solution.py:153
  14.6 0.0 collective-permute-start.9
  14.6 0.9 %collective-permute-start.7 = (f32[2,32]{1,0:T(2,128)S(1)}, f32[2,32]{1,0:T(2,128)S(1)}, u32[]{:S(2)}, u32[]{:S(2)}) collective-permute-start(f32[2,32]{1,0:T(2,128)S(1)} %get-tuple-element.14), channel_id=1, source_target_pairs={{0,4},{1,7},{2,6},{3,5},{4,0},{5,3},{6,2},{7,1},{8,12},{9,15},{10,... | collective-permute-start | bytes 776 | tf_op jit(solution)/shard_map/ppermute | solution.py:153
  15.5 1.4 %collective-permute-start.5 = (f32[2,32]{1,0:T(2,128)S(1)}, f32[2,32]{1,0:T(2,128)S(1)}, u32[]{:S(2)}, u32[]{:S(2)}) collective-permute-start(f32[2,32]{1,0:T(2,128)S(1)} %get-tuple-element.13), channel_id=1, source_target_pairs={{0,2},{1,3},{2,0},{3,1},{4,6},{5,7},{6,4},{7,5},{8,10},{9,11},{10,... | collective-permute-start | bytes 776 | tf_op jit(solution)/shard_map/ppermute | solution.py:153
  16.9 0.0 collective-permute-done.11
  16.9 0.6 %collective-permute-start.12 = (f32[2,32]{1,0:T(2,128)S(1)}, f32[2,32]{1,0:T(2,128)S(1)}, u32[]{:S(2)}, u32[]{:S(2)}) collective-permute-start(f32[2,32]{1,0:T(2,128)S(1)} %broadcast_select_fusion.refs_6_), channel_id=1, source_target_pairs={{0,1},{1,0},{2,3},{3,2},{4,5},{5,4},{6,7},{7,6},{8,9},{9,8},{10,11... | collective-permute-start | bytes 776 | tf_op jit(solution)/shard_map/ppermute | solution.py:156
  17.5 1.6 %collective-permute-done.9 = f32[2,32]{1,0:T(2,128)S(1)} collective-permute-done((f32[2,32]{1,0:T(2,128)S(1)}, f32[2,32]{1,0:T(2,128)S(1)}, u32[]{:S(2)}, u32[]{:S(2)}) %collective-permute-start.9) | collective-permute-done | bytes 288 | tf_op jit(solution)/shard_map/ppermute | solution.py:153
  19.1 0.1 collective-permute-start.10
  19.2 0.0 collective-permute-done.7
  19.2 0.4 %collective-permute-start.8 = (f32[2,32]{1,0:T(2,128)S(1)}, f32[2,32]{1,0:T(2,128)S(1)}, u32[]{:S(2)}, u32[]{:S(2)}) collective-permute-start(f32[2,32]{1,0:T(2,128)S(1)} %broadcast_select_fusion.2.refs_2_), channel_id=1, source_target_pairs={{0,1},{1,0},{2,3},{3,2},{4,5},{5,4},{6,7},{7,6},{8,9},{9,8},{10,11... | collective-permute-start | bytes 776 | tf_op jit(solution)/shard_map/ppermute | solution.py:156
  19.6 0.0 collective-permute-done.5
  19.6 0.1 collective-permute-start.6
  19.7 0.0 copy-done.1
  19.7 0.0 collective-permute-done.12.refs_7_
  19.7 0.5 %collective-permute-done.10.refs_5_ = f32[2,32]{1,0:T(2,128)S(1)} collective-permute-done((f32[2,32]{1,0:T(2,128)S(1)}, f32[2,32]{1,0:T(2,128)S(1)}, u32[]{:S(2)}, u32[]{:S(2)}) %collective-permute-start.10) | collective-permute-done | bytes 288 | tf_op jit(solution)/shard_map/ppermute | solution.py:156
  20.2 0.2 collective-permute-done.8.refs_3_
  20.4 0.3 %collective-permute-done.6.refs_1_ = f32[2,32]{1,0:T(2,128)S(1)} collective-permute-done((f32[2,32]{1,0:T(2,128)S(1)}, f32[2,32]{1,0:T(2,128)S(1)}, u32[]{:S(2)}, u32[]{:S(2)}) %collective-permute-start.6) | collective-permute-done | bytes 288 | tf_op jit(solution)/shard_map/ppermute | solution.py:156
  20.7 0.8 %pick.1 = f32[2,1000]{1,0:T(2,128)} custom-call(s32[2,1000]{1,0:T(2,128)S(1)} %broadcast_xor_fusion.spot_ref, f32[2,32]{1,0:T(2,128)S(1)} %broadcast_select_fusion.3.refs_0_, f32[2,32]{1,0:T(2,128)S(1)} %collective-permute-done.6.refs_1_, f32[2,32]{1,0:T(2,128)S(1)} %broadcast_select_fusion.2.refs_2_, f32[2,32]{1,0:T(2,128)S(1)} %collective-permute-done.8.refs_3_, ...), custom_call_target="tpu_custom_call" | custom-call | tf_op jit(solution)/shard_map/pick/pallas_call | solution.py:134
  (6 shorter events, 0.0 us)
Async XLA Ops:
  0.0 7.6 %collective-permute-start.4 = (bf16[32,64,128]{2,1,0:T(8,128)(2,1)}, bf16[32,64,128]{2,1,0:T(8,128)(2,1)S(1)}, u32[]{:S(2)}, u32[]{:S(2)}) collective-permute-start(bf16[32,64,128]{2,1,0:T(8,128)(2,1)} %own_ref.1), channel_id=1, source_target_pairs={{0,1},{1,0},{2,3},{3,2},{4,5},{5,4},{6,7},{7,6},{8,9},{9,8},{10,11... | collective-permute-start | bytes 1572872 | tf_op jit(solution)/shard_map/ppermute | solution.py:156
  0.5 9.6 %collective-permute-start = (bf16[2,32,128]{2,1,0:T(8,128)(2,1)}, bf16[2,32,128]{2,1,0:T(8,128)(2,1)S(1)}, u32[]{:S(2)}, u32[]{:S(2)}) collective-permute-start(bf16[2,32,128]{2,1,0:T(8,128)(2,1)} %param.4), channel_id=1, source_target_pairs={{0,12},{1,15},{2,14},{3,13},{4,8},{5,11},{6,10},{7,9},{8,4},{9,7},... | collective-permute-start | bytes 49160 | tf_op jit(solution)/shard_map/ppermute | solution.py:153
  5.1 5.1 %collective-permute-start.1 = (bf16[2,32,128]{2,1,0:T(8,128)(2,1)}, bf16[2,32,128]{2,1,0:T(8,128)(2,1)S(1)}, u32[]{:S(2)}, u32[]{:S(2)}) collective-permute-start(bf16[2,32,128]{2,1,0:T(8,128)(2,1)} %param.4), channel_id=1, source_target_pairs={{0,8},{1,11},{2,10},{3,9},{4,12},{5,15},{6,14},{7,13},{8,0},{9,3},... | collective-permute-start | bytes 49160 | tf_op jit(solution)/shard_map/ppermute | solution.py:153
  5.1 5.1 %collective-permute-start.2 = (bf16[2,32,128]{2,1,0:T(8,128)(2,1)}, bf16[2,32,128]{2,1,0:T(8,128)(2,1)S(1)}, u32[]{:S(2)}, u32[]{:S(2)}) collective-permute-start(bf16[2,32,128]{2,1,0:T(8,128)(2,1)} %param.4), channel_id=1, source_target_pairs={{0,4},{1,7},{2,6},{3,5},{4,0},{5,3},{6,2},{7,1},{8,12},{9,15},{10,... | collective-permute-start | bytes 49160 | tf_op jit(solution)/shard_map/ppermute | solution.py:153
  5.7 4.4 %collective-permute-start.3 = (bf16[2,32,128]{2,1,0:T(8,128)(2,1)}, bf16[2,32,128]{2,1,0:T(8,128)(2,1)S(1)}, u32[]{:S(2)}, u32[]{:S(2)}) collective-permute-start(bf16[2,32,128]{2,1,0:T(8,128)(2,1)} %param.4), channel_id=1, source_target_pairs={{0,3},{1,0},{2,1},{3,2},{4,7},{5,4},{6,5},{7,6},{8,11},{9,8},{10,9... | collective-permute-start | bytes 49160 | tf_op jit(solution)/shard_map/ppermute | solution.py:165
  7.6 0.7 %copy-start = (s32[32]{0:T(128)S(1)}, s32[32]{0:T(128)}, u32[]{:S(2)}) copy-start(s32[32]{0:T(128)} %lens_ref.1) | copy-start | bytes 388
  11.0 5.9 %collective-permute-start.11 = (f32[2,32]{1,0:T(2,128)S(1)}, f32[2,32]{1,0:T(2,128)S(1)}, u32[]{:S(2)}, u32[]{:S(2)}) collective-permute-start(f32[2,32]{1,0:T(2,128)S(1)} %get-tuple-element.16), channel_id=1, source_target_pairs={{0,12},{1,15},{2,14},{3,13},{4,8},{5,11},{6,10},{7,9},{8,4},{9,7},... | collective-permute-start | bytes 776 | tf_op jit(solution)/shard_map/ppermute | solution.py:153
  14.6 4.5 %collective-permute-start.9 = (f32[2,32]{1,0:T(2,128)S(1)}, f32[2,32]{1,0:T(2,128)S(1)}, u32[]{:S(2)}, u32[]{:S(2)}) collective-permute-start(f32[2,32]{1,0:T(2,128)S(1)} %get-tuple-element.15), channel_id=1, source_target_pairs={{0,8},{1,11},{2,10},{3,9},{4,12},{5,15},{6,14},{7,13},{8,0},{9,3},... | collective-permute-start | bytes 776 | tf_op jit(solution)/shard_map/ppermute | solution.py:153
  14.6 5.1 %copy-start.1 = (s32[2,1000]{1,0:T(2,128)S(1)}, s32[2,1000]{1,0:T(2,128)}, u32[]{:S(2)}) copy-start(s32[2,1000]{1,0:T(2,128)} %param.7) | copy-start | bytes 24004
  14.6 4.6 %collective-permute-start.7 = (f32[2,32]{1,0:T(2,128)S(1)}, f32[2,32]{1,0:T(2,128)S(1)}, u32[]{:S(2)}, u32[]{:S(2)}) collective-permute-start(f32[2,32]{1,0:T(2,128)S(1)} %get-tuple-element.14), channel_id=1, source_target_pairs={{0,4},{1,7},{2,6},{3,5},{4,0},{5,3},{6,2},{7,1},{8,12},{9,15},{10,... | collective-permute-start | bytes 776 | tf_op jit(solution)/shard_map/ppermute | solution.py:153
  15.5 4.1 %collective-permute-start.5 = (f32[2,32]{1,0:T(2,128)S(1)}, f32[2,32]{1,0:T(2,128)S(1)}, u32[]{:S(2)}, u32[]{:S(2)}) collective-permute-start(f32[2,32]{1,0:T(2,128)S(1)} %get-tuple-element.13), channel_id=1, source_target_pairs={{0,2},{1,3},{2,0},{3,1},{4,6},{5,7},{6,4},{7,5},{8,10},{9,11},{10,... | collective-permute-start | bytes 776 | tf_op jit(solution)/shard_map/ppermute | solution.py:153
  16.9 2.8 %collective-permute-start.12 = (f32[2,32]{1,0:T(2,128)S(1)}, f32[2,32]{1,0:T(2,128)S(1)}, u32[]{:S(2)}, u32[]{:S(2)}) collective-permute-start(f32[2,32]{1,0:T(2,128)S(1)} %broadcast_select_fusion.refs_6_), channel_id=1, source_target_pairs={{0,1},{1,0},{2,3},{3,2},{4,5},{5,4},{6,7},{7,6},{8,9},{9,8},{10,11... | collective-permute-start | bytes 776 | tf_op jit(solution)/shard_map/ppermute | solution.py:156
  19.1 1.1 %collective-permute-start.10 = (f32[2,32]{1,0:T(2,128)S(1)}, f32[2,32]{1,0:T(2,128)S(1)}, u32[]{:S(2)}, u32[]{:S(2)}) collective-permute-start(f32[2,32]{1,0:T(2,128)S(1)} %broadcast_select_fusion.1.refs_4_), channel_id=1, source_target_pairs={{0,1},{1,0},{2,3},{3,2},{4,5},{5,4},{6,7},{7,6},{8,9},{9,8},{10,11... | collective-permute-start | bytes 776 | tf_op jit(solution)/shard_map/ppermute | solution.py:156
  19.2 1.2 %collective-permute-start.8 = (f32[2,32]{1,0:T(2,128)S(1)}, f32[2,32]{1,0:T(2,128)S(1)}, u32[]{:S(2)}, u32[]{:S(2)}) collective-permute-start(f32[2,32]{1,0:T(2,128)S(1)} %broadcast_select_fusion.2.refs_2_), channel_id=1, source_target_pairs={{0,1},{1,0},{2,3},{3,2},{4,5},{5,4},{6,7},{7,6},{8,9},{9,8},{10,11... | collective-permute-start | bytes 776 | tf_op jit(solution)/shard_map/ppermute | solution.py:156
  19.6 1.1 %collective-permute-start.6 = (f32[2,32]{1,0:T(2,128)S(1)}, f32[2,32]{1,0:T(2,128)S(1)}, u32[]{:S(2)}, u32[]{:S(2)}) collective-permute-start(f32[2,32]{1,0:T(2,128)S(1)} %broadcast_select_fusion.3.refs_0_), channel_id=1, source_target_pairs={{0,1},{1,0},{2,3},{3,2},{4,5},{5,4},{6,7},{7,6},{8,9},{9,8},{10,11... | collective-permute-start | bytes 776 | tf_op jit(solution)/shard_map/ppermute | solution.py:156

commit v9 on v8

--- a/solution.py
+++ b/solution.py
@@ -13,44 +13,59 @@
 BLOCK = 256
 
 
-def stage_kernel(core_ref, lens_ref, own_ref, other_ref, own_out, other_out, held_ref, sem):
-    core = core_ref[0]
+def stage_kernel(lens_hbm_ref, own_ref, other_ref, own_out, other_out, lens_ref, held_ref, lens_sem, sems):
+    core = lax.axis_index("dim")
     count, half, width = own_ref.shape
-    fetch = pltpu.make_async_copy(own_ref, held_ref, sem)
-    fetch.start()
-    fetch.wait()
-    rows = lax.broadcasted_iota(jnp.int32, (half, width), 0)
-    step = min(count, 4)
-
-    def group(g, _):
-        for k in range(step):
-            p = g * step + k
-            own = held_ref[p].astype(jnp.float32)
-            other = other_ref[p].astype(jnp.float32)
+    chunks = sems.shape[0]
+    size = count // chunks
+    lens_copy = pltpu.make_async_copy(lens_hbm_ref, lens_ref, lens_sem)
+    lens_copy.start()
+    fetches = []
+    for c in range(chunks):
+        part = pl.ds(c * size, size)
+        fetches.append(pltpu.make_async_copy(own_ref.at[part], held_ref.at[part], sems.at[c]))
+        fetches[-1].start()
+    rows = lax.broadcasted_iota(jnp.int32, (half, width), 0).astype(jnp.int16)
+    lens_copy.wait()
+    for c in range(chunks):
+        fetches[c].wait()
+
+        def one(k, _):
+            p = c * size + k
+            own, other = held_ref[p], other_ref[p]
             first = jnp.where(core == 0, own[:1], other[:1])
             length = lens_ref[p]
-            own_out[p] = jnp.where(rows < length - core * half, own, first).astype(own_out.dtype)
-            other_out[p] = jnp.where(rows < length - (1 - core) * half, other, first).astype(own_out.dtype)
-        return 0
-
-    lax.fori_loop(0, count // step, group, 0)
-
-
-def stage(core, doc_lens, doc_tokens, other):
-    smem = pl.BlockSpec(memory_space=pltpu.SMEM)
+            own_valid = rows < (length - core * half).astype(jnp.int16)
+            other_valid = rows < (length - (1 - core) * half).astype(jnp.int16)
+            own_out[p] = jnp.where(own_valid, own, first)
+            other_out[p] = jnp.where(other_valid, other, first)
+            return 0
+
+        lax.fori_loop(0, size, one, 0, unroll=True)
+
+
+def stage(doc_lens, doc_tokens, other):
     vmem = pl.BlockSpec(memory_space=pltpu.VMEM)
     hbm = pl.BlockSpec(memory_space=pltpu.HBM)
     doc_tokens = pltpu.with_memory_space_constraint(doc_tokens, pltpu.HBM)
+    doc_lens = pltpu.with_memory_space_constraint(doc_lens, pltpu.HBM)
+    count = doc_tokens.shape[0]
+    chunks = 4 if count % 4 == 0 else 1
     return pl.pallas_call(
         stage_kernel,
         out_shape=[jax.ShapeDtypeStruct(doc_tokens.shape, doc_tokens.dtype)] * 2,
-        in_specs=[smem, smem, hbm, vmem],
+        in_specs=[hbm, hbm, vmem],
         out_specs=[vmem] * 2,
-        scratch_shapes=[pltpu.VMEM(doc_tokens.shape, doc_tokens.dtype), pltpu.SemaphoreType.DMA(())],
+        scratch_shapes=[
+            pltpu.SMEM(doc_lens.shape, jnp.int32),
+            pltpu.VMEM(doc_tokens.shape, doc_tokens.dtype),
+            pltpu.SemaphoreType.DMA(()),
+            pltpu.SemaphoreType.DMA((chunks,)),
+        ],
         compiler_params=pltpu.CompilerParams(vmem_limit_bytes=8 * 1024 * 1024),
         cost_estimate=pl.CostEstimate(flops=4 * doc_tokens.size, bytes_accessed=8 * doc_tokens.size, transcendentals=0),
         name="stage",
-    )(core.reshape(1), doc_lens, doc_tokens, other)
+    )(doc_lens, doc_tokens, other)
 
 
 def score_kernel(n_pieces, put, *refs):
@@ -106,11 +121,9 @@
     )(*pieces, own, other)
 
 
-def pick_kernel(n_pieces, wide, spot_ref, *refs):
-    piece_refs, out_ref = refs[:n_pieces], refs[n_pieces]
-    parts = [ref[...] for ref in piece_refs]
-    parts = [part[:, t: t + wide] for group in zip(*[iter(parts)] * min(2, n_pieces))
-             for t in range(0, parts[0].shape[1], wide) for part in group]
+def pick_kernel(order, spot_ref, *refs):
+    out_ref = refs[len(order)]
+    parts = [refs[k][...] for k in order]
     table = jnp.concatenate(parts, axis=1) if len(parts) > 1 else parts[0]
     size = table.shape[1]
     rows, width = spot_ref.shape
@@ -129,10 +142,10 @@
         out_ref[:, pl.ds(at, wide)] = value[:, :wide]
 
 
-def pick(spots, pieces, wide):
+def pick(spots, pieces, order):
     vmem = pl.BlockSpec(memory_space=pltpu.VMEM)
     return pl.pallas_call(
-        functools.partial(pick_kernel, len(pieces), wide),
+        functools.partial(pick_kernel, order),
         out_shape=jax.ShapeDtypeStruct(spots.shape, jnp.float32),
         in_specs=[vmem] * (1 + len(pieces)),
         out_specs=vmem,
@@ -141,14 +154,14 @@
     )(spots, *pieces)
 
 
-def two_columns(queries, doc_tokens, doc_lens, candidates, n_z, core):
+def two_columns(queries, doc_tokens, doc_lens, candidates, core):
     q_owned = queries.shape[0]
     count = doc_tokens.shape[0]
 
     def exchange(array, dz, dx0, dx1):
         pairs = [
             ((z * 2 + x) * 2 + d, ((z ^ dz) * 2 + (x ^ dx)) * 2 + d)
-            for z in range(n_z) for x in range(2) for d, dx in enumerate((dx0, dx1))
+            for z in range(4) for x in range(2) for d, dx in enumerate((dx0, dx1))
         ]
         return lax.ppermute(array, ALL_AXES, pairs)
 
@@ -158,27 +171,30 @@
     other = cross(doc_tokens)
     def from_column(array):
         pairs = []
-        for z in range(n_z):
+        for z in range(4):
             for x in range(2):
                 pairs.append(((z * 2 + x) * 2, (z * 2 + 1 - x) * 2 + 1))
                 pairs.append(((z * 2 + x) * 2 + 1, (z * 2 + x) * 2))
         return lax.ppermute(array, ALL_AXES, pairs)
 
-    far_first = list(reversed(range(n_z)))
-    pieces = [exchange(queries, dz, 0, 1) for dz in far_first[:-1]] + [from_column(queries)]
-    own, other = stage(core, doc_lens, doc_tokens, other)
+    steps = (2, 3, 1, 0)
+    pieces = [exchange(queries, dz, 0, 1) if dz else from_column(queries) for dz in steps]
+    own, other = stage(doc_lens, doc_tokens, other)
 
     def put(scores, out_refs):
         for k, out_ref in enumerate(out_refs):
             out_ref[...] = scores[k * q_owned: (k + 1) * q_owned]
 
-    blocks = score(pieces, own, other, put, [(q_owned, count)] * n_z)
+    blocks = score(pieces, own, other, put, [(q_owned, count)] * 4)
+    blocks = dict(zip(steps, blocks))
+    steps = (1, 0, 2, 3)
     table = []
-    for dz, block in zip(reversed(far_first), reversed(blocks)):
-        moved = jnp.where(core == -dz, block, exchange(block, dz, int(dz == 0), 1))
+    for dz in steps:
+        moved = jnp.where(core == -dz, blocks[dz], exchange(blocks[dz], dz, int(dz == 0), 1))
         table += [moved, cross(moved)]
+    order = [2 * steps.index(dz) + side for dz in range(4) for side in range(2)]
     base = (lax.axis_index("shard") * 2 + (lax.axis_index("qgrp") ^ core)) * count
-    return pick(candidates ^ base, table, count)
+    return pick(candidates ^ base, table, order)
 
 
 def any_columns(queries, doc_tokens, doc_lens, candidates, n, cores, core):
@@ -190,21 +206,21 @@
     def put(scores, out_refs):
         out_refs[0][...] = scores
 
-    own, other = stage(core, doc_lens, doc_tokens, other)
+    own, other = stage(doc_lens, doc_tokens, other)
     block = score([gathered], own, other, put, [(n * q_owned, count)])[0]
     moved = lax.all_to_all(
         block.reshape(n, q_owned, count), INDEX_AXES, split_axis=0, concat_axis=0, tiled=True
     )
     table = moved.transpose(1, 0, 2).reshape(q_owned, n * count)
-    return pick(candidates, [table], n * count)
+    return pick(candidates, [table], [0])
 
 
 def per_device(queries, doc_tokens, doc_lens, candidates):
     sizes = n_z, n_x, cores = tuple(lax.axis_size(axis) for axis in ALL_AXES)
     count = doc_tokens.shape[0]
     core = lax.axis_index("dim")
-    if sizes in ((4, 2, 2), (2, 2, 2)) and count & (count - 1) == 0:
-        return two_columns(queries, doc_tokens, doc_lens, candidates, n_z, core)
+    if sizes == (4, 2, 2) and count & (count - 1) == 0:
+        return two_columns(queries, doc_tokens, doc_lens, candidates, core)
     return any_columns(queries, doc_tokens, doc_lens, candidates, n_z * n_x, cores, core)
 
 

time: 21.7 us -> 20.7 us (0.954)
  starting transfers between devices: 14.6 us -> 15.8 us
  waiting for transfers between devices: 2.61 us -> 1.86 us
  Pallas kernels: 3.51 us -> 2.83 us
  local copies, waits for them, and re-layouts: 0.66 us -> 0.01 us
    ppermute x5, starting transfers between devices: 1.68 us -> 2.7 us  [cross(): return lax.ppermute(array, 'dim', [(0, 1), (1, 0)])]
    pallas_call x1, Pallas kernels: 1.87 us -> 1.19 us  [stage(): pl.pallas_call(stage_kernel, out_shape=[jax.ShapeDtypeStruct(doc_tokens.s...]
    unnamed x4 -> x2, local copies, waits for them, and re-layouts: 0.66 us -> 0.01 us
    ppermute x7, waiting for transfers between devices: 1.61 us -> 1.04 us  [exchange(): return lax.ppermute(array, ALL_AXES, pairs)]
  transfers between devices with their start and end apart: 13 -> 13, of which waited for: 4 -> 4; matrix products, arithmetic and copies ran while one was open for 0% -> 0% of each run, Pallas kernels for 9% -> 6%
where the time goes in v9:
time: 20.7 us; the launch traced here: 20.5 us
  starting transfers between devices  15.8 us (76%)
  Pallas kernels  2.83 us (14%)
  waiting for transfers between devices  1.86 us (9%)
    ppermute x7, starting transfers between devices, exchange(): return lax.ppermute(array, ALL_AXES, pairs)  11.1 us
    ppermute x5, starting transfers between devices, cross(): return lax.ppermute(array, 'dim', [(0, 1), (1, 0)])  2.7 us
    ppermute x1, starting transfers between devices, from_column(): return lax.ppermute(array, ALL_AXES, pairs)  1.94 us
    pallas_call x1, Pallas kernels, stage(): pl.pallas_call(stage_kernel, out_shape=[jax.ShapeDtypeStruct(doc_tokens.s...  1.19 us
    ppermute x7, waiting for transfers between devices, exchange(): return lax.ppermute(array, ALL_AXES, pairs)  1.04 us
    pallas_call x1, Pallas kernels, score(): pl.pallas_call(functools.partial(score_kernel, len(pieces), put), out_sha...  0.86 us
    ppermute x5, waiting for transfers between devices, cross(): return lax.ppermute(array, 'dim', [(0, 1), (1, 0)])  0.81 us
    pallas_call x1, Pallas kernels, pick(): pl.pallas_call(functools.partial(pick_kernel, order), out_shape=jax.Shape...  0.78 us
  transfers between devices with their start and end apart: 13, of which 4 were waited for; matrix products, arithmetic and copies ran while one was open for 0% of the time, Pallas kernels for 6%

profile of v9, /device:TPU:0, one launch (start us, length us, event | category | flops | bytes accessed | tf_op | source)
XLA Modules:
  0.0 20.5 jit_solution(16275552525825799154)
XLA Ops:
  0.0 0.5 %collective-permute-start.4 = (bf16[32,64,128]{2,1,0:T(8,128)(2,1)}, bf16[32,64,128]{2,1,0:T(8,128)(2,1)S(1)}, u32[]{:S(2)}, u32[]{:S(2)}) collective-permute-start(bf16[32,64,128]{2,1,0:T(8,128)(2,1)} %own_ref.1), channel_id=1, source_target_pairs={{0,1},{1,0},{2,3},{3,2},{4,5},{5,4},{6,7},{7,6},{8,9},{9,8},{10,11... | collective-permute-start | bytes 1572872 | tf_op jit(solution)/shard_map/ppermute | solution.py:169
  0.5 3.6 %collective-permute-start = (bf16[2,32,128]{2,1,0:T(8,128)(2,1)}, bf16[2,32,128]{2,1,0:T(8,128)(2,1)S(1)}, u32[]{:S(2)}, u32[]{:S(2)}) collective-permute-start(bf16[2,32,128]{2,1,0:T(8,128)(2,1)} %param.4), channel_id=1, source_target_pairs={{0,8},{1,11},{2,10},{3,9},{4,12},{5,15},{6,14},{7,13},{8,0},{9,3},... | collective-permute-start | bytes 49160 | tf_op jit(solution)/shard_map/ppermute | solution.py:166
  4.0 1.3 %collective-permute-start.1 = (bf16[2,32,128]{2,1,0:T(8,128)(2,1)}, bf16[2,32,128]{2,1,0:T(8,128)(2,1)S(1)}, u32[]{:S(2)}, u32[]{:S(2)}) collective-permute-start(bf16[2,32,128]{2,1,0:T(8,128)(2,1)} %param.4), channel_id=1, source_target_pairs={{0,12},{1,15},{2,14},{3,13},{4,8},{5,11},{6,10},{7,9},{8,4},{9,7},... | collective-permute-start | bytes 49160 | tf_op jit(solution)/shard_map/ppermute | solution.py:166
  5.4 0.2 %collective-permute-start.2 = (bf16[2,32,128]{2,1,0:T(8,128)(2,1)}, bf16[2,32,128]{2,1,0:T(8,128)(2,1)S(1)}, u32[]{:S(2)}, u32[]{:S(2)}) collective-permute-start(bf16[2,32,128]{2,1,0:T(8,128)(2,1)} %param.4), channel_id=1, source_target_pairs={{0,4},{1,7},{2,6},{3,5},{4,0},{5,3},{6,2},{7,1},{8,12},{9,15},{10,... | collective-permute-start | bytes 49160 | tf_op jit(solution)/shard_map/ppermute | solution.py:166
  5.6 1.9 %collective-permute-start.3 = (bf16[2,32,128]{2,1,0:T(8,128)(2,1)}, bf16[2,32,128]{2,1,0:T(8,128)(2,1)S(1)}, u32[]{:S(2)}, u32[]{:S(2)}) collective-permute-start(bf16[2,32,128]{2,1,0:T(8,128)(2,1)} %param.4), channel_id=1, source_target_pairs={{0,3},{1,0},{2,1},{3,2},{4,7},{5,4},{6,5},{7,6},{8,11},{9,8},{10,9... | collective-permute-start | bytes 49160 | tf_op jit(solution)/shard_map/ppermute | solution.py:178
  7.6 0.0 collective-permute-done.4.other_ref
  7.6 1.2 %stage.1 = (bf16[32,64,128]{2,1,0:T(8,128)(2,1)S(1)}, bf16[32,64,128]{2,1,0:T(8,128)(2,1)S(1)}) custom-call(s32[32]{0:T(128)} %lens_hbm_ref.1, bf16[32,64,128]{2,1,0:T(8,128)(2,1)} %own_ref.1, bf16[32,64,128]{2,1,0:T(8,128)(2,1)S(1)} %collective-permute-done.4.other_ref), custom_call_target="tpu_custom_call" | custom-call | flops 1048576 | bytes 2097152 | tf_op jit(solution)/shard_map/stage/pallas_call | solution.py:54
  8.8 0.0 collective-permute-done.refs_0_
  8.8 1.0 %collective-permute-done.1.refs_1_ = bf16[2,32,128]{2,1,0:T(8,128)(2,1)S(1)} collective-permute-done((bf16[2,32,128]{2,1,0:T(8,128)(2,1)}, bf16[2,32,128]{2,1,0:T(8,128)(2,1)S(1)}, u32[]{:S(2)}, u32[]{:S(2)}) %collective-permute-start.1) | collective-permute-done | bytes 16416 | tf_op jit(solution)/shard_map/ppermute | solution.py:166
  9.8 0.0 collective-permute-done.2.refs_2_
  9.8 0.0 collective-permute-done.3.refs_3_
  9.8 0.9 %score.1 = (f32[2,32]{1,0:T(2,128)S(1)}, f32[2,32]{1,0:T(2,128)S(1)}, f32[2,32]{1,0:T(2,128)S(1)}, f32[2,32]{1,0:T(2,128)S(1)}) custom-call(bf16[2,32,128]{2,1,0:T(8,128)(2,1)S(1)} %collective-permute-done.refs_0_, bf16[2,32,128]{2,1,0:T(8,128)(2,1)S(1)} %collective-permute-done.1.refs_1_, bf16[2,32,128]{2,1,0:T(8,128)(2,1)S(1)} %collective-permute-done.2.refs_2_, ...), custom_call_target="tpu_custom_call" | custom-call | tf_op jit(solution)/shard_map/score/pallas_call | solution.py:109
  10.7 2.1 %collective-permute-start.11 = (f32[2,32]{1,0:T(2,128)S(1)}, f32[2,32]{1,0:T(2,128)S(1)}, u32[]{:S(2)}, u32[]{:S(2)}) collective-permute-start(f32[2,32]{1,0:T(2,128)S(1)} %get-tuple-element.16), channel_id=1, source_target_pairs={{0,12},{1,15},{2,14},{3,13},{4,8},{5,11},{6,10},{7,9},{8,4},{9,7},... | collective-permute-start | bytes 776 | tf_op jit(solution)/shard_map/ppermute | solution.py:166
  12.8 0.3 %collective-permute-start.9 = (f32[2,32]{1,0:T(2,128)S(1)}, f32[2,32]{1,0:T(2,128)S(1)}, u32[]{:S(2)}, u32[]{:S(2)}) collective-permute-start(f32[2,32]{1,0:T(2,128)S(1)} %get-tuple-element.15), channel_id=1, source_target_pairs={{0,8},{1,11},{2,10},{3,9},{4,12},{5,15},{6,14},{7,13},{8,0},{9,3},... | collective-permute-start | bytes 776 | tf_op jit(solution)/shard_map/ppermute | solution.py:166
  13.1 0.0 copy-start
  13.1 1.5 %collective-permute-start.7 = (f32[2,32]{1,0:T(2,128)S(1)}, f32[2,32]{1,0:T(2,128)S(1)}, u32[]{:S(2)}, u32[]{:S(2)}) collective-permute-start(f32[2,32]{1,0:T(2,128)S(1)} %get-tuple-element.14), channel_id=1, source_target_pairs={{0,2},{1,3},{2,0},{3,1},{4,6},{5,7},{6,4},{7,5},{8,10},{9,11},{10,... | collective-permute-start | bytes 776 | tf_op jit(solution)/shard_map/ppermute | solution.py:166
  14.6 2.0 %collective-permute-start.5 = (f32[2,32]{1,0:T(2,128)S(1)}, f32[2,32]{1,0:T(2,128)S(1)}, u32[]{:S(2)}, u32[]{:S(2)}) collective-permute-start(f32[2,32]{1,0:T(2,128)S(1)} %get-tuple-element.13), channel_id=1, source_target_pairs={{0,4},{1,7},{2,6},{3,5},{4,0},{5,3},{6,2},{7,1},{8,12},{9,15},{10,... | collective-permute-start | bytes 776 | tf_op jit(solution)/shard_map/ppermute | solution.py:166
  16.6 0.0 collective-permute-done.11
  16.6 0.7 %collective-permute-start.12 = (f32[2,32]{1,0:T(2,128)S(1)}, f32[2,32]{1,0:T(2,128)S(1)}, u32[]{:S(2)}, u32[]{:S(2)}) collective-permute-start(f32[2,32]{1,0:T(2,128)S(1)} %broadcast_select_fusion.refs_6_), channel_id=1, source_target_pairs={{0,1},{1,0},{2,3},{3,2},{4,5},{5,4},{6,7},{7,6},{8,9},{9,8},{10,11... | collective-permute-start | bytes 776 | tf_op jit(solution)/shard_map/ppermute | solution.py:169
  17.3 0.0 collective-permute-done.9
  17.3 1.1 %collective-permute-start.10 = (f32[2,32]{1,0:T(2,128)S(1)}, f32[2,32]{1,0:T(2,128)S(1)}, u32[]{:S(2)}, u32[]{:S(2)}) collective-permute-start(f32[2,32]{1,0:T(2,128)S(1)} %broadcast_select_fusion.1.refs_4_), channel_id=1, source_target_pairs={{0,1},{1,0},{2,3},{3,2},{4,5},{5,4},{6,7},{7,6},{8,9},{9,8},{10,11... | collective-permute-start | bytes 776 | tf_op jit(solution)/shard_map/ppermute | solution.py:169
  18.4 0.0 collective-permute-done.7
  18.4 0.1 collective-permute-start.8
  18.5 0.0 collective-permute-done.5
  18.5 0.4 %collective-permute-start.6 = (f32[2,32]{1,0:T(2,128)S(1)}, f32[2,32]{1,0:T(2,128)S(1)}, u32[]{:S(2)}, u32[]{:S(2)}) collective-permute-start(f32[2,32]{1,0:T(2,128)S(1)} %broadcast_select_fusion.3.refs_0_), channel_id=1, source_target_pairs={{0,1},{1,0},{2,3},{3,2},{4,5},{5,4},{6,7},{7,6},{8,9},{9,8},{10,11... | collective-permute-start | bytes 776 | tf_op jit(solution)/shard_map/ppermute | solution.py:169
  18.9 0.0 copy-done
  18.9 0.0 collective-permute-done.12.refs_7_
  18.9 0.3 %collective-permute-done.10.refs_5_ = f32[2,32]{1,0:T(2,128)S(1)} collective-permute-done((f32[2,32]{1,0:T(2,128)S(1)}, f32[2,32]{1,0:T(2,128)S(1)}, u32[]{:S(2)}, u32[]{:S(2)}) %collective-permute-start.10) | collective-permute-done | bytes 288 | tf_op jit(solution)/shard_map/ppermute | solution.py:169
  19.2 0.3 %collective-permute-done.8.refs_3_ = f32[2,32]{1,0:T(2,128)S(1)} collective-permute-done((f32[2,32]{1,0:T(2,128)S(1)}, f32[2,32]{1,0:T(2,128)S(1)}, u32[]{:S(2)}, u32[]{:S(2)}) %collective-permute-start.8) | collective-permute-done | bytes 288 | tf_op jit(solution)/shard_map/ppermute | solution.py:169
  19.5 0.2 collective-permute-done.6.refs_1_
  19.7 0.8 %pick.1 = f32[2,1000]{1,0:T(2,128)} custom-call(s32[2,1000]{1,0:T(2,128)S(1)} %broadcast_xor_fusion.spot_ref, f32[2,32]{1,0:T(2,128)S(1)} %broadcast_select_fusion.3.refs_0_, f32[2,32]{1,0:T(2,128)S(1)} %collective-permute-done.6.refs_1_, f32[2,32]{1,0:T(2,128)S(1)} %broadcast_select_fusion.2.refs_2_, f32[2,32]{1,0:T(2,128)S(1)} %collective-permute-done.8.refs_3_, ...), custom_call_target="tpu_custom_call" | custom-call | tf_op jit(solution)/shard_map/pick/pallas_call | solution.py:147
  (5 shorter events, 0.0 us)
Async XLA Ops:
  0.0 7.6 %collective-permute-start.4 = (bf16[32,64,128]{2,1,0:T(8,128)(2,1)}, bf16[32,64,128]{2,1,0:T(8,128)(2,1)S(1)}, u32[]{:S(2)}, u32[]{:S(2)}) collective-permute-start(bf16[32,64,128]{2,1,0:T(8,128)(2,1)} %own_ref.1), channel_id=1, source_target_pairs={{0,1},{1,0},{2,3},{3,2},{4,5},{5,4},{6,7},{7,6},{8,9},{9,8},{10,11... | collective-permute-start | bytes 1572872 | tf_op jit(solution)/shard_map/ppermute | solution.py:169
  0.5 8.3 %collective-permute-start = (bf16[2,32,128]{2,1,0:T(8,128)(2,1)}, bf16[2,32,128]{2,1,0:T(8,128)(2,1)S(1)}, u32[]{:S(2)}, u32[]{:S(2)}) collective-permute-start(bf16[2,32,128]{2,1,0:T(8,128)(2,1)} %param.4), channel_id=1, source_target_pairs={{0,8},{1,11},{2,10},{3,9},{4,12},{5,15},{6,14},{7,13},{8,0},{9,3},... | collective-permute-start | bytes 49160 | tf_op jit(solution)/shard_map/ppermute | solution.py:166
  4.0 5.8 %collective-permute-start.1 = (bf16[2,32,128]{2,1,0:T(8,128)(2,1)}, bf16[2,32,128]{2,1,0:T(8,128)(2,1)S(1)}, u32[]{:S(2)}, u32[]{:S(2)}) collective-permute-start(bf16[2,32,128]{2,1,0:T(8,128)(2,1)} %param.4), channel_id=1, source_target_pairs={{0,12},{1,15},{2,14},{3,13},{4,8},{5,11},{6,10},{7,9},{8,4},{9,7},... | collective-permute-start | bytes 49160 | tf_op jit(solution)/shard_map/ppermute | solution.py:166
  5.4 4.4 %collective-permute-start.2 = (bf16[2,32,128]{2,1,0:T(8,128)(2,1)}, bf16[2,32,128]{2,1,0:T(8,128)(2,1)S(1)}, u32[]{:S(2)}, u32[]{:S(2)}) collective-permute-start(bf16[2,32,128]{2,1,0:T(8,128)(2,1)} %param.4), channel_id=1, source_target_pairs={{0,4},{1,7},{2,6},{3,5},{4,0},{5,3},{6,2},{7,1},{8,12},{9,15},{10,... | collective-permute-start | bytes 49160 | tf_op jit(solution)/shard_map/ppermute | solution.py:166
  5.6 4.2 %collective-permute-start.3 = (bf16[2,32,128]{2,1,0:T(8,128)(2,1)}, bf16[2,32,128]{2,1,0:T(8,128)(2,1)S(1)}, u32[]{:S(2)}, u32[]{:S(2)}) collective-permute-start(bf16[2,32,128]{2,1,0:T(8,128)(2,1)} %param.4), channel_id=1, source_target_pairs={{0,3},{1,0},{2,1},{3,2},{4,7},{5,4},{6,5},{7,6},{8,11},{9,8},{10,9... | collective-permute-start | bytes 49160 | tf_op jit(solution)/shard_map/ppermute | solution.py:178
  10.7 6.0 %collective-permute-start.11 = (f32[2,32]{1,0:T(2,128)S(1)}, f32[2,32]{1,0:T(2,128)S(1)}, u32[]{:S(2)}, u32[]{:S(2)}) collective-permute-start(f32[2,32]{1,0:T(2,128)S(1)} %get-tuple-element.16), channel_id=1, source_target_pairs={{0,12},{1,15},{2,14},{3,13},{4,8},{5,11},{6,10},{7,9},{8,4},{9,7},... | collective-permute-start | bytes 776 | tf_op jit(solution)/shard_map/ppermute | solution.py:166
  12.8 4.5 %collective-permute-start.9 = (f32[2,32]{1,0:T(2,128)S(1)}, f32[2,32]{1,0:T(2,128)S(1)}, u32[]{:S(2)}, u32[]{:S(2)}) collective-permute-start(f32[2,32]{1,0:T(2,128)S(1)} %get-tuple-element.15), channel_id=1, source_target_pairs={{0,8},{1,11},{2,10},{3,9},{4,12},{5,15},{6,14},{7,13},{8,0},{9,3},... | collective-permute-start | bytes 776 | tf_op jit(solution)/shard_map/ppermute | solution.py:166
  13.1 5.8 %copy-start = (s32[2,1000]{1,0:T(2,128)S(1)}, s32[2,1000]{1,0:T(2,128)}, u32[]{:S(2)}) copy-start(s32[2,1000]{1,0:T(2,128)} %param.7) | copy-start | bytes 24004
  13.1 5.3 %collective-permute-start.7 = (f32[2,32]{1,0:T(2,128)S(1)}, f32[2,32]{1,0:T(2,128)S(1)}, u32[]{:S(2)}, u32[]{:S(2)}) collective-permute-start(f32[2,32]{1,0:T(2,128)S(1)} %get-tuple-element.14), channel_id=1, source_target_pairs={{0,2},{1,3},{2,0},{3,1},{4,6},{5,7},{6,4},{7,5},{8,10},{9,11},{10,... | collective-permute-start | bytes 776 | tf_op jit(solution)/shard_map/ppermute | solution.py:166
  14.6 3.9 %collective-permute-start.5 = (f32[2,32]{1,0:T(2,128)S(1)}, f32[2,32]{1,0:T(2,128)S(1)}, u32[]{:S(2)}, u32[]{:S(2)}) collective-permute-start(f32[2,32]{1,0:T(2,128)S(1)} %get-tuple-element.13), channel_id=1, source_target_pairs={{0,4},{1,7},{2,6},{3,5},{4,0},{5,3},{6,2},{7,1},{8,12},{9,15},{10,... | collective-permute-start | bytes 776 | tf_op jit(solution)/shard_map/ppermute | solution.py:166
  16.6 2.3 %collective-permute-start.12 = (f32[2,32]{1,0:T(2,128)S(1)}, f32[2,32]{1,0:T(2,128)S(1)}, u32[]{:S(2)}, u32[]{:S(2)}) collective-permute-start(f32[2,32]{1,0:T(2,128)S(1)} %broadcast_select_fusion.refs_6_), channel_id=1, source_target_pairs={{0,1},{1,0},{2,3},{3,2},{4,5},{5,4},{6,7},{7,6},{8,9},{9,8},{10,11... | collective-permute-start | bytes 776 | tf_op jit(solution)/shard_map/ppermute | solution.py:169
  17.3 1.9 %collective-permute-start.10 = (f32[2,32]{1,0:T(2,128)S(1)}, f32[2,32]{1,0:T(2,128)S(1)}, u32[]{:S(2)}, u32[]{:S(2)}) collective-permute-start(f32[2,32]{1,0:T(2,128)S(1)} %broadcast_select_fusion.1.refs_4_), channel_id=1, source_target_pairs={{0,1},{1,0},{2,3},{3,2},{4,5},{5,4},{6,7},{7,6},{8,9},{9,8},{10,11... | collective-permute-start | bytes 776 | tf_op jit(solution)/shard_map/ppermute | solution.py:169
  18.4 1.1 %collective-permute-start.8 = (f32[2,32]{1,0:T(2,128)S(1)}, f32[2,32]{1,0:T(2,128)S(1)}, u32[]{:S(2)}, u32[]{:S(2)}) collective-permute-start(f32[2,32]{1,0:T(2,128)S(1)} %broadcast_select_fusion.2.refs_2_), channel_id=1, source_target_pairs={{0,1},{1,0},{2,3},{3,2},{4,5},{5,4},{6,7},{7,6},{8,9},{9,8},{10,11... | collective-permute-start | bytes 776 | tf_op jit(solution)/shard_map/ppermute | solution.py:169
  18.5 1.3 %collective-permute-start.6 = (f32[2,32]{1,0:T(2,128)S(1)}, f32[2,32]{1,0:T(2,128)S(1)}, u32[]{:S(2)}, u32[]{:S(2)}) collective-permute-start(f32[2,32]{1,0:T(2,128)S(1)} %broadcast_select_fusion.3.refs_0_), channel_id=1, source_target_pairs={{0,1},{1,0},{2,3},{3,2},{4,5},{5,4},{6,7},{7,6},{8,9},{9,8},{10,11... | collective-permute-start | bytes 776 | tf_op jit(solution)/shard_map/ppermute | solution.py:169

commit v10 on v9

--- a/solution.py
+++ b/solution.py
@@ -11,6 +11,8 @@
 ALL_AXES = ("shard", "qgrp", "dim")
 LANES = 128
 BLOCK = 256
+ISSUE = (0, 1, 2, 3)
+OPERANDS = (4, 5, 6, 7, 0, 1, 2, 3)
 
 
 def stage_kernel(lens_hbm_ref, own_ref, other_ref, own_out, other_out, lens_ref, held_ref, lens_sem, sems):
@@ -154,47 +156,55 @@
     )(spots, *pieces)
 
 
-def two_columns(queries, doc_tokens, doc_lens, candidates, core):
+QUERY_STEPS = (((0, 1), (3, 0), 1), ((2, 1), (3, 1), 1), ((2, 0), (1, 1), 1), (None, (1, 0), 1))
+SCORE_STEPS = (((2, 1), (3, 1), 0), ((2, 0), (3, 0), 1), ((0, 1), (1, 1), 0), (None, (1, 0), 1))
+
+
+def move(array, steps, owner_sends):
+    pairs = []
+    for z in range(4):
+        for x in range(2):
+            for core in range(2):
+                dz, dx = steps[core] or (0, 0)
+                here = (z * 2 + x) * 2 + core
+                owner = ((z ^ dz) * 2 + (x ^ dx)) * 2 + (core ^ steps[2])
+                pairs.append((owner, here) if owner_sends else (here, owner))
+    return lax.ppermute(array, ALL_AXES, pairs)
+
+
+def four_by_two(queries, doc_tokens, doc_lens, candidates, core):
     q_owned = queries.shape[0]
     count = doc_tokens.shape[0]
-
-    def exchange(array, dz, dx0, dx1):
-        pairs = [
-            ((z * 2 + x) * 2 + d, ((z ^ dz) * 2 + (x ^ dx)) * 2 + d)
-            for z in range(4) for x in range(2) for d, dx in enumerate((dx0, dx1))
-        ]
-        return lax.ppermute(array, ALL_AXES, pairs)
 
     def cross(array):
         return lax.ppermute(array, "dim", [(0, 1), (1, 0)])
 
     other = cross(doc_tokens)
-    def from_column(array):
-        pairs = []
-        for z in range(4):
-            for x in range(2):
-                pairs.append(((z * 2 + x) * 2, (z * 2 + 1 - x) * 2 + 1))
-                pairs.append(((z * 2 + x) * 2 + 1, (z * 2 + x) * 2))
-        return lax.ppermute(array, ALL_AXES, pairs)
-
-    steps = (2, 3, 1, 0)
-    pieces = [exchange(queries, dz, 0, 1) if dz else from_column(queries) for dz in steps]
+    pieces = [move(queries, steps, True) for steps in QUERY_STEPS]
     own, other = stage(doc_lens, doc_tokens, other)
+    origin = [[[q[c] for q in QUERY_STEPS].index(steps[c]) for c in range(2)] for steps in SCORE_STEPS]
 
     def put(scores, out_refs):
-        for k, out_ref in enumerate(out_refs):
-            out_ref[...] = scores[k * q_owned: (k + 1) * q_owned]
+        core = lax.axis_index("dim")
+        block = [scores[k * q_owned: (k + 1) * q_owned] for k in range(4)]
+        for (k0, k1), out_ref in zip(origin, out_refs):
+            out_ref[...] = block[k0] if k0 == k1 else jnp.where(core == 0, block[k0], block[k1])
 
     blocks = score(pieces, own, other, put, [(q_owned, count)] * 4)
-    blocks = dict(zip(steps, blocks))
-    steps = (1, 0, 2, 3)
-    table = []
-    for dz in steps:
-        moved = jnp.where(core == -dz, blocks[dz], exchange(blocks[dz], dz, int(dz == 0), 1))
-        table += [moved, cross(moved)]
-    order = [2 * steps.index(dz) + side for dz in range(4) for side in range(2)]
-    base = (lax.axis_index("shard") * 2 + (lax.axis_index("qgrp") ^ core)) * count
-    return pick(candidates ^ base, table, order)
+    table = [None] * 8
+    for k in ISSUE:
+        moved = move(blocks[k], SCORE_STEPS[k], False)
+        table[2 * k: 2 * k + 2] = [moved, cross(moved)]
+    groups = 0
+    for k, steps in enumerate(SCORE_STEPS):
+        for c in range(2):
+            dz, dx = steps[c] or (0, 0)
+            groups |= (2 * k + (c ^ steps[2])) << (3 * (2 * dz + dx))
+    chip = lax.axis_index("shard") * 2 + lax.axis_index("qgrp")
+    step = lax.shift_right_logical(candidates, count.bit_length() - 1) ^ chip
+    group = (lax.shift_right_logical(jnp.full_like(step, groups), 3 * step) & 7) ^ core
+    spots = group * count + (candidates & (count - 1))
+    return pick(spots, [table[k] for k in OPERANDS], [OPERANDS.index(k) for k in range(8)])
 
 
 def any_columns(queries, doc_tokens, doc_lens, candidates, n, cores, core):
@@ -220,7 +230,7 @@
     count = doc_tokens.shape[0]
     core = lax.axis_index("dim")
     if sizes == (4, 2, 2) and count & (count - 1) == 0:
-        return two_columns(queries, doc_tokens, doc_lens, candidates, core)
+        return four_by_two(queries, doc_tokens, doc_lens, candidates, core)
     return any_columns(queries, doc_tokens, doc_lens, candidates, n_z * n_x, cores, core)
 
 

time: 20.7 us -> 19.9 us (0.961)
  starting transfers between devices: 15.8 us -> 12 us
  waiting for transfers between devices: 1.86 us -> 4.87 us
    ppermute x8, waiting for transfers between devices: 1.05 us -> 4.05 us  [move(): return lax.ppermute(array, ALL_AXES, pairs)]
    ppermute x8, starting transfers between devices: 13.1 us -> 10.4 us  [move(): return lax.ppermute(array, ALL_AXES, pairs)]
    ppermute x5, starting transfers between devices: 2.7 us -> 1.53 us  [cross(): return lax.ppermute(array, 'dim', [(0, 1), (1, 0)])]
  transfers between devices with their start and end apart: 13 -> 13, of which waited for: 4 -> 7; matrix products, arithmetic and copies ran while one was open for 0% -> 0% of each run, Pallas kernels for 6% -> 6%
where the time goes in v10:
time: 19.9 us; the launch traced here: 19.7 us
  starting transfers between devices  12 us (60%)
  waiting for transfers between devices  4.87 us (24%)
  Pallas kernels  2.83 us (14%)
    ppermute x8, starting transfers between devices, move(): return lax.ppermute(array, ALL_AXES, pairs)  10.4 us
    ppermute x8, waiting for transfers between devices, move(): return lax.ppermute(array, ALL_AXES, pairs)  4.05 us
    ppermute x5, starting transfers between devices, cross(): return lax.ppermute(array, 'dim', [(0, 1), (1, 0)])  1.53 us
    pallas_call x1, Pallas kernels, stage(): pl.pallas_call(stage_kernel, out_shape=[jax.ShapeDtypeStruct(doc_tokens.s...  1.19 us
    pallas_call x1, Pallas kernels, score(): pl.pallas_call(functools.partial(score_kernel, len(pieces), put), out_sha...  0.86 us
    ppermute x5, waiting for transfers between devices, cross(): return lax.ppermute(array, 'dim', [(0, 1), (1, 0)])  0.82 us
    pallas_call x1, Pallas kernels, pick(): pl.pallas_call(functools.partial(pick_kernel, order), out_shape=jax.Shape...  0.78 us
  transfers between devices with their start and end apart: 13, of which 7 were waited for; matrix products, arithmetic and copies ran while one was open for 0% of the time, Pallas kernels for 6%

profile of v10, /device:TPU:0, one launch (start us, length us, event | category | flops | bytes accessed | tf_op | source)
XLA Modules:
  0.0 19.7 jit_solution(17894105997001039442)
XLA Ops:
  0.0 0.5 %collective-permute-start.4 = (bf16[32,64,128]{2,1,0:T(8,128)(2,1)}, bf16[32,64,128]{2,1,0:T(8,128)(2,1)S(1)}, u32[]{:S(2)}, u32[]{:S(2)}) collective-permute-start(bf16[32,64,128]{2,1,0:T(8,128)(2,1)} %own_ref.1), channel_id=1, source_target_pairs={{0,1},{1,0},{2,3},{3,2},{4,5},{5,4},{6,7},{7,6},{8,9},{9,8},{10,11... | collective-permute-start | bytes 1572872 | tf_op jit(solution)/shard_map/ppermute | solution.py:180
  0.5 4.7 %collective-permute-start = (bf16[2,32,128]{2,1,0:T(8,128)(2,1)}, bf16[2,32,128]{2,1,0:T(8,128)(2,1)S(1)}, u32[]{:S(2)}, u32[]{:S(2)}) collective-permute-start(bf16[2,32,128]{2,1,0:T(8,128)(2,1)} %param.4), channel_id=1, source_target_pairs={{3,0},{12,1},{1,2},{14,3},{7,4},{8,5},{5,6},{10,7},{11,8},{4,9},{9... | collective-permute-start | bytes 49160 | tf_op jit(solution)/shard_map/ppermute | solution.py:172
  5.2 1.1 %collective-permute-start.1 = (bf16[2,32,128]{2,1,0:T(8,128)(2,1)}, bf16[2,32,128]{2,1,0:T(8,128)(2,1)S(1)}, u32[]{:S(2)}, u32[]{:S(2)}) collective-permute-start(bf16[2,32,128]{2,1,0:T(8,128)(2,1)} %param.4), channel_id=1, source_target_pairs={{11,0},{14,1},{9,2},{12,3},{15,4},{10,5},{13,6},{8,7},{3,8},{6,9},... | collective-permute-start | bytes 49160 | tf_op jit(solution)/shard_map/ppermute | solution.py:172
  6.2 0.1 collective-permute-start.2
  6.3 0.3 %collective-permute-start.3 = (bf16[2,32,128]{2,1,0:T(8,128)(2,1)}, bf16[2,32,128]{2,1,0:T(8,128)(2,1)S(1)}, u32[]{:S(2)}, u32[]{:S(2)}) collective-permute-start(bf16[2,32,128]{2,1,0:T(8,128)(2,1)} %param.4), channel_id=1, source_target_pairs={{1,0},{4,1},{3,2},{6,3},{5,4},{0,5},{7,6},{2,7},{9,8},{12,9},{11,1... | collective-permute-start | bytes 49160 | tf_op jit(solution)/shard_map/ppermute | solution.py:172
  6.6 0.0 collective-permute-done.4.other_ref
  6.6 1.2 %stage.1 = (bf16[32,64,128]{2,1,0:T(8,128)(2,1)S(1)}, bf16[32,64,128]{2,1,0:T(8,128)(2,1)S(1)}) custom-call(s32[32]{0:T(128)} %lens_hbm_ref.1, bf16[32,64,128]{2,1,0:T(8,128)(2,1)} %own_ref.1, bf16[32,64,128]{2,1,0:T(8,128)(2,1)S(1)} %collective-permute-done.4.other_ref), custom_call_target="tpu_custom_call" | custom-call | flops 1048576 | bytes 2097152 | tf_op jit(solution)/shard_map/stage/pallas_call | solution.py:56
  7.8 0.0 collective-permute-done.refs_0_
  7.8 2.6 %collective-permute-done.1.refs_1_ = bf16[2,32,128]{2,1,0:T(8,128)(2,1)S(1)} collective-permute-done((bf16[2,32,128]{2,1,0:T(8,128)(2,1)}, bf16[2,32,128]{2,1,0:T(8,128)(2,1)S(1)}, u32[]{:S(2)}, u32[]{:S(2)}) %collective-permute-start.1) | collective-permute-done | bytes 16416 | tf_op jit(solution)/shard_map/ppermute | solution.py:172
  10.4 0.1 collective-permute-done.2.refs_2_
  10.5 0.0 collective-permute-done.3.refs_3_
  10.5 0.0 copy-start
  10.5 0.9 %score.1 = (f32[2,32]{1,0:T(2,128)S(1)}, f32[2,32]{1,0:T(2,128)S(1)}, f32[2,32]{1,0:T(2,128)S(1)}, f32[2,32]{1,0:T(2,128)S(1)}) custom-call(bf16[2,32,128]{2,1,0:T(8,128)(2,1)S(1)} %collective-permute-done.refs_0_, bf16[2,32,128]{2,1,0:T(8,128)(2,1)S(1)} %collective-permute-done.1.refs_1_, bf16[2,32,128]{2,1,0:T(8,128)(2,1)S(1)} %collective-permute-done.2.refs_2_, ...), custom_call_target="tpu_custom_call" | custom-call | tf_op jit(solution)/shard_map/score/pallas_call | solution.py:111
  11.4 0.6 %collective-permute-start.9 = (f32[2,32]{1,0:T(2,128)S(1)}, f32[2,32]{1,0:T(2,128)S(1)}, u32[]{:S(2)}, u32[]{:S(2)}) collective-permute-start(f32[2,32]{1,0:T(2,128)S(1)} %get-tuple-element.15), channel_id=1, source_target_pairs={{0,10},{1,15},{2,8},{3,13},{4,14},{5,11},{6,12},{7,9},{8,2},{9,7},... | collective-permute-start | bytes 776 | tf_op jit(solution)/shard_map/ppermute | solution.py:172
  12.0 2.0 %collective-permute-start.11 = (f32[2,32]{1,0:T(2,128)S(1)}, f32[2,32]{1,0:T(2,128)S(1)}, u32[]{:S(2)}, u32[]{:S(2)}) collective-permute-start(f32[2,32]{1,0:T(2,128)S(1)} %get-tuple-element.16), channel_id=1, source_target_pairs={{0,9},{1,12},{2,11},{3,14},{4,13},{5,8},{6,15},{7,10},{8,1},{9,4},... | collective-permute-start | bytes 776 | tf_op jit(solution)/shard_map/ppermute | solution.py:172
  14.0 0.7 %collective-permute-start.5 = (f32[2,32]{1,0:T(2,128)S(1)}, f32[2,32]{1,0:T(2,128)S(1)}, u32[]{:S(2)}, u32[]{:S(2)}) collective-permute-start(f32[2,32]{1,0:T(2,128)S(1)} %get-tuple-element.13), channel_id=1, source_target_pairs={{0,2},{1,7},{2,0},{3,5},{4,6},{5,3},{6,4},{7,1},{8,10},{9,15},{10,... | collective-permute-start | bytes 776 | tf_op jit(solution)/shard_map/ppermute | solution.py:172
  14.8 1.0 %collective-permute-start.7 = (f32[2,32]{1,0:T(2,128)S(1)}, f32[2,32]{1,0:T(2,128)S(1)}, u32[]{:S(2)}, u32[]{:S(2)}) collective-permute-start(f32[2,32]{1,0:T(2,128)S(1)} %get-tuple-element.14), channel_id=1, source_target_pairs={{0,1},{1,4},{2,3},{3,6},{4,5},{5,0},{6,7},{7,2},{8,9},{9,12},{10,1... | collective-permute-start | bytes 776 | tf_op jit(solution)/shard_map/ppermute | solution.py:172
  15.7 1.1 %collective-permute-done.9.refs_4_ = f32[2,32]{1,0:T(2,128)S(1)} collective-permute-done((f32[2,32]{1,0:T(2,128)S(1)}, f32[2,32]{1,0:T(2,128)S(1)}, u32[]{:S(2)}, u32[]{:S(2)}) %collective-permute-start.9) | collective-permute-done | bytes 288 | tf_op jit(solution)/shard_map/ppermute | solution.py:172
  16.9 0.0 collective-permute-start.10
  16.9 0.0 collective-permute-done.11.refs_6_
  16.9 0.6 %collective-permute-start.12 = (f32[2,32]{1,0:T(2,128)S(1)}, f32[2,32]{1,0:T(2,128)S(1)}, u32[]{:S(2)}, u32[]{:S(2)}) collective-permute-start(f32[2,32]{1,0:T(2,128)S(1)} %collective-permute-done.11.refs_6_), channel_id=1, source_target_pairs={{0,1},{1,0},{2,3},{3,2},{4,5},{5,4},{6,7},{7,6},{8,9},{9,8},{10,11... | collective-permute-start | bytes 776 | tf_op jit(solution)/shard_map/ppermute | solution.py:180
  17.4 0.2 collective-permute-done.5.refs_0_
  17.6 0.2 %collective-permute-start.6 = (f32[2,32]{1,0:T(2,128)S(1)}, f32[2,32]{1,0:T(2,128)S(1)}, u32[]{:S(2)}, u32[]{:S(2)}) collective-permute-start(f32[2,32]{1,0:T(2,128)S(1)} %collective-permute-done.5.refs_0_), channel_id=1, source_target_pairs={{0,1},{1,0},{2,3},{3,2},{4,5},{5,4},{6,7},{7,6},{8,9},{9,8},{10,11... | collective-permute-start | bytes 776 | tf_op jit(solution)/shard_map/ppermute | solution.py:180
  17.8 0.0 collective-permute-done.7.refs_2_
  17.8 0.3 %collective-permute-start.8 = (f32[2,32]{1,0:T(2,128)S(1)}, f32[2,32]{1,0:T(2,128)S(1)}, u32[]{:S(2)}, u32[]{:S(2)}) collective-permute-start(f32[2,32]{1,0:T(2,128)S(1)} %collective-permute-done.7.refs_2_), channel_id=1, source_target_pairs={{0,1},{1,0},{2,3},{3,2},{4,5},{5,4},{6,7},{7,6},{8,9},{9,8},{10,11... | collective-permute-start | bytes 776 | tf_op jit(solution)/shard_map/ppermute | solution.py:180
  18.1 0.0 copy-done
  18.1 0.0 collective-permute-done.10.refs_5_
  18.1 0.1 collective-permute-done.12.refs_7_
  18.2 0.5 %collective-permute-done.6.refs_1_ = f32[2,32]{1,0:T(2,128)S(1)} collective-permute-done((f32[2,32]{1,0:T(2,128)S(1)}, f32[2,32]{1,0:T(2,128)S(1)}, u32[]{:S(2)}, u32[]{:S(2)}) %collective-permute-start.6) | collective-permute-done | bytes 288 | tf_op jit(solution)/shard_map/ppermute | solution.py:180
  18.7 0.2 %collective-permute-done.8.refs_3_ = f32[2,32]{1,0:T(2,128)S(1)} collective-permute-done((f32[2,32]{1,0:T(2,128)S(1)}, f32[2,32]{1,0:T(2,128)S(1)}, u32[]{:S(2)}, u32[]{:S(2)}) %collective-permute-start.8) | collective-permute-done | bytes 288 | tf_op jit(solution)/shard_map/ppermute | solution.py:180
  19.0 0.8 %pick.1 = f32[2,1000]{1,0:T(2,128)} custom-call(s32[2,1000]{1,0:T(2,128)S(1)} %and_add_fusion.spot_ref, f32[2,32]{1,0:T(2,128)S(1)} %collective-permute-done.5.refs_0_, f32[2,32]{1,0:T(2,128)S(1)} %collective-permute-done.6.refs_1_, f32[2,32]{1,0:T(2,128)S(1)} %collective-permute-done.7.refs_2_, f32[2,32]{1,0:T(2,128)S(1)} %collective-permute-done.8.refs_3_, ...), custom_call_target="tpu_custom_call" | custom-call | tf_op jit(solution)/shard_map/pick/pallas_call | solution.py:149
  (1 shorter events, 0.0 us)
Async XLA Ops:
  0.0 6.6 %collective-permute-start.4 = (bf16[32,64,128]{2,1,0:T(8,128)(2,1)}, bf16[32,64,128]{2,1,0:T(8,128)(2,1)S(1)}, u32[]{:S(2)}, u32[]{:S(2)}) collective-permute-start(bf16[32,64,128]{2,1,0:T(8,128)(2,1)} %own_ref.1), channel_id=1, source_target_pairs={{0,1},{1,0},{2,3},{3,2},{4,5},{5,4},{6,7},{7,6},{8,9},{9,8},{10,11... | collective-permute-start | bytes 1572872 | tf_op jit(solution)/shard_map/ppermute | solution.py:180
  0.5 7.4 %collective-permute-start = (bf16[2,32,128]{2,1,0:T(8,128)(2,1)}, bf16[2,32,128]{2,1,0:T(8,128)(2,1)S(1)}, u32[]{:S(2)}, u32[]{:S(2)}) collective-permute-start(bf16[2,32,128]{2,1,0:T(8,128)(2,1)} %param.4), channel_id=1, source_target_pairs={{3,0},{12,1},{1,2},{14,3},{7,4},{8,5},{5,6},{10,7},{11,8},{4,9},{9... | collective-permute-start | bytes 49160 | tf_op jit(solution)/shard_map/ppermute | solution.py:172
  5.2 5.3 %collective-permute-start.1 = (bf16[2,32,128]{2,1,0:T(8,128)(2,1)}, bf16[2,32,128]{2,1,0:T(8,128)(2,1)S(1)}, u32[]{:S(2)}, u32[]{:S(2)}) collective-permute-start(bf16[2,32,128]{2,1,0:T(8,128)(2,1)} %param.4), channel_id=1, source_target_pairs={{11,0},{14,1},{9,2},{12,3},{15,4},{10,5},{13,6},{8,7},{3,8},{6,9},... | collective-permute-start | bytes 49160 | tf_op jit(solution)/shard_map/ppermute | solution.py:172
  6.2 4.3 %collective-permute-start.2 = (bf16[2,32,128]{2,1,0:T(8,128)(2,1)}, bf16[2,32,128]{2,1,0:T(8,128)(2,1)S(1)}, u32[]{:S(2)}, u32[]{:S(2)}) collective-permute-start(bf16[2,32,128]{2,1,0:T(8,128)(2,1)} %param.4), channel_id=1, source_target_pairs={{9,0},{6,1},{11,2},{4,3},{13,4},{2,5},{15,6},{0,7},{1,8},{14,9},{3... | collective-permute-start | bytes 49160 | tf_op jit(solution)/shard_map/ppermute | solution.py:172
  6.3 4.3 %collective-permute-start.3 = (bf16[2,32,128]{2,1,0:T(8,128)(2,1)}, bf16[2,32,128]{2,1,0:T(8,128)(2,1)S(1)}, u32[]{:S(2)}, u32[]{:S(2)}) collective-permute-start(bf16[2,32,128]{2,1,0:T(8,128)(2,1)} %param.4), channel_id=1, source_target_pairs={{1,0},{4,1},{3,2},{6,3},{5,4},{0,5},{7,6},{2,7},{9,8},{12,9},{11,1... | collective-permute-start | bytes 49160 | tf_op jit(solution)/shard_map/ppermute | solution.py:172
  10.5 7.6 %copy-start = (s32[2,1000]{1,0:T(2,128)S(1)}, s32[2,1000]{1,0:T(2,128)}, u32[]{:S(2)}) copy-start(s32[2,1000]{1,0:T(2,128)} %param.7) | copy-start | bytes 24004
  11.4 5.4 %collective-permute-start.9 = (f32[2,32]{1,0:T(2,128)S(1)}, f32[2,32]{1,0:T(2,128)S(1)}, u32[]{:S(2)}, u32[]{:S(2)}) collective-permute-start(f32[2,32]{1,0:T(2,128)S(1)} %get-tuple-element.15), channel_id=1, source_target_pairs={{0,10},{1,15},{2,8},{3,13},{4,14},{5,11},{6,12},{7,9},{8,2},{9,7},... | collective-permute-start | bytes 776 | tf_op jit(solution)/shard_map/ppermute | solution.py:172
  12.0 4.8 %collective-permute-start.11 = (f32[2,32]{1,0:T(2,128)S(1)}, f32[2,32]{1,0:T(2,128)S(1)}, u32[]{:S(2)}, u32[]{:S(2)}) collective-permute-start(f32[2,32]{1,0:T(2,128)S(1)} %get-tuple-element.16), channel_id=1, source_target_pairs={{0,9},{1,12},{2,11},{3,14},{4,13},{5,8},{6,15},{7,10},{8,1},{9,4},... | collective-permute-start | bytes 776 | tf_op jit(solution)/shard_map/ppermute | solution.py:172
  14.0 3.6 %collective-permute-start.5 = (f32[2,32]{1,0:T(2,128)S(1)}, f32[2,32]{1,0:T(2,128)S(1)}, u32[]{:S(2)}, u32[]{:S(2)}) collective-permute-start(f32[2,32]{1,0:T(2,128)S(1)} %get-tuple-element.13), channel_id=1, source_target_pairs={{0,2},{1,7},{2,0},{3,5},{4,6},{5,3},{6,4},{7,1},{8,10},{9,15},{10,... | collective-permute-start | bytes 776 | tf_op jit(solution)/shard_map/ppermute | solution.py:172
  14.8 3.1 %collective-permute-start.7 = (f32[2,32]{1,0:T(2,128)S(1)}, f32[2,32]{1,0:T(2,128)S(1)}, u32[]{:S(2)}, u32[]{:S(2)}) collective-permute-start(f32[2,32]{1,0:T(2,128)S(1)} %get-tuple-element.14), channel_id=1, source_target_pairs={{0,1},{1,4},{2,3},{3,6},{4,5},{5,0},{6,7},{7,2},{8,9},{9,12},{10,1... | collective-permute-start | bytes 776 | tf_op jit(solution)/shard_map/ppermute | solution.py:172
  16.9 1.3 %collective-permute-start.10 = (f32[2,32]{1,0:T(2,128)S(1)}, f32[2,32]{1,0:T(2,128)S(1)}, u32[]{:S(2)}, u32[]{:S(2)}) collective-permute-start(f32[2,32]{1,0:T(2,128)S(1)} %collective-permute-done.9.refs_4_), channel_id=1, source_target_pairs={{0,1},{1,0},{2,3},{3,2},{4,5},{5,4},{6,7},{7,6},{8,9},{9,8},{10,11... | collective-permute-start | bytes 776 | tf_op jit(solution)/shard_map/ppermute | solution.py:180
  16.9 1.4 %collective-permute-start.12 = (f32[2,32]{1,0:T(2,128)S(1)}, f32[2,32]{1,0:T(2,128)S(1)}, u32[]{:S(2)}, u32[]{:S(2)}) collective-permute-start(f32[2,32]{1,0:T(2,128)S(1)} %collective-permute-done.11.refs_6_), channel_id=1, source_target_pairs={{0,1},{1,0},{2,3},{3,2},{4,5},{5,4},{6,7},{7,6},{8,9},{9,8},{10,11... | collective-permute-start | bytes 776 | tf_op jit(solution)/shard_map/ppermute | solution.py:180
  17.6 1.1 %collective-permute-start.6 = (f32[2,32]{1,0:T(2,128)S(1)}, f32[2,32]{1,0:T(2,128)S(1)}, u32[]{:S(2)}, u32[]{:S(2)}) collective-permute-start(f32[2,32]{1,0:T(2,128)S(1)} %collective-permute-done.5.refs_0_), channel_id=1, source_target_pairs={{0,1},{1,0},{2,3},{3,2},{4,5},{5,4},{6,7},{7,6},{8,9},{9,8},{10,11... | collective-permute-start | bytes 776 | tf_op jit(solution)/shard_map/ppermute | solution.py:180
  17.8 1.1 %collective-permute-start.8 = (f32[2,32]{1,0:T(2,128)S(1)}, f32[2,32]{1,0:T(2,128)S(1)}, u32[]{:S(2)}, u32[]{:S(2)}) collective-permute-start(f32[2,32]{1,0:T(2,128)S(1)} %collective-permute-done.7.refs_2_), channel_id=1, source_target_pairs={{0,1},{1,0},{2,3},{3,2},{4,5},{5,4},{6,7},{7,6},{8,9},{9,8},{10,11... | collective-permute-start | bytes 776 | tf_op jit(solution)/shard_map/ppermute | solution.py:180

commit v11 on v10

--- a/solution.py
+++ b/solution.py
@@ -73,8 +73,8 @@
 def score_kernel(n_pieces, put, *refs):
     piece_refs = refs[:n_pieces]
     own_ref, other_ref = refs[n_pieces: n_pieces + 2]
-    out_refs = refs[n_pieces + 2: -3]
-    flat_ref, turned_ref, max_ref = refs[-3:]
+    out_refs = refs[n_pieces + 2: -2]
+    flat_ref, max_ref = refs[-2:]
     q_tokens, width = piece_refs[0].shape[1:]
     count, half, _ = own_ref.shape
     total = flat_ref.shape[0]
@@ -83,7 +83,6 @@
         rows = piece_ref.shape[0] * q_tokens
         flat_ref[pl.ds(at, rows), :] = piece_ref[...].reshape(rows, width)
         at += rows
-    turned_ref[...] = flat_ref[...].T
     block = min(total, BLOCK)
     step = min(count, 8)
 
@@ -93,7 +92,9 @@
             best = None
             for ref in (own_ref, other_ref):
                 docs = ref[pl.ds(start, step)].reshape(step * half, width)
-                part = jnp.dot(docs, turned_ref[:, pl.ds(at, block)], preferred_element_type=jnp.float32)
+                part = lax.dot_general(
+                    docs, flat_ref[pl.ds(at, block), :], (((1,), (1,)), ((), ())), preferred_element_type=jnp.float32
+                )
                 part = jnp.max(part.reshape(step, half // 8, 8, block), axis=1)
                 best = part if best is None else jnp.maximum(best, part)
             max_ref[pl.ds(start, step), pl.ds(at, block)] = jnp.max(best, axis=1)
@@ -115,7 +116,6 @@
         out_specs=[vmem] * len(out_shapes),
         scratch_shapes=[
             pltpu.VMEM((queries * q_tokens, width), jnp.bfloat16),
-            pltpu.VMEM((width, queries * q_tokens), jnp.bfloat16),
             pltpu.VMEM((count, queries * q_tokens), jnp.float32),
         ],
         compiler_params=pltpu.CompilerParams(vmem_limit_bytes=(8 + queries // 10) * 1024 * 1024),

time: 19.9 us -> 19.8 us (level)
  no operation moved by 1% of the time
where the time goes in v11:
time: 19.8 us; the launch traced here: 19.7 us
  starting transfers between devices  12 us (61%)
  waiting for transfers between devices  4.88 us (25%)
  Pallas kernels  2.79 us (14%)
    ppermute x8, starting transfers between devices, move(): return lax.ppermute(array, ALL_AXES, pairs)  10.4 us
    ppermute x8, waiting for transfers between devices, move(): return lax.ppermute(array, ALL_AXES, pairs)  4.05 us
    ppermute x5, starting transfers between devices, cross(): return lax.ppermute(array, 'dim', [(0, 1), (1, 0)])  1.52 us
    pallas_call x1, Pallas kernels, stage(): pl.pallas_call(stage_kernel, out_shape=[jax.ShapeDtypeStruct(doc_tokens.s...  1.19 us
    pallas_call x1, Pallas kernels, score(): pl.pallas_call(functools.partial(score_kernel, len(pieces), put), out_sha...  0.83 us
    ppermute x5, waiting for transfers between devices, cross(): return lax.ppermute(array, 'dim', [(0, 1), (1, 0)])  0.83 us
    pallas_call x1, Pallas kernels, pick(): pl.pallas_call(functools.partial(pick_kernel, order), out_shape=jax.Shape...  0.78 us
  transfers between devices with their start and end apart: 13, of which 7 were waited for; matrix products, arithmetic and copies ran while one was open for 0% of the time, Pallas kernels for 6%

profile of v11, /device:TPU:0, one launch (start us, length us, event | category | flops | bytes accessed | tf_op | source)
XLA Modules:
  0.0 19.7 jit_solution(16867375396979247587)
XLA Ops:
  0.0 0.5 %collective-permute-start.4 = (bf16[32,64,128]{2,1,0:T(8,128)(2,1)}, bf16[32,64,128]{2,1,0:T(8,128)(2,1)S(1)}, u32[]{:S(2)}, u32[]{:S(2)}) collective-permute-start(bf16[32,64,128]{2,1,0:T(8,128)(2,1)} %own_ref.1), channel_id=1, source_target_pairs={{0,1},{1,0},{2,3},{3,2},{4,5},{5,4},{6,7},{7,6},{8,9},{9,8},{10,11... | collective-permute-start | bytes 1572872 | tf_op jit(solution)/shard_map/ppermute | solution.py:180
  0.5 4.7 %collective-permute-start = (bf16[2,32,128]{2,1,0:T(8,128)(2,1)}, bf16[2,32,128]{2,1,0:T(8,128)(2,1)S(1)}, u32[]{:S(2)}, u32[]{:S(2)}) collective-permute-start(bf16[2,32,128]{2,1,0:T(8,128)(2,1)} %param.4), channel_id=1, source_target_pairs={{3,0},{12,1},{1,2},{14,3},{7,4},{8,5},{5,6},{10,7},{11,8},{4,9},{9... | collective-permute-start | bytes 49160 | tf_op jit(solution)/shard_map/ppermute | solution.py:172
  5.2 1.1 %collective-permute-start.1 = (bf16[2,32,128]{2,1,0:T(8,128)(2,1)}, bf16[2,32,128]{2,1,0:T(8,128)(2,1)S(1)}, u32[]{:S(2)}, u32[]{:S(2)}) collective-permute-start(bf16[2,32,128]{2,1,0:T(8,128)(2,1)} %param.4), channel_id=1, source_target_pairs={{11,0},{14,1},{9,2},{12,3},{15,4},{10,5},{13,6},{8,7},{3,8},{6,9},... | collective-permute-start | bytes 49160 | tf_op jit(solution)/shard_map/ppermute | solution.py:172
  6.2 0.1 collective-permute-start.2
  6.3 0.3 %collective-permute-start.3 = (bf16[2,32,128]{2,1,0:T(8,128)(2,1)}, bf16[2,32,128]{2,1,0:T(8,128)(2,1)S(1)}, u32[]{:S(2)}, u32[]{:S(2)}) collective-permute-start(bf16[2,32,128]{2,1,0:T(8,128)(2,1)} %param.4), channel_id=1, source_target_pairs={{1,0},{4,1},{3,2},{6,3},{5,4},{0,5},{7,6},{2,7},{9,8},{12,9},{11,1... | collective-permute-start | bytes 49160 | tf_op jit(solution)/shard_map/ppermute | solution.py:172
  6.6 0.0 collective-permute-done.4.other_ref
  6.6 1.2 %stage.1 = (bf16[32,64,128]{2,1,0:T(8,128)(2,1)S(1)}, bf16[32,64,128]{2,1,0:T(8,128)(2,1)S(1)}) custom-call(s32[32]{0:T(128)} %lens_hbm_ref.1, bf16[32,64,128]{2,1,0:T(8,128)(2,1)} %own_ref.1, bf16[32,64,128]{2,1,0:T(8,128)(2,1)S(1)} %collective-permute-done.4.other_ref), custom_call_target="tpu_custom_call" | custom-call | flops 1048576 | bytes 2097152 | tf_op jit(solution)/shard_map/stage/pallas_call | solution.py:56
  7.8 0.0 collective-permute-done.refs_0_
  7.8 2.6 %collective-permute-done.1.refs_1_ = bf16[2,32,128]{2,1,0:T(8,128)(2,1)S(1)} collective-permute-done((bf16[2,32,128]{2,1,0:T(8,128)(2,1)}, bf16[2,32,128]{2,1,0:T(8,128)(2,1)S(1)}, u32[]{:S(2)}, u32[]{:S(2)}) %collective-permute-start.1) | collective-permute-done | bytes 16416 | tf_op jit(solution)/shard_map/ppermute | solution.py:172
  10.4 0.1 collective-permute-done.2.refs_2_
  10.5 0.0 collective-permute-done.3.refs_3_
  10.5 0.0 copy-start
  10.5 0.8 %score.1 = (f32[2,32]{1,0:T(2,128)S(1)}, f32[2,32]{1,0:T(2,128)S(1)}, f32[2,32]{1,0:T(2,128)S(1)}, f32[2,32]{1,0:T(2,128)S(1)}) custom-call(bf16[2,32,128]{2,1,0:T(8,128)(2,1)S(1)} %collective-permute-done.refs_0_, bf16[2,32,128]{2,1,0:T(8,128)(2,1)S(1)} %collective-permute-done.1.refs_1_, bf16[2,32,128]{2,1,0:T(8,128)(2,1)S(1)} %collective-permute-done.2.refs_2_, ...), custom_call_target="tpu_custom_call" | custom-call | tf_op jit(solution)/shard_map/score/pallas_call | solution.py:112
  11.4 0.6 %collective-permute-start.9 = (f32[2,32]{1,0:T(2,128)S(1)}, f32[2,32]{1,0:T(2,128)S(1)}, u32[]{:S(2)}, u32[]{:S(2)}) collective-permute-start(f32[2,32]{1,0:T(2,128)S(1)} %get-tuple-element.15), channel_id=1, source_target_pairs={{0,10},{1,15},{2,8},{3,13},{4,14},{5,11},{6,12},{7,9},{8,2},{9,7},... | collective-permute-start | bytes 776 | tf_op jit(solution)/shard_map/ppermute | solution.py:172
  12.0 2.0 %collective-permute-start.11 = (f32[2,32]{1,0:T(2,128)S(1)}, f32[2,32]{1,0:T(2,128)S(1)}, u32[]{:S(2)}, u32[]{:S(2)}) collective-permute-start(f32[2,32]{1,0:T(2,128)S(1)} %get-tuple-element.16), channel_id=1, source_target_pairs={{0,9},{1,12},{2,11},{3,14},{4,13},{5,8},{6,15},{7,10},{8,1},{9,4},... | collective-permute-start | bytes 776 | tf_op jit(solution)/shard_map/ppermute | solution.py:172
  14.0 0.7 %collective-permute-start.5 = (f32[2,32]{1,0:T(2,128)S(1)}, f32[2,32]{1,0:T(2,128)S(1)}, u32[]{:S(2)}, u32[]{:S(2)}) collective-permute-start(f32[2,32]{1,0:T(2,128)S(1)} %get-tuple-element.13), channel_id=1, source_target_pairs={{0,2},{1,7},{2,0},{3,5},{4,6},{5,3},{6,4},{7,1},{8,10},{9,15},{10,... | collective-permute-start | bytes 776 | tf_op jit(solution)/shard_map/ppermute | solution.py:172
  14.7 1.0 %collective-permute-start.7 = (f32[2,32]{1,0:T(2,128)S(1)}, f32[2,32]{1,0:T(2,128)S(1)}, u32[]{:S(2)}, u32[]{:S(2)}) collective-permute-start(f32[2,32]{1,0:T(2,128)S(1)} %get-tuple-element.14), channel_id=1, source_target_pairs={{0,1},{1,4},{2,3},{3,6},{4,5},{5,0},{6,7},{7,2},{8,9},{9,12},{10,1... | collective-permute-start | bytes 776 | tf_op jit(solution)/shard_map/ppermute | solution.py:172
  15.7 1.1 %collective-permute-done.9.refs_4_ = f32[2,32]{1,0:T(2,128)S(1)} collective-permute-done((f32[2,32]{1,0:T(2,128)S(1)}, f32[2,32]{1,0:T(2,128)S(1)}, u32[]{:S(2)}, u32[]{:S(2)}) %collective-permute-start.9) | collective-permute-done | bytes 288 | tf_op jit(solution)/shard_map/ppermute | solution.py:172
  16.8 0.0 collective-permute-start.10
  16.8 0.0 collective-permute-done.11.refs_6_
  16.8 0.6 %collective-permute-start.12 = (f32[2,32]{1,0:T(2,128)S(1)}, f32[2,32]{1,0:T(2,128)S(1)}, u32[]{:S(2)}, u32[]{:S(2)}) collective-permute-start(f32[2,32]{1,0:T(2,128)S(1)} %collective-permute-done.11.refs_6_), channel_id=1, source_target_pairs={{0,1},{1,0},{2,3},{3,2},{4,5},{5,4},{6,7},{7,6},{8,9},{9,8},{10,11... | collective-permute-start | bytes 776 | tf_op jit(solution)/shard_map/ppermute | solution.py:180
  17.4 0.2 collective-permute-done.5.refs_0_
  17.6 0.2 %collective-permute-start.6 = (f32[2,32]{1,0:T(2,128)S(1)}, f32[2,32]{1,0:T(2,128)S(1)}, u32[]{:S(2)}, u32[]{:S(2)}) collective-permute-start(f32[2,32]{1,0:T(2,128)S(1)} %collective-permute-done.5.refs_0_), channel_id=1, source_target_pairs={{0,1},{1,0},{2,3},{3,2},{4,5},{5,4},{6,7},{7,6},{8,9},{9,8},{10,11... | collective-permute-start | bytes 776 | tf_op jit(solution)/shard_map/ppermute | solution.py:180
  17.8 0.0 collective-permute-done.7.refs_2_
  17.8 0.3 %collective-permute-start.8 = (f32[2,32]{1,0:T(2,128)S(1)}, f32[2,32]{1,0:T(2,128)S(1)}, u32[]{:S(2)}, u32[]{:S(2)}) collective-permute-start(f32[2,32]{1,0:T(2,128)S(1)} %collective-permute-done.7.refs_2_), channel_id=1, source_target_pairs={{0,1},{1,0},{2,3},{3,2},{4,5},{5,4},{6,7},{7,6},{8,9},{9,8},{10,11... | collective-permute-start | bytes 776 | tf_op jit(solution)/shard_map/ppermute | solution.py:180
  18.1 0.0 copy-done
  18.1 0.0 collective-permute-done.10.refs_5_
  18.1 0.1 collective-permute-done.12.refs_7_
  18.2 0.5 %collective-permute-done.6.refs_1_ = f32[2,32]{1,0:T(2,128)S(1)} collective-permute-done((f32[2,32]{1,0:T(2,128)S(1)}, f32[2,32]{1,0:T(2,128)S(1)}, u32[]{:S(2)}, u32[]{:S(2)}) %collective-permute-start.6) | collective-permute-done | bytes 288 | tf_op jit(solution)/shard_map/ppermute | solution.py:180
  18.7 0.2 %collective-permute-done.8.refs_3_ = f32[2,32]{1,0:T(2,128)S(1)} collective-permute-done((f32[2,32]{1,0:T(2,128)S(1)}, f32[2,32]{1,0:T(2,128)S(1)}, u32[]{:S(2)}, u32[]{:S(2)}) %collective-permute-start.8) | collective-permute-done | bytes 288 | tf_op jit(solution)/shard_map/ppermute | solution.py:180
  18.9 0.8 %pick.1 = f32[2,1000]{1,0:T(2,128)} custom-call(s32[2,1000]{1,0:T(2,128)S(1)} %and_add_fusion.spot_ref, f32[2,32]{1,0:T(2,128)S(1)} %collective-permute-done.5.refs_0_, f32[2,32]{1,0:T(2,128)S(1)} %collective-permute-done.6.refs_1_, f32[2,32]{1,0:T(2,128)S(1)} %collective-permute-done.7.refs_2_, f32[2,32]{1,0:T(2,128)S(1)} %collective-permute-done.8.refs_3_, ...), custom_call_target="tpu_custom_call" | custom-call | tf_op jit(solution)/shard_map/pick/pallas_call | solution.py:149
  (1 shorter events, 0.0 us)
Async XLA Ops:
  0.0 6.6 %collective-permute-start.4 = (bf16[32,64,128]{2,1,0:T(8,128)(2,1)}, bf16[32,64,128]{2,1,0:T(8,128)(2,1)S(1)}, u32[]{:S(2)}, u32[]{:S(2)}) collective-permute-start(bf16[32,64,128]{2,1,0:T(8,128)(2,1)} %own_ref.1), channel_id=1, source_target_pairs={{0,1},{1,0},{2,3},{3,2},{4,5},{5,4},{6,7},{7,6},{8,9},{9,8},{10,11... | collective-permute-start | bytes 1572872 | tf_op jit(solution)/shard_map/ppermute | solution.py:180
  0.5 7.4 %collective-permute-start = (bf16[2,32,128]{2,1,0:T(8,128)(2,1)}, bf16[2,32,128]{2,1,0:T(8,128)(2,1)S(1)}, u32[]{:S(2)}, u32[]{:S(2)}) collective-permute-start(bf16[2,32,128]{2,1,0:T(8,128)(2,1)} %param.4), channel_id=1, source_target_pairs={{3,0},{12,1},{1,2},{14,3},{7,4},{8,5},{5,6},{10,7},{11,8},{4,9},{9... | collective-permute-start | bytes 49160 | tf_op jit(solution)/shard_map/ppermute | solution.py:172
  5.2 5.3 %collective-permute-start.1 = (bf16[2,32,128]{2,1,0:T(8,128)(2,1)}, bf16[2,32,128]{2,1,0:T(8,128)(2,1)S(1)}, u32[]{:S(2)}, u32[]{:S(2)}) collective-permute-start(bf16[2,32,128]{2,1,0:T(8,128)(2,1)} %param.4), channel_id=1, source_target_pairs={{11,0},{14,1},{9,2},{12,3},{15,4},{10,5},{13,6},{8,7},{3,8},{6,9},... | collective-permute-start | bytes 49160 | tf_op jit(solution)/shard_map/ppermute | solution.py:172
  6.2 4.3 %collective-permute-start.2 = (bf16[2,32,128]{2,1,0:T(8,128)(2,1)}, bf16[2,32,128]{2,1,0:T(8,128)(2,1)S(1)}, u32[]{:S(2)}, u32[]{:S(2)}) collective-permute-start(bf16[2,32,128]{2,1,0:T(8,128)(2,1)} %param.4), channel_id=1, source_target_pairs={{9,0},{6,1},{11,2},{4,3},{13,4},{2,5},{15,6},{0,7},{1,8},{14,9},{3... | collective-permute-start | bytes 49160 | tf_op jit(solution)/shard_map/ppermute | solution.py:172
  6.3 4.3 %collective-permute-start.3 = (bf16[2,32,128]{2,1,0:T(8,128)(2,1)}, bf16[2,32,128]{2,1,0:T(8,128)(2,1)S(1)}, u32[]{:S(2)}, u32[]{:S(2)}) collective-permute-start(bf16[2,32,128]{2,1,0:T(8,128)(2,1)} %param.4), channel_id=1, source_target_pairs={{1,0},{4,1},{3,2},{6,3},{5,4},{0,5},{7,6},{2,7},{9,8},{12,9},{11,1... | collective-permute-start | bytes 49160 | tf_op jit(solution)/shard_map/ppermute | solution.py:172
  10.5 7.5 %copy-start = (s32[2,1000]{1,0:T(2,128)S(1)}, s32[2,1000]{1,0:T(2,128)}, u32[]{:S(2)}) copy-start(s32[2,1000]{1,0:T(2,128)} %param.7) | copy-start | bytes 24004
  11.4 5.4 %collective-permute-start.9 = (f32[2,32]{1,0:T(2,128)S(1)}, f32[2,32]{1,0:T(2,128)S(1)}, u32[]{:S(2)}, u32[]{:S(2)}) collective-permute-start(f32[2,32]{1,0:T(2,128)S(1)} %get-tuple-element.15), channel_id=1, source_target_pairs={{0,10},{1,15},{2,8},{3,13},{4,14},{5,11},{6,12},{7,9},{8,2},{9,7},... | collective-permute-start | bytes 776 | tf_op jit(solution)/shard_map/ppermute | solution.py:172
  12.0 4.8 %collective-permute-start.11 = (f32[2,32]{1,0:T(2,128)S(1)}, f32[2,32]{1,0:T(2,128)S(1)}, u32[]{:S(2)}, u32[]{:S(2)}) collective-permute-start(f32[2,32]{1,0:T(2,128)S(1)} %get-tuple-element.16), channel_id=1, source_target_pairs={{0,9},{1,12},{2,11},{3,14},{4,13},{5,8},{6,15},{7,10},{8,1},{9,4},... | collective-permute-start | bytes 776 | tf_op jit(solution)/shard_map/ppermute | solution.py:172
  14.0 3.6 %collective-permute-start.5 = (f32[2,32]{1,0:T(2,128)S(1)}, f32[2,32]{1,0:T(2,128)S(1)}, u32[]{:S(2)}, u32[]{:S(2)}) collective-permute-start(f32[2,32]{1,0:T(2,128)S(1)} %get-tuple-element.13), channel_id=1, source_target_pairs={{0,2},{1,7},{2,0},{3,5},{4,6},{5,3},{6,4},{7,1},{8,10},{9,15},{10,... | collective-permute-start | bytes 776 | tf_op jit(solution)/shard_map/ppermute | solution.py:172
  14.7 3.1 %collective-permute-start.7 = (f32[2,32]{1,0:T(2,128)S(1)}, f32[2,32]{1,0:T(2,128)S(1)}, u32[]{:S(2)}, u32[]{:S(2)}) collective-permute-start(f32[2,32]{1,0:T(2,128)S(1)} %get-tuple-element.14), channel_id=1, source_target_pairs={{0,1},{1,4},{2,3},{3,6},{4,5},{5,0},{6,7},{7,2},{8,9},{9,12},{10,1... | collective-permute-start | bytes 776 | tf_op jit(solution)/shard_map/ppermute | solution.py:172
  16.8 1.3 %collective-permute-start.10 = (f32[2,32]{1,0:T(2,128)S(1)}, f32[2,32]{1,0:T(2,128)S(1)}, u32[]{:S(2)}, u32[]{:S(2)}) collective-permute-start(f32[2,32]{1,0:T(2,128)S(1)} %collective-permute-done.9.refs_4_), channel_id=1, source_target_pairs={{0,1},{1,0},{2,3},{3,2},{4,5},{5,4},{6,7},{7,6},{8,9},{9,8},{10,11... | collective-permute-start | bytes 776 | tf_op jit(solution)/shard_map/ppermute | solution.py:180
  16.8 1.4 %collective-permute-start.12 = (f32[2,32]{1,0:T(2,128)S(1)}, f32[2,32]{1,0:T(2,128)S(1)}, u32[]{:S(2)}, u32[]{:S(2)}) collective-permute-start(f32[2,32]{1,0:T(2,128)S(1)} %collective-permute-done.11.refs_6_), channel_id=1, source_target_pairs={{0,1},{1,0},{2,3},{3,2},{4,5},{5,4},{6,7},{7,6},{8,9},{9,8},{10,11... | collective-permute-start | bytes 776 | tf_op jit(solution)/shard_map/ppermute | solution.py:180
  17.6 1.1 %collective-permute-start.6 = (f32[2,32]{1,0:T(2,128)S(1)}, f32[2,32]{1,0:T(2,128)S(1)}, u32[]{:S(2)}, u32[]{:S(2)}) collective-permute-start(f32[2,32]{1,0:T(2,128)S(1)} %collective-permute-done.5.refs_0_), channel_id=1, source_target_pairs={{0,1},{1,0},{2,3},{3,2},{4,5},{5,4},{6,7},{7,6},{8,9},{9,8},{10,11... | collective-permute-start | bytes 776 | tf_op jit(solution)/shard_map/ppermute | solution.py:180
  17.8 1.1 %collective-permute-start.8 = (f32[2,32]{1,0:T(2,128)S(1)}, f32[2,32]{1,0:T(2,128)S(1)}, u32[]{:S(2)}, u32[]{:S(2)}) collective-permute-start(f32[2,32]{1,0:T(2,128)S(1)} %collective-permute-done.7.refs_2_), channel_id=1, source_target_pairs={{0,1},{1,0},{2,3},{3,2},{4,5},{5,4},{6,7},{7,6},{8,9},{9,8},{10,11... | collective-permute-start | bytes 776 | tf_op jit(solution)/shard_map/ppermute | solution.py:180

commit v12 on v11

--- a/solution.py
+++ b/solution.py
@@ -84,7 +84,7 @@
         flat_ref[pl.ds(at, rows), :] = piece_ref[...].reshape(rows, width)
         at += rows
     block = min(total, BLOCK)
-    step = min(count, 8)
+    step = min(count, 16)
 
     def group(g, _):
         start = pl.multiple_of(g * step, step)

time: 19.8 us -> 19.8 us (level)
  no operation moved by 1% of the time
where the time goes in v12:
time: 19.8 us; the launch traced here: 19.7 us
  starting transfers between devices  12 us (61%)
  waiting for transfers between devices  4.88 us (25%)
  Pallas kernels  2.79 us (14%)
    ppermute x8, starting transfers between devices, move(): return lax.ppermute(array, ALL_AXES, pairs)  10.4 us
    ppermute x8, waiting for transfers between devices, move(): return lax.ppermute(array, ALL_AXES, pairs)  4.05 us
    ppermute x5, starting transfers between devices, cross(): return lax.ppermute(array, 'dim', [(0, 1), (1, 0)])  1.53 us
    pallas_call x1, Pallas kernels, stage(): pl.pallas_call(stage_kernel, out_shape=[jax.ShapeDtypeStruct(doc_tokens.s...  1.19 us
    ppermute x5, waiting for transfers between devices, cross(): return lax.ppermute(array, 'dim', [(0, 1), (1, 0)])  0.83 us
    pallas_call x1, Pallas kernels, score(): pl.pallas_call(functools.partial(score_kernel, len(pieces), put), out_sha...  0.82 us
    pallas_call x1, Pallas kernels, pick(): pl.pallas_call(functools.partial(pick_kernel, order), out_shape=jax.Shape...  0.78 us
  transfers between devices with their start and end apart: 13, of which 7 were waited for; matrix products, arithmetic and copies ran while one was open for 0% of the time, Pallas kernels for 6%

profile of v12, /device:TPU:0, one launch (start us, length us, event | category | flops | bytes accessed | tf_op | source)
XLA Modules:
  0.0 19.7 jit_solution(2808462111612249747)
XLA Ops:
  0.0 0.5 %collective-permute-start.4 = (bf16[32,64,128]{2,1,0:T(8,128)(2,1)}, bf16[32,64,128]{2,1,0:T(8,128)(2,1)S(1)}, u32[]{:S(2)}, u32[]{:S(2)}) collective-permute-start(bf16[32,64,128]{2,1,0:T(8,128)(2,1)} %own_ref.1), channel_id=1, source_target_pairs={{0,1},{1,0},{2,3},{3,2},{4,5},{5,4},{6,7},{7,6},{8,9},{9,8},{10,11... | collective-permute-start | bytes 1572872 | tf_op jit(solution)/shard_map/ppermute | solution.py:180
  0.5 4.7 %collective-permute-start = (bf16[2,32,128]{2,1,0:T(8,128)(2,1)}, bf16[2,32,128]{2,1,0:T(8,128)(2,1)S(1)}, u32[]{:S(2)}, u32[]{:S(2)}) collective-permute-start(bf16[2,32,128]{2,1,0:T(8,128)(2,1)} %param.4), channel_id=1, source_target_pairs={{3,0},{12,1},{1,2},{14,3},{7,4},{8,5},{5,6},{10,7},{11,8},{4,9},{9... | collective-permute-start | bytes 49160 | tf_op jit(solution)/shard_map/ppermute | solution.py:172
  5.2 1.1 %collective-permute-start.1 = (bf16[2,32,128]{2,1,0:T(8,128)(2,1)}, bf16[2,32,128]{2,1,0:T(8,128)(2,1)S(1)}, u32[]{:S(2)}, u32[]{:S(2)}) collective-permute-start(bf16[2,32,128]{2,1,0:T(8,128)(2,1)} %param.4), channel_id=1, source_target_pairs={{11,0},{14,1},{9,2},{12,3},{15,4},{10,5},{13,6},{8,7},{3,8},{6,9},... | collective-permute-start | bytes 49160 | tf_op jit(solution)/shard_map/ppermute | solution.py:172
  6.2 0.1 collective-permute-start.2
  6.3 0.3 %collective-permute-start.3 = (bf16[2,32,128]{2,1,0:T(8,128)(2,1)}, bf16[2,32,128]{2,1,0:T(8,128)(2,1)S(1)}, u32[]{:S(2)}, u32[]{:S(2)}) collective-permute-start(bf16[2,32,128]{2,1,0:T(8,128)(2,1)} %param.4), channel_id=1, source_target_pairs={{1,0},{4,1},{3,2},{6,3},{5,4},{0,5},{7,6},{2,7},{9,8},{12,9},{11,1... | collective-permute-start | bytes 49160 | tf_op jit(solution)/shard_map/ppermute | solution.py:172
  6.6 0.0 collective-permute-done.4.other_ref
  6.6 1.2 %stage.1 = (bf16[32,64,128]{2,1,0:T(8,128)(2,1)S(1)}, bf16[32,64,128]{2,1,0:T(8,128)(2,1)S(1)}) custom-call(s32[32]{0:T(128)} %lens_hbm_ref.1, bf16[32,64,128]{2,1,0:T(8,128)(2,1)} %own_ref.1, bf16[32,64,128]{2,1,0:T(8,128)(2,1)S(1)} %collective-permute-done.4.other_ref), custom_call_target="tpu_custom_call" | custom-call | flops 1048576 | bytes 2097152 | tf_op jit(solution)/shard_map/stage/pallas_call | solution.py:56
  7.8 0.0 collective-permute-done.refs_0_
  7.8 2.6 %collective-permute-done.1.refs_1_ = bf16[2,32,128]{2,1,0:T(8,128)(2,1)S(1)} collective-permute-done((bf16[2,32,128]{2,1,0:T(8,128)(2,1)}, bf16[2,32,128]{2,1,0:T(8,128)(2,1)S(1)}, u32[]{:S(2)}, u32[]{:S(2)}) %collective-permute-start.1) | collective-permute-done | bytes 16416 | tf_op jit(solution)/shard_map/ppermute | solution.py:172
  10.4 0.1 collective-permute-done.2.refs_2_
  10.5 0.0 collective-permute-done.3.refs_3_
  10.5 0.0 copy-start
  10.5 0.8 %score.1 = (f32[2,32]{1,0:T(2,128)S(1)}, f32[2,32]{1,0:T(2,128)S(1)}, f32[2,32]{1,0:T(2,128)S(1)}, f32[2,32]{1,0:T(2,128)S(1)}) custom-call(bf16[2,32,128]{2,1,0:T(8,128)(2,1)S(1)} %collective-permute-done.refs_0_, bf16[2,32,128]{2,1,0:T(8,128)(2,1)S(1)} %collective-permute-done.1.refs_1_, bf16[2,32,128]{2,1,0:T(8,128)(2,1)S(1)} %collective-permute-done.2.refs_2_, ...), custom_call_target="tpu_custom_call" | custom-call | tf_op jit(solution)/shard_map/score/pallas_call | solution.py:112
  11.4 0.6 %collective-permute-start.9 = (f32[2,32]{1,0:T(2,128)S(1)}, f32[2,32]{1,0:T(2,128)S(1)}, u32[]{:S(2)}, u32[]{:S(2)}) collective-permute-start(f32[2,32]{1,0:T(2,128)S(1)} %get-tuple-element.15), channel_id=1, source_target_pairs={{0,10},{1,15},{2,8},{3,13},{4,14},{5,11},{6,12},{7,9},{8,2},{9,7},... | collective-permute-start | bytes 776 | tf_op jit(solution)/shard_map/ppermute | solution.py:172
  12.0 2.0 %collective-permute-start.11 = (f32[2,32]{1,0:T(2,128)S(1)}, f32[2,32]{1,0:T(2,128)S(1)}, u32[]{:S(2)}, u32[]{:S(2)}) collective-permute-start(f32[2,32]{1,0:T(2,128)S(1)} %get-tuple-element.16), channel_id=1, source_target_pairs={{0,9},{1,12},{2,11},{3,14},{4,13},{5,8},{6,15},{7,10},{8,1},{9,4},... | collective-permute-start | bytes 776 | tf_op jit(solution)/shard_map/ppermute | solution.py:172
  14.0 0.7 %collective-permute-start.5 = (f32[2,32]{1,0:T(2,128)S(1)}, f32[2,32]{1,0:T(2,128)S(1)}, u32[]{:S(2)}, u32[]{:S(2)}) collective-permute-start(f32[2,32]{1,0:T(2,128)S(1)} %get-tuple-element.13), channel_id=1, source_target_pairs={{0,2},{1,7},{2,0},{3,5},{4,6},{5,3},{6,4},{7,1},{8,10},{9,15},{10,... | collective-permute-start | bytes 776 | tf_op jit(solution)/shard_map/ppermute | solution.py:172
  14.7 0.9 %collective-permute-start.7 = (f32[2,32]{1,0:T(2,128)S(1)}, f32[2,32]{1,0:T(2,128)S(1)}, u32[]{:S(2)}, u32[]{:S(2)}) collective-permute-start(f32[2,32]{1,0:T(2,128)S(1)} %get-tuple-element.14), channel_id=1, source_target_pairs={{0,1},{1,4},{2,3},{3,6},{4,5},{5,0},{6,7},{7,2},{8,9},{9,12},{10,1... | collective-permute-start | bytes 776 | tf_op jit(solution)/shard_map/ppermute | solution.py:172
  15.7 1.1 %collective-permute-done.9.refs_4_ = f32[2,32]{1,0:T(2,128)S(1)} collective-permute-done((f32[2,32]{1,0:T(2,128)S(1)}, f32[2,32]{1,0:T(2,128)S(1)}, u32[]{:S(2)}, u32[]{:S(2)}) %collective-permute-start.9) | collective-permute-done | bytes 288 | tf_op jit(solution)/shard_map/ppermute | solution.py:172
  16.8 0.0 collective-permute-start.10
  16.8 0.0 collective-permute-done.11.refs_6_
  16.8 0.6 %collective-permute-start.12 = (f32[2,32]{1,0:T(2,128)S(1)}, f32[2,32]{1,0:T(2,128)S(1)}, u32[]{:S(2)}, u32[]{:S(2)}) collective-permute-start(f32[2,32]{1,0:T(2,128)S(1)} %collective-permute-done.11.refs_6_), channel_id=1, source_target_pairs={{0,1},{1,0},{2,3},{3,2},{4,5},{5,4},{6,7},{7,6},{8,9},{9,8},{10,11... | collective-permute-start | bytes 776 | tf_op jit(solution)/shard_map/ppermute | solution.py:180
  17.4 0.2 collective-permute-done.5.refs_0_
  17.6 0.2 %collective-permute-start.6 = (f32[2,32]{1,0:T(2,128)S(1)}, f32[2,32]{1,0:T(2,128)S(1)}, u32[]{:S(2)}, u32[]{:S(2)}) collective-permute-start(f32[2,32]{1,0:T(2,128)S(1)} %collective-permute-done.5.refs_0_), channel_id=1, source_target_pairs={{0,1},{1,0},{2,3},{3,2},{4,5},{5,4},{6,7},{7,6},{8,9},{9,8},{10,11... | collective-permute-start | bytes 776 | tf_op jit(solution)/shard_map/ppermute | solution.py:180
  17.8 0.0 collective-permute-done.7.refs_2_
  17.8 0.3 %collective-permute-start.8 = (f32[2,32]{1,0:T(2,128)S(1)}, f32[2,32]{1,0:T(2,128)S(1)}, u32[]{:S(2)}, u32[]{:S(2)}) collective-permute-start(f32[2,32]{1,0:T(2,128)S(1)} %collective-permute-done.7.refs_2_), channel_id=1, source_target_pairs={{0,1},{1,0},{2,3},{3,2},{4,5},{5,4},{6,7},{7,6},{8,9},{9,8},{10,11... | collective-permute-start | bytes 776 | tf_op jit(solution)/shard_map/ppermute | solution.py:180
  18.1 0.0 copy-done
  18.1 0.0 collective-permute-done.10.refs_5_
  18.1 0.1 collective-permute-done.12.refs_7_
  18.2 0.5 %collective-permute-done.6.refs_1_ = f32[2,32]{1,0:T(2,128)S(1)} collective-permute-done((f32[2,32]{1,0:T(2,128)S(1)}, f32[2,32]{1,0:T(2,128)S(1)}, u32[]{:S(2)}, u32[]{:S(2)}) %collective-permute-start.6) | collective-permute-done | bytes 288 | tf_op jit(solution)/shard_map/ppermute | solution.py:180
  18.7 0.2 %collective-permute-done.8.refs_3_ = f32[2,32]{1,0:T(2,128)S(1)} collective-permute-done((f32[2,32]{1,0:T(2,128)S(1)}, f32[2,32]{1,0:T(2,128)S(1)}, u32[]{:S(2)}, u32[]{:S(2)}) %collective-permute-start.8) | collective-permute-done | bytes 288 | tf_op jit(solution)/shard_map/ppermute | solution.py:180
  18.9 0.8 %pick.1 = f32[2,1000]{1,0:T(2,128)} custom-call(s32[2,1000]{1,0:T(2,128)S(1)} %and_add_fusion.spot_ref, f32[2,32]{1,0:T(2,128)S(1)} %collective-permute-done.5.refs_0_, f32[2,32]{1,0:T(2,128)S(1)} %collective-permute-done.6.refs_1_, f32[2,32]{1,0:T(2,128)S(1)} %collective-permute-done.7.refs_2_, f32[2,32]{1,0:T(2,128)S(1)} %collective-permute-done.8.refs_3_, ...), custom_call_target="tpu_custom_call" | custom-call | tf_op jit(solution)/shard_map/pick/pallas_call | solution.py:149
  (1 shorter events, 0.0 us)
Async XLA Ops:
  0.0 6.6 %collective-permute-start.4 = (bf16[32,64,128]{2,1,0:T(8,128)(2,1)}, bf16[32,64,128]{2,1,0:T(8,128)(2,1)S(1)}, u32[]{:S(2)}, u32[]{:S(2)}) collective-permute-start(bf16[32,64,128]{2,1,0:T(8,128)(2,1)} %own_ref.1), channel_id=1, source_target_pairs={{0,1},{1,0},{2,3},{3,2},{4,5},{5,4},{6,7},{7,6},{8,9},{9,8},{10,11... | collective-permute-start | bytes 1572872 | tf_op jit(solution)/shard_map/ppermute | solution.py:180
  0.5 7.4 %collective-permute-start = (bf16[2,32,128]{2,1,0:T(8,128)(2,1)}, bf16[2,32,128]{2,1,0:T(8,128)(2,1)S(1)}, u32[]{:S(2)}, u32[]{:S(2)}) collective-permute-start(bf16[2,32,128]{2,1,0:T(8,128)(2,1)} %param.4), channel_id=1, source_target_pairs={{3,0},{12,1},{1,2},{14,3},{7,4},{8,5},{5,6},{10,7},{11,8},{4,9},{9... | collective-permute-start | bytes 49160 | tf_op jit(solution)/shard_map/ppermute | solution.py:172
  5.2 5.3 %collective-permute-start.1 = (bf16[2,32,128]{2,1,0:T(8,128)(2,1)}, bf16[2,32,128]{2,1,0:T(8,128)(2,1)S(1)}, u32[]{:S(2)}, u32[]{:S(2)}) collective-permute-start(bf16[2,32,128]{2,1,0:T(8,128)(2,1)} %param.4), channel_id=1, source_target_pairs={{11,0},{14,1},{9,2},{12,3},{15,4},{10,5},{13,6},{8,7},{3,8},{6,9},... | collective-permute-start | bytes 49160 | tf_op jit(solution)/shard_map/ppermute | solution.py:172
  6.2 4.3 %collective-permute-start.2 = (bf16[2,32,128]{2,1,0:T(8,128)(2,1)}, bf16[2,32,128]{2,1,0:T(8,128)(2,1)S(1)}, u32[]{:S(2)}, u32[]{:S(2)}) collective-permute-start(bf16[2,32,128]{2,1,0:T(8,128)(2,1)} %param.4), channel_id=1, source_target_pairs={{9,0},{6,1},{11,2},{4,3},{13,4},{2,5},{15,6},{0,7},{1,8},{14,9},{3... | collective-permute-start | bytes 49160 | tf_op jit(solution)/shard_map/ppermute | solution.py:172
  6.3 4.3 %collective-permute-start.3 = (bf16[2,32,128]{2,1,0:T(8,128)(2,1)}, bf16[2,32,128]{2,1,0:T(8,128)(2,1)S(1)}, u32[]{:S(2)}, u32[]{:S(2)}) collective-permute-start(bf16[2,32,128]{2,1,0:T(8,128)(2,1)} %param.4), channel_id=1, source_target_pairs={{1,0},{4,1},{3,2},{6,3},{5,4},{0,5},{7,6},{2,7},{9,8},{12,9},{11,1... | collective-permute-start | bytes 49160 | tf_op jit(solution)/shard_map/ppermute | solution.py:172
  10.5 7.5 %copy-start = (s32[2,1000]{1,0:T(2,128)S(1)}, s32[2,1000]{1,0:T(2,128)}, u32[]{:S(2)}) copy-start(s32[2,1000]{1,0:T(2,128)} %param.7) | copy-start | bytes 24004
  11.4 5.4 %collective-permute-start.9 = (f32[2,32]{1,0:T(2,128)S(1)}, f32[2,32]{1,0:T(2,128)S(1)}, u32[]{:S(2)}, u32[]{:S(2)}) collective-permute-start(f32[2,32]{1,0:T(2,128)S(1)} %get-tuple-element.15), channel_id=1, source_target_pairs={{0,10},{1,15},{2,8},{3,13},{4,14},{5,11},{6,12},{7,9},{8,2},{9,7},... | collective-permute-start | bytes 776 | tf_op jit(solution)/shard_map/ppermute | solution.py:172
  12.0 4.8 %collective-permute-start.11 = (f32[2,32]{1,0:T(2,128)S(1)}, f32[2,32]{1,0:T(2,128)S(1)}, u32[]{:S(2)}, u32[]{:S(2)}) collective-permute-start(f32[2,32]{1,0:T(2,128)S(1)} %get-tuple-element.16), channel_id=1, source_target_pairs={{0,9},{1,12},{2,11},{3,14},{4,13},{5,8},{6,15},{7,10},{8,1},{9,4},... | collective-permute-start | bytes 776 | tf_op jit(solution)/shard_map/ppermute | solution.py:172
  14.0 3.6 %collective-permute-start.5 = (f32[2,32]{1,0:T(2,128)S(1)}, f32[2,32]{1,0:T(2,128)S(1)}, u32[]{:S(2)}, u32[]{:S(2)}) collective-permute-start(f32[2,32]{1,0:T(2,128)S(1)} %get-tuple-element.13), channel_id=1, source_target_pairs={{0,2},{1,7},{2,0},{3,5},{4,6},{5,3},{6,4},{7,1},{8,10},{9,15},{10,... | collective-permute-start | bytes 776 | tf_op jit(solution)/shard_map/ppermute | solution.py:172
  14.7 3.1 %collective-permute-start.7 = (f32[2,32]{1,0:T(2,128)S(1)}, f32[2,32]{1,0:T(2,128)S(1)}, u32[]{:S(2)}, u32[]{:S(2)}) collective-permute-start(f32[2,32]{1,0:T(2,128)S(1)} %get-tuple-element.14), channel_id=1, source_target_pairs={{0,1},{1,4},{2,3},{3,6},{4,5},{5,0},{6,7},{7,2},{8,9},{9,12},{10,1... | collective-permute-start | bytes 776 | tf_op jit(solution)/shard_map/ppermute | solution.py:172
  16.8 1.3 %collective-permute-start.10 = (f32[2,32]{1,0:T(2,128)S(1)}, f32[2,32]{1,0:T(2,128)S(1)}, u32[]{:S(2)}, u32[]{:S(2)}) collective-permute-start(f32[2,32]{1,0:T(2,128)S(1)} %collective-permute-done.9.refs_4_), channel_id=1, source_target_pairs={{0,1},{1,0},{2,3},{3,2},{4,5},{5,4},{6,7},{7,6},{8,9},{9,8},{10,11... | collective-permute-start | bytes 776 | tf_op jit(solution)/shard_map/ppermute | solution.py:180
  16.8 1.4 %collective-permute-start.12 = (f32[2,32]{1,0:T(2,128)S(1)}, f32[2,32]{1,0:T(2,128)S(1)}, u32[]{:S(2)}, u32[]{:S(2)}) collective-permute-start(f32[2,32]{1,0:T(2,128)S(1)} %collective-permute-done.11.refs_6_), channel_id=1, source_target_pairs={{0,1},{1,0},{2,3},{3,2},{4,5},{5,4},{6,7},{7,6},{8,9},{9,8},{10,11... | collective-permute-start | bytes 776 | tf_op jit(solution)/shard_map/ppermute | solution.py:180
  17.6 1.1 %collective-permute-start.6 = (f32[2,32]{1,0:T(2,128)S(1)}, f32[2,32]{1,0:T(2,128)S(1)}, u32[]{:S(2)}, u32[]{:S(2)}) collective-permute-start(f32[2,32]{1,0:T(2,128)S(1)} %collective-permute-done.5.refs_0_), channel_id=1, source_target_pairs={{0,1},{1,0},{2,3},{3,2},{4,5},{5,4},{6,7},{7,6},{8,9},{9,8},{10,11... | collective-permute-start | bytes 776 | tf_op jit(solution)/shard_map/ppermute | solution.py:180
  17.8 1.1 %collective-permute-start.8 = (f32[2,32]{1,0:T(2,128)S(1)}, f32[2,32]{1,0:T(2,128)S(1)}, u32[]{:S(2)}, u32[]{:S(2)}) collective-permute-start(f32[2,32]{1,0:T(2,128)S(1)} %collective-permute-done.7.refs_2_), channel_id=1, source_target_pairs={{0,1},{1,0},{2,3},{3,2},{4,5},{5,4},{6,7},{7,6},{8,9},{9,8},{10,11... | collective-permute-start | bytes 776 | tf_op jit(solution)/shard_map/ppermute | solution.py:180
